TPU v7x, 256 devices: a whole 4x4x8 slice. The times are simulated.
256 devices in a mesh: slab: 64 (over x_hi, z, y), mode: 4 (over x_lo, core).
Axes of the slice: x: 4 (x_hi: 2, x_lo: 2; x = x_hi * 2 + x_lo), y: 4, z: 8, core: 2. Of those that a mesh axis runs over, the one named last changes fastest.
Arguments:
- subspace: float32 [192, 3, 128, 8, 128], P('mode', None, 'slab'), may hold values from -32 to 32
- modulus: float32 [128, 8, 128], P('slab'), may hold values from 0.3 to 3
- mass: float32 [128, 8, 128], P('slab'), may hold values from 0.3 to 3
- support: int32 [128, 8, 128], P('slab'), may hold values 0 or 1
- stiffness: float32 [24, 24], replicated, may hold values from -0.04 to 1.5, as said below
Outputs:
- filtered: float32 [192, 3, 128, 8, 128], P('mode', None, 'slab')
- stiffness_gram: float32 [192, 192], P('mode')
- mass_gram: float32 [192, 192], P('mode')
Inputs may be any that keep to these rules, and one draw needn't show every extreme that they name: `stiffness`: Symmetric; the diagonal lies in 1 to 1.5 and the magnitudes off the diagonal of each row sum to less than 0.9.
All inputs are finite; a program needn't handle non-finite values. No bound on the sum of `support` on one device may be relied on, other than what follows from the above.
Results may differ from a plain program's by a relative error of at most 0.0001.
Values sent between devices are 32-bit elements; how exact they have to be, the bound alone decides.
No kernel may reach another device: no remote copies, remote signals or barrier semaphores. Data moves between devices by JAX's collectives and lax.ppermute only.
A program may use at most 128 MiB of HBM per device.

v0:
```python
from functools import partial
import math

import jax
import jax.numpy as jnp
from jax import lax
from jax.sharding import PartitionSpec as P

DEGREE = 4


corner_offsets = (
    (0, 0, 0),
    (0, 0, 1),
    (0, 1, 0),
    (0, 1, 1),
    (1, 0, 0),
    (1, 0, 1),
    (1, 1, 0),
    (1, 1, 1),
)
center_value = 110.0
half_width = 90.0
highest = lax.Precision.HIGHEST


def passed_along(x, axis, by):
    length = lax.axis_size(axis)
    pairs = [(i, i + by) for i in range(length) if 0 <= i + by < length]
    return lax.ppermute(x, axis, pairs)


def with_halo(cells, sides, width):
    for axis, dim in sides:
        count = lax.axis_size(axis)
        ends = count - 1
        head = lax.slice_in_dim(cells, 0, width, axis=dim)
        tail = lax.slice_in_dim(cells, cells.shape[dim] - width, cells.shape[dim], axis=dim)
        cells = jnp.concatenate(
            [
                lax.ppermute(tail, axis, [(i, (i + 1) % count) for i in range(ends)]),
                cells,
                lax.ppermute(head, axis, [((i + 1) % count, i) for i in range(ends)]),
            ],
            axis=dim,
        )
    return cells


def element_nodes(block, effective, stiffness, grown_axis):
    group = block.shape[0]
    extents = list(block.shape[2:])
    grown_number = grown_axis - 2
    interior = list(extents)
    interior[grown_number] = extents[grown_number] - 2
    layer_shape = list(interior)
    layer_shape[grown_number] = extents[grown_number] - 1
    padding = [(0, 0), (0, 0)]
    for axis_number in range(3):
        padding.append((0, 0) if axis_number == grown_number else (0, 1))
    padded = jnp.pad(block, padding)
    corners = []
    for offsets in corner_offsets:
        window = padded
        for axis_number in range(3):
            window = lax.slice_in_dim(
                window,
                offsets[axis_number],
                offsets[axis_number] + layer_shape[axis_number],
                axis=axis_number + 2,
            )
        corners.append(window)
    local = (
        jnp.stack(corners, 0).transpose(0, 2, 1, 3, 4, 5).reshape(tuple([24, group] + layer_shape))
    )
    force = (
        jnp.einsum("rs,sgxyz->rgxyz", stiffness, local, precision=highest) * effective[None, None]
    )
    force = force.reshape(tuple([8, 3, group] + layer_shape))
    total = None
    for index in range(8):
        offsets = corner_offsets[index]
        contrib = force[index]
        for axis_number in range(3):
            shift_value = offsets[axis_number]
            if axis_number == grown_number:
                contrib = lax.slice_in_dim(
                    contrib,
                    1 - shift_value,
                    1 - shift_value + interior[axis_number],
                    axis=axis_number + 2,
                )
            elif shift_value:
                widths = [(0, 0)] * 5
                widths[axis_number + 2] = (shift_value, 0)
                contrib = lax.slice_in_dim(
                    jnp.pad(contrib, widths), 0, interior[axis_number], axis=axis_number + 2
                )
        total = contrib if total is None else total + contrib
    return total.transpose(1, 0, 2, 3, 4)


def apply_grouped(grown, effective, stiffness, grown_axis, target_shape):
    modes = grown.shape[0]
    group = modes if modes <= 8 else math.gcd(modes, 8)
    blocks = grown.reshape((modes // group, group) + grown.shape[1:])
    apply_block = partial(
        element_nodes, effective=effective, stiffness=stiffness, grown_axis=grown_axis
    )
    nodes = lax.map(apply_block, blocks)
    return nodes.reshape(target_shape)


def run_filter(start, operate, weights, free):
    previous = free * start
    current = (operate(previous) / weights - center_value * previous) / half_width
    for step in range(DEGREE - 1):
        following = (
            2.0 * (operate(current) / weights - center_value * current) / half_width - previous
        )
        previous, current = (current, following)
    return (current, operate(current))


def body(subspace, modulus, mass, support, stiffness):
    modes, comps, planes, rows, depth = subspace.shape
    slabs = lax.axis_size("slab")
    free_nodes = (1 - support).astype(jnp.float32)
    free = free_nodes[None, None]
    weights = mass[None, None]
    lower = passed_along(modulus[planes - 1 :], "slab", 1)
    layers = jnp.concatenate([lower, modulus], 0)
    plane_index = (
        lax.axis_index("slab") * planes - 1 + lax.broadcasted_iota(jnp.int32, layers.shape, 0)
    )
    row_index = lax.broadcasted_iota(jnp.int32, layers.shape, 1)
    depth_index = lax.broadcasted_iota(jnp.int32, layers.shape, 2)
    valid = (plane_index < planes * slabs - 1) & (row_index < rows - 1) & (depth_index < depth - 1)
    effective = jnp.where(valid, layers, jnp.zeros_like(layers))

    def operate(field):
        grown = with_halo(field, (("slab", 2),), 1)
        return free * apply_grouped(grown, effective, stiffness, 2, field.shape)

    filtered, stiffened = run_filter(subspace, operate, weights, free)
    weights_here = mass[None, None]
    weighted = filtered * weights_here
    piece = lax.all_gather(filtered, "mode", axis=0, tiled=True)
    stiff_part = jnp.einsum("acxyz,bcxyz->ab", stiffened, piece, precision=highest)
    mass_part = jnp.einsum("acxyz,bcxyz->ab", weighted, piece, precision=highest)
    grams = jnp.stack([stiff_part, mass_part], 0)
    dof_count = 3.0 * planes * slabs * rows * depth
    grams = lax.psum(grams / dof_count, "slab")
    return (filtered, grams[0], grams[1])


def solution(mesh):
    placed = (
        P("mode", None, "slab", None, None),
        P("slab", None, None),
        P("slab", None, None),
        P("slab", None, None),
        P(),
    )
    return jax.shard_map(
        body,
        mesh=mesh,
        in_specs=placed,
        out_specs=(P("mode", None, "slab", None, None), P("mode", None), P("mode", None)),
        check_vma=False,
    )
```

profile of v0, /device:TPU:32, one launch (start us, length us, event | category | flops | bytes accessed | tf_op | source)
XLA Modules:
  0.0 990.8 jit_solution(5432373451217978833)
XLA Ops:
  13.9 4.5 collective-permute-start.1
  20.4 9.4 collective-permute-done.2
  32.4 39.5 %while.60 = (s32[]{:T(128)}, f32[6,8,3,2,8,128]{5,1,0,4,3,2:T(8,128)S(1)}, f32[6,8,3,4,8,128]{5,1,0,4,3,2:T(8,128)}, f32[24,24]{1,0:T(8,128)S(1)}, f32[3,8,128]{2,1,0:T(8,128)S(1)}, /*index=5*/s32[]{:T(128)}) while((s32[]{:T(128)}, f32[6,8,3,2,8,128]{5,1,0,4,3,2:T(8,128)S(1)}, f32[6,8,3,4,8,128]{5,1,0,4,3,2:T(8,128)}, f32[24,24]{1,0:T(8,128)S(1)}, ...), condition=%wide.region_1.2_spmd, body=%wide.region_0.1_spmd.sunk | while | flops 170803200 | bytes 16988492 | solution.py:110
  34.4 3.5 multiply_bitcast_fusion.10
  40.9 3.5 multiply_bitcast_fusion.10
  77.8 5.3 collective-permute-start.4
  83.1 10.1 %collective-permute-done.3 = f32[48,3,1,8,128]{4,0,3,2,1:T(8,128)S(1)} collective-permute-done((f32[48,3,1,8,128]{4,0,3,2,1:T(8,128)}, f32[48,3,1,8,128]{4,0,3,2,1:T(8,128)S(1)}, u32[]{:S(2)}, u32[]{:S(2)}) %collective-permute-start.3) | collective-permute-done | bytes 589856 | tf_op jit(solution)/shard_map/ppermute | solution.py:41
  98.3 44.0 %while.61 = (s32[]{:T(128)}, f32[6,8,3,2,8,128]{5,1,0,4,3,2:T(8,128)}, f32[6,8,3,4,8,128]{5,1,0,4,3,2:T(8,128)}, f32[24,24]{1,0:T(8,128)S(1)}, f32[3,8,128]{2,1,0:T(8,128)S(1)}, /*index=5*/s32[]{:T(128)}) while((s32[]{:T(128)}, f32[6,8,3,2,8,128]{5,1,0,4,3,2:T(8,128)}, f32[6,8,3,4,8,128]{5,1,0,4,3,2:T(8,128)}, f32[24,24]{1,0:T(8,128)S(1)}, ...), condition=%wide.region_3.4_spmd, body=%wide.region_2.3_spmd.sunk | while | flops 170803200 | bytes 16923464 | solution.py:110
  107.5 3.5 multiply_bitcast_fusion.11
  122.2 3.5 multiply_bitcast_fusion.11
  136.9 3.5 multiply_bitcast_fusion.11
  146.5 4.2 collective-permute-start.5
  150.8 4.7 collective-permute-start.6
  155.5 8.9 collective-permute-done.5
  169.6 44.0 %while.62 = (s32[]{:T(128)}, f32[6,8,3,2,8,128]{5,1,0,4,3,2:T(8,128)}, f32[6,8,3,4,8,128]{5,1,0,4,3,2:T(8,128)}, f32[24,24]{1,0:T(8,128)S(1)}, f32[3,8,128]{2,1,0:T(8,128)S(1)}, /*index=5*/s32[]{:T(128)}) while((s32[]{:T(128)}, f32[6,8,3,2,8,128]{5,1,0,4,3,2:T(8,128)}, f32[6,8,3,4,8,128]{5,1,0,4,3,2:T(8,128)}, f32[24,24]{1,0:T(8,128)S(1)}, ...), condition=%wide.region_5.6_spmd, body=%wide.region_4.5_spmd.sunk | while | flops 170803200 | bytes 16923464 | solution.py:110
  178.7 3.5 multiply_bitcast_fusion.12
  193.4 3.5 multiply_bitcast_fusion.12
  208.1 3.5 multiply_bitcast_fusion.12
  216.3 4.2 collective-permute-start.7
  220.6 4.4 collective-permute-start.8
  224.9 8.4 collective-permute-done.7
  238.4 43.3 %while.63 = (s32[]{:T(128)}, f32[6,8,3,2,8,128]{5,1,0,4,3,2:T(8,128)}, f32[6,8,3,4,8,128]{5,1,0,4,3,2:T(8,128)}, f32[24,24]{1,0:T(8,128)S(1)}, f32[3,8,128]{2,1,0:T(8,128)S(1)}, /*index=5*/s32[]{:T(128)}) while((s32[]{:T(128)}, f32[6,8,3,2,8,128]{5,1,0,4,3,2:T(8,128)}, f32[6,8,3,4,8,128]{5,1,0,4,3,2:T(8,128)}, f32[24,24]{1,0:T(8,128)S(1)}, ...), condition=%wide.region_7.8_spmd, body=%wide.region_6.7_spmd.sunk | while | flops 170803200 | bytes 16923464 | solution.py:110
  261.9 3.5 multiply_bitcast_fusion.13
  269.1 3.5 multiply_bitcast_fusion.13
  284.1 6.5 collective-permute-start.10
  292.8 6.4 collective-permute-done.10
  299.2 6.2 collective-permute-done.9
  308.1 38.5 %while.64 = (s32[]{:T(128)}, f32[6,8,3,2,8,128]{5,1,0,4,3,2:T(8,128)}, f32[6,8,3,4,8,128]{5,1,0,4,3,2:T(8,128)S(1)}, f32[24,24]{1,0:T(8,128)}, f32[3,8,128]{2,1,0:T(8,128)S(1)}, /*index=5*/s32[]{:T(128)}) while((s32[]{:T(128)}, f32[6,8,3,2,8,128]{5,1,0,4,3,2:T(8,128)}, f32[6,8,3,4,8,128]{5,1,0,4,3,2:T(8,128)S(1)}, f32[24,24]{1,0:T(8,128)}, ...), condition=%wide.region_9.10_spmd, body=%wide.region_8.9_spmd.sunk | while | flops 170803200 | bytes 16932708 | solution.py:110
  346.6 17.8 %all-gather.2.cloned.1.call-done = f32[192,3,2,8,128]{4,0,3,2,1:T(8,128)} async-done(((f32[48,3,2,8,128]{4,0,3,2,1:T(8,128)}), f32[192,3,2,8,128]{4,0,3,2,1:T(8,128)}) %all-gather.2.cloned.1.call-update) | async-done | bytes 4718608 | tf_op jit(solution)/shard_map/all_gather | solution.py:148
  364.4 6.6 fusion.152
  371.0 5.8 fusion.155
  378.9 603.4 %all-reduce.47.cloned.1.call-done = f32[2,48,192]{2,1,0:T(8,128)} async-done(((f32[2,48,192]{2,1,0:T(8,128)}), f32[2,48,192]{2,1,0:T(8,128)}) %all-reduce.47.cloned.1.call-update) | async-done | bytes 73744 | tf_op jit(solution)/shard_map/psum | solution.py:153
  (522 shorter events, 221.0 us)
Async XLA Ops:
  7.2 357.2 %all-gather.2.cloned.1.call-start = ((), (), s32[]{:S(2)}) async-start(), calls=%async_computation | async-start | bytes 5898240 | tf_op jit(solution)/shard_map/all_gather | solution.py:148
  7.9 2.5 copy-start.12
  7.9 10.5 %copy-start.14 = (f32[2,8,128]{2,1,0:T(8,128)S(1)}, f32[2,8,128]{2,1,0:T(8,128)}, u32[]{:S(2)}) copy-start(f32[2,8,128]{2,1,0:T(8,128)} %param.16) | copy-start | bytes 24580
  10.5 19.4 %collective-permute-start = (f32[48,3,1,8,128]{4,0,3,2,1:T(8,128)}, f32[48,3,1,8,128]{4,0,3,2,1:T(8,128)S(1)}, u32[]{:S(2)}, u32[]{:S(2)}) collective-permute-start(f32[48,3,1,8,128]{4,0,3,2,1:T(8,128)} %get-tuple-element.487), channel_id=1, source_target_pairs={{0,4},{4,8},{8,12},{12,16},{16,20},{20,24},{24,28},{28,32},{32,36}... | collective-permute-start | bytes 1769480 | tf_op jit(solution)/shard_map/ppermute | solution.py:41
  13.9 16.8 %collective-permute-start.1 = (f32[48,3,1,8,128]{4,0,3,2,1:T(8,128)S(1)}, f32[48,3,1,8,128]{4,0,3,2,1:T(8,128)S(1)}, u32[]{:S(2)}, u32[]{:S(2)}) collective-permute-start(f32[48,3,1,8,128]{4,0,3,2,1:T(8,128)S(1)} %get-tuple-element.488), channel_id=1, source_target_pairs={{4,0},{8,4},{12,8},{16,12},{20,16},{24,20},{28,24},{32,28},{36,32}... | collective-permute-start | bytes 1769480 | tf_op jit(solution)/shard_map/ppermute | solution.py:43
  18.4 11.4 %collective-permute-start.2 = (f32[1,8,128]{2,1,0:T(8,128)S(1)}, f32[1,8,128]{2,1,0:T(8,128)S(1)}, u32[]{:S(2)}, u32[]{:S(2)}) collective-permute-start(f32[1,8,128]{2,1,0:T(8,128)S(1)} %slice.1031), channel_id=1, source_target_pairs={{0,4},{4,8},{8,12},{12,16},{16,20},{20,24},{24,28},{28,32},{32,36}... | collective-permute-start | bytes 12296 | tf_op jit(solution)/shard_map/ppermute | solution.py:30
  29.9 2.5 copy-start.5
  32.4 39.5 %copy-start.3 = (f32[48,3,2,8,128]{4,3,2,1,0:T(8,128)S(1)}, f32[48,3,2,8,128]{4,3,2,1,0:T(8,128)}, u32[]{:S(2)}) copy-start(f32[48,3,2,8,128]{4,3,2,1,0:T(8,128)} %param.15) | copy-start | bytes 3538948
  71.9 2.5 copy-start.4
  74.4 18.8 %collective-permute-start.3 = (f32[48,3,1,8,128]{4,0,3,2,1:T(8,128)}, f32[48,3,1,8,128]{4,0,3,2,1:T(8,128)S(1)}, u32[]{:S(2)}, u32[]{:S(2)}) collective-permute-start(f32[48,3,1,8,128]{4,0,3,2,1:T(8,128)} %get-tuple-element.485), channel_id=1, source_target_pairs={{0,4},{4,8},{8,12},{12,16},{16,20},{20,24},{24,28},{28,32},{32,36}... | collective-permute-start | bytes 1769480 | tf_op jit(solution)/shard_map/ppermute | solution.py:41
  77.8 16.7 %collective-permute-start.4 = (f32[48,3,1,8,128]{4,0,3,2,1:T(8,128)}, f32[48,3,1,8,128]{4,0,3,2,1:T(8,128)}, u32[]{:S(2)}, u32[]{:S(2)}) collective-permute-start(f32[48,3,1,8,128]{4,0,3,2,1:T(8,128)} %get-tuple-element.486), channel_id=1, source_target_pairs={{4,0},{8,4},{12,8},{16,12},{20,16},{24,20},{28,24},{32,28},{36,32}... | collective-permute-start | bytes 1769480 | tf_op jit(solution)/shard_map/ppermute | solution.py:43
  83.1 15.2 %copy-start.6 = (f32[24,24]{1,0:T(8,128)S(1)}, f32[24,24]{1,0:T(8,128)}, u32[]{:S(2)}) copy-start(f32[24,24]{1,0:T(8,128)} %param.19) | copy-start | bytes 6916
  142.4 0.6 copy-start.7
  146.5 17.9 %collective-permute-start.5 = (f32[48,3,1,8,128]{4,0,3,2,1:T(8,128)}, f32[48,3,1,8,128]{4,0,3,2,1:T(8,128)S(1)}, u32[]{:S(2)}, u32[]{:S(2)}) collective-permute-start(f32[48,3,1,8,128]{4,0,3,2,1:T(8,128)} %get-tuple-element.483), channel_id=1, source_target_pairs={{0,4},{4,8},{8,12},{12,16},{16,20},{20,24},{24,28},{28,32},{32,36}... | collective-permute-start | bytes 1769480 | tf_op jit(solution)/shard_map/ppermute | solution.py:41
  150.8 15.0 %collective-permute-start.6 = (f32[48,3,1,8,128]{4,0,3,2,1:T(8,128)}, f32[48,3,1,8,128]{4,0,3,2,1:T(8,128)}, u32[]{:S(2)}, u32[]{:S(2)}) collective-permute-start(f32[48,3,1,8,128]{4,0,3,2,1:T(8,128)} %get-tuple-element.484), channel_id=1, source_target_pairs={{4,0},{8,4},{12,8},{16,12},{20,16},{24,20},{28,24},{32,28},{36,32}... | collective-permute-start | bytes 1769480 | tf_op jit(solution)/shard_map/ppermute | solution.py:43
  155.5 14.1 %copy-start.8 = (f32[24,24]{1,0:T(8,128)S(1)}, f32[24,24]{1,0:T(8,128)}, u32[]{:S(2)}) copy-start(f32[24,24]{1,0:T(8,128)} %copy-done.7) | copy-start | bytes 6916
  216.3 17.0 %collective-permute-start.7 = (f32[48,3,1,8,128]{4,0,3,2,1:T(8,128)}, f32[48,3,1,8,128]{4,0,3,2,1:T(8,128)S(1)}, u32[]{:S(2)}, u32[]{:S(2)}) collective-permute-start(f32[48,3,1,8,128]{4,0,3,2,1:T(8,128)} %get-tuple-element.481), channel_id=1, source_target_pairs={{0,4},{4,8},{8,12},{12,16},{16,20},{20,24},{24,28},{28,32},{32,36}... | collective-permute-start | bytes 1769480 | tf_op jit(solution)/shard_map/ppermute | solution.py:41
  220.6 14.0 %collective-permute-start.8 = (f32[48,3,1,8,128]{4,0,3,2,1:T(8,128)}, f32[48,3,1,8,128]{4,0,3,2,1:T(8,128)}, u32[]{:S(2)}, u32[]{:S(2)}) collective-permute-start(f32[48,3,1,8,128]{4,0,3,2,1:T(8,128)} %get-tuple-element.482), channel_id=1, source_target_pairs={{4,0},{8,4},{12,8},{16,12},{20,16},{24,20},{28,24},{32,28},{36,32}... | collective-permute-start | bytes 1769480 | tf_op jit(solution)/shard_map/ppermute | solution.py:43
  224.9 13.5 %copy-start.9 = (f32[24,24]{1,0:T(8,128)S(1)}, f32[24,24]{1,0:T(8,128)}, u32[]{:S(2)}) copy-start(f32[24,24]{1,0:T(8,128)} %copy-done.7) | copy-start | bytes 6916
  284.0 8.6 copy-start
  284.1 15.1 %collective-permute-start.10 = (f32[48,3,1,8,128]{4,0,3,2,1:T(8,128)S(1)}, f32[48,3,1,8,128]{4,0,3,2,1:T(8,128)S(1)}, u32[]{:S(2)}, u32[]{:S(2)}) collective-permute-start(f32[48,3,1,8,128]{4,0,3,2,1:T(8,128)S(1)} %get-tuple-element.480), channel_id=1, source_target_pairs={{4,0},{8,4},{12,8},{16,12},{20,16},{24,20},{28,24},{32,28},{36,32}... | collective-permute-start | bytes 1769480 | tf_op jit(solution)/shard_map/ppermute | solution.py:43
  290.6 14.8 %collective-permute-start.9 = (f32[48,3,1,8,128]{4,0,3,2,1:T(8,128)S(1)}, f32[48,3,1,8,128]{4,0,3,2,1:T(8,128)S(1)}, u32[]{:S(2)}, u32[]{:S(2)}) collective-permute-start(f32[48,3,1,8,128]{4,0,3,2,1:T(8,128)S(1)} %get-tuple-element.479), channel_id=1, source_target_pairs={{0,4},{4,8},{8,12},{12,16},{16,20},{20,24},{24,28},{28,32},{32,36}... | collective-permute-start | bytes 1769480 | tf_op jit(solution)/shard_map/ppermute | solution.py:41
  292.5 689.7 %all-reduce.47.cloned.1.call-start = ((), (), s32[]{:S(2)}) async-start(), calls=%async_computation.1 | async-start | bytes 196608 | tf_op jit(solution)/shard_map/psum | solution.py:153
  308.1 56.2 %copy-start.1 = (f32[48,3,2,8,128]{4,0,3,2,1:T(8,128)S(1)}, f32[48,3,2,8,128]{4,0,3,2,1:T(8,128)}, u32[]{:S(2)}) copy-start(f32[48,3,2,8,128]{4,0,3,2,1:T(8,128)} %copy-done) | copy-start | bytes 3538948
  308.3 0.8 copy-start.11
  314.7 0.7 copy-start.11
  321.1 0.7 copy-start.11
  327.5 0.7 copy-start.11
  333.9 0.7 copy-start.11
  340.3 0.7 copy-start.11
  346.6 24.4 %copy-start.13 = (f32[2,8,128]{2,1,0:T(8,128)S(1)}, f32[2,8,128]{2,1,0:T(8,128)}, u32[]{:S(2)}) copy-start(f32[2,8,128]{2,1,0:T(8,128)} %copy-done.12) | copy-start | bytes 24580
  364.4 6.6 copy-start.2
  (1 other events, 0.6 us)
Sparse Core Ops, SparseCore 0:
  292.7 71.6 all-gather.1
  377.6 604.5 all-reduce.46
where the time goes:
time: 1000 us; the launch traced here: 991 us
  waiting for transfers between devices  675 us (68%)
  matrix products  118 us (12%)
  local copies, waits for them, and re-layouts  94.8 us (9%)
  starting transfers between devices  44.8 us (4%)
  other arithmetic  40 us (4%)
  between operations  14.6 us (1%)
    psum x1, waiting for transfers between devices, body(): grams = lax.psum(grams / dof_count, 'slab')  603 us
    dot_general x30, matrix products, element_nodes(): jnp.einsum('rs,sgxyz->rgxyz', stiffness, local, precision=highest)  106 us
    ppermute x5, waiting for transfers between devices, with_halo(): lax.ppermute(tail, axis, [(i, (i + 1) % count) for i in range(ends)])  33.6 us
    dynamic_slice x60, local copies, waits for them, and re-layouts, apply_grouped(): nodes = lax.map(apply_block, blocks)  26.9 us
    ppermute x5, starting transfers between devices, with_halo(): lax.ppermute(head, axis, [((i + 1) % count, i) for i in range(ends)])  25.3 us
    dynamic_update_slice x30, local copies, waits for them, and re-layouts, apply_grouped(): nodes = lax.map(apply_block, blocks)  20.2 us
  transfers between devices with their start and end apart: 13, of which 12 were waited for; matrix products, arithmetic and copies ran while one was open for 4% of the time, Pallas kernels for 0%

commit v1 on v0

v1 whole, which is shorter than its diff:
```python
from functools import partial

import jax
import jax.numpy as jnp
from jax import lax
from jax.experimental import pallas as pl
from jax.experimental.pallas import tpu as pltpu
from jax.sharding import Mesh, PartitionSpec as P

CENTER = 110.0
HALF = 90.0
SLAB = ("xh", "z", "y")
MODE = ("xl", "core")
STEPS = (0, 1, -1)
VMEM_LIMIT = 48 * 1024 * 1024


def spec(shape):
    return jax.ShapeDtypeStruct(shape, jnp.float32)


def own_index(dz, q, e, dy, c, p):
    return ((((STEPS.index(dz) * 2 + q) * 3 + e) * 3 + STEPS.index(dy)) * 3 + c) * 2 + p


def halo_index(dz, side, e, dy, c):
    return (((STEPS.index(dz) * 2 + side) * 3 + e) * 3 + STEPS.index(dy)) * 3 + c


def rolled(x, by, axis):
    by = by % x.shape[axis]
    return x if by == 0 else pltpu.roll(x, by, axis)


def coefficient_kernel(stiff_ref, layers_ref, own_ref, halo_ref):
    turned = {}
    for layer in range(3):
        for b in range(2):
            for d in range(2):
                turned[layer, b, d] = rolled(rolled(layers_ref[layer], b, 0), d, 1)
    for p in range(2):
        for q in range(-1, 3):
            dx = q - p
            if abs(dx) > 1:
                continue
            for dy in STEPS:
                for dz in STEPS:
                    corners = [
                        (a, b, d)
                        for a in range(2)
                        for b in range(2)
                        for d in range(2)
                        if 0 <= a + dx <= 1 and 0 <= b + dy <= 1 and 0 <= d + dz <= 1
                    ]
                    for c in range(3):
                        for e in range(3):
                            total = None
                            for a, b, d in corners:
                                row = 3 * (4 * a + 2 * b + d) + c
                                col = 3 * (4 * (a + dx) + 2 * (b + dy) + d + dz) + e
                                term = stiff_ref[row, col] * turned[p - a + 1, b + dy, d]
                                total = term if total is None else total + term
                            if 0 <= q <= 1:
                                own_ref[own_index(dz, q, e, dy, c, p)] = total
                            else:
                                halo_ref[halo_index(dz, 0 if q < 0 else 1, e, dy, c)] = total


def coefficients(stiffness, layers):
    rows, depth = layers.shape[1:]
    return pl.pallas_call(
        coefficient_kernel,
        in_specs=[pl.BlockSpec(memory_space=pltpu.SMEM), pl.BlockSpec(memory_space=pltpu.VMEM)],
        out_specs=[pl.BlockSpec(memory_space=pltpu.VMEM)] * 2,
        out_shape=[spec((324, rows, depth)), spec((162, rows, depth))],
        compiler_params=pltpu.CompilerParams(vmem_limit_bytes=VMEM_LIMIT),
    )(stiffness, layers)


PAIR = 2


def gathered(acc):
    return acc[0] + rolled(acc[1], -1, 0) + rolled(acc[2], 1, 0)


def own_kernel(low_ref, high_ref, coef_ref, part_ref):
    planes = (low_ref, high_ref)

    def pair(i, _):
        base = i * (3 * PAIR)
        acc = {}
        for dz in STEPS:
            for q in range(2):
                for e in range(3):
                    fields = [rolled(planes[q][base + 3 * u + e], -dz, 1) for u in range(PAIR)]
                    for s, dy in enumerate(STEPS):
                        for c in range(3):
                            for p in range(2):
                                coef = coef_ref[own_index(dz, q, e, dy, c, p)]
                                for u in range(PAIR):
                                    term = coef * fields[u]
                                    key = (u, c, p, s)
                                    acc[key] = acc[key] + term if key in acc else term
        for u in range(PAIR):
            for c in range(3):
                for p in range(2):
                    part_ref[base + 3 * u + c, p] = gathered([acc[u, c, p, s] for s in range(3)])
        return 0

    lax.fori_loop(0, low_ref.shape[0] // (3 * PAIR), pair, 0)


def block(shape):
    return pl.BlockSpec(shape, lambda i: (i,) + (0,) * (len(shape) - 1))


def whole(shape):
    return pl.BlockSpec(shape, lambda i: (0,) * len(shape))


def cost(flops, nbytes):
    return pl.CostEstimate(flops=flops, bytes_accessed=nbytes, transcendentals=0)


GRID = 4


def own_part(low, high, coef):
    count, rows, depth = low.shape
    tile = count // GRID
    return pl.pallas_call(
        own_kernel,
        grid=(GRID,),
        in_specs=[block((tile, rows, depth)), block((tile, rows, depth)), whole(coef.shape)],
        out_specs=block((tile, 2, rows, depth)),
        out_shape=spec((count, 2, rows, depth)),
        cost_estimate=cost(2 * 108 * count * rows * depth, 4 * (4 * count + 324) * rows * depth),
        compiler_params=pltpu.CompilerParams(vmem_limit_bytes=VMEM_LIMIT),
    )(low, high, coef)


def halo_body(lower_ref, upper_ref, part_ref, coef_ref, base):
    sides = (lower_ref, upper_ref)
    acc = {}
    for dz in STEPS:
        for side in range(2):
            for e in range(3):
                fields = [rolled(sides[side][base + 3 * u + e], -dz, 1) for u in range(PAIR)]
                for s, dy in enumerate(STEPS):
                    for c in range(3):
                        coef = coef_ref[halo_index(dz, side, e, dy, c)]
                        for u in range(PAIR):
                            term = coef * fields[u]
                            key = (u, c, side, s)
                            acc[key] = acc[key] + term if key in acc else term
    force = {}
    for u in range(PAIR):
        for c in range(3):
            for p in range(2):
                near = gathered([acc[u, c, p, s] for s in range(3)])
                force[u, c, p] = part_ref[base + 3 * u + c, p] + near
    return force


def step_kernel(first, last, *refs):
    lower_ref, upper_ref, part_ref, coef_ref, scale_ref, low_ref, high_ref = refs[:7]
    if first:
        outs = refs[7:]
    else:
        before = refs[7:9]
        outs = refs[9:]
    current = (low_ref, high_ref)

    def pair(i, _):
        base = i * (3 * PAIR)
        force = halo_body(lower_ref, upper_ref, part_ref, coef_ref, base)
        for u in range(PAIR):
            for c in range(3):
                for p in range(2):
                    at = base + 3 * u + c
                    value = scale_ref[p] * force[u, c, p] - (CENTER / HALF) * current[p][at]
                    if not first:
                        value = 2.0 * value - before[p][at]
                    outs[p][at] = value
                    if last:
                        outs[2][at, p] = value
        return 0

    lax.fori_loop(0, low_ref.shape[0] // (3 * PAIR), pair, 0)


def step(first, last, lower, upper, part, coef, scale, current, before):
    count, rows, depth = lower.shape
    tile = count // GRID
    plane = block((tile, rows, depth))
    both = block((tile, 2, rows, depth))
    args = [lower, upper, part, coef, scale, *current] + ([] if first else list(before))
    return pl.pallas_call(
        partial(step_kernel, first, last),
        grid=(GRID,),
        in_specs=[plane, plane, both, whole(coef.shape), whole(scale.shape)]
        + [plane] * (len(args) - 5),
        out_specs=[plane, plane] + ([both] if last else []),
        out_shape=[spec(lower.shape)] * 2 + ([spec((count, 2, rows, depth))] if last else []),
        cost_estimate=cost(2 * 54 * count * rows * depth, 4 * (10 * count + 162) * rows * depth),
        compiler_params=pltpu.CompilerParams(vmem_limit_bytes=VMEM_LIMIT),
    )(*args)


def force_kernel(lower_ref, upper_ref, part_ref, coef_ref, free_ref, out_ref):
    def pair(i, _):
        base = i * (3 * PAIR)
        force = halo_body(lower_ref, upper_ref, part_ref, coef_ref, base)
        for u in range(PAIR):
            for c in range(3):
                for p in range(2):
                    out_ref[base + 3 * u + c, p] = free_ref[p] * force[u, c, p]
        return 0

    lax.fori_loop(0, lower_ref.shape[0] // (3 * PAIR), pair, 0)


def forced(lower, upper, part, coef, free):
    count, rows, depth = lower.shape
    tile = count // GRID
    plane = block((tile, rows, depth))
    both = block((tile, 2, rows, depth))
    return pl.pallas_call(
        force_kernel,
        grid=(GRID,),
        in_specs=[plane, plane, both, whole(coef.shape), whole(free.shape)],
        out_specs=both,
        out_shape=spec((count, 2, rows, depth)),
        cost_estimate=cost(2 * 54 * count * rows * depth, 4 * (6 * count + 162) * rows * depth),
        compiler_params=pltpu.CompilerParams(vmem_limit_bytes=VMEM_LIMIT),
    )(lower, upper, part, coef, free)


def split(x):
    top = x.astype(jnp.bfloat16)
    return top, (x - top.astype(jnp.float32)).astype(jnp.bfloat16)


def dot_t(a, b):
    return lax.dot_general(a, b, (((1,), (1,)), ((), ())), preferred_element_type=jnp.float32)


def gram_kernel(stiff_ref, mass_ref, *refs):
    fields, out_ref = refs[:4], refs[4]
    modes = out_ref.shape[1]
    nodes = mass_ref.shape[0]
    comps = stiff_ref.shape[0] // (modes * nodes)

    out_ref[...] = jnp.zeros_like(out_ref)

    def slice_at(ref, c, n):
        return ref[pl.ds(c * nodes + n, modes, stride=comps * nodes), :]

    def some(n, _):
        weight = mass_ref[pl.ds(n, 1), :]
        for c in range(comps):
            own = slice_at(fields[0], c, n)
            left = jnp.concatenate([slice_at(stiff_ref, c, n), own * weight], 0)
            left_top, left_rest = split(left)
            for r in range(4):
                top, rest = split(own if r == 0 else slice_at(fields[r], c, n))
                out = dot_t(left_top, top) + (dot_t(left_top, rest) + dot_t(left_rest, top))
                out_ref[r] = out_ref[r] + jnp.concatenate([out[:modes], out[modes:]], 1)
        return 0

    lax.fori_loop(0, nodes, some, 0)


def gram(stiff, mass, fields, modes):
    return pl.pallas_call(
        gram_kernel,
        out_shape=spec((4, modes, 2 * modes)),
        compiler_params=pltpu.CompilerParams(vmem_limit_bytes=VMEM_LIMIT),
    )(stiff, mass, *fields)


def total_over(x, axis):
    count = lax.axis_size(axis)
    parts = [
        lax.ppermute(x, axis, [(i, (i + k) % count) for i in range(count)]) for k in range(1, count)
    ]
    for part in parts:
        x = x + part
    return x


def body(subspace, modulus, mass, support, stiffness):
    modes, comps, planes, rows, depth = subspace.shape
    slabs = lax.axis_size(SLAB)
    up = [(i, (i + 1) % slabs) for i in range(slabs)]
    down = [((i + 1) % slabs, i) for i in range(slabs)]
    lower_layer = lax.ppermute(modulus[planes - 1 :], SLAB, up)
    free = (1 - support).astype(jnp.float32)

    def masked(p):
        return (free[p] * subspace[:, :, p]).reshape(modes * comps, rows, depth)

    current = (masked(0), masked(1))
    layers = jnp.concatenate([lower_layer, modulus], 0)
    plane_index = (
        lax.axis_index(SLAB) * planes - 1 + lax.broadcasted_iota(jnp.int32, layers.shape, 0)
    )
    row_index = lax.broadcasted_iota(jnp.int32, layers.shape, 1)
    depth_index = lax.broadcasted_iota(jnp.int32, layers.shape, 2)
    valid = (
        (plane_index >= 0)
        & (plane_index < planes * slabs - 1)
        & (row_index < rows - 1)
        & (depth_index < depth - 1)
    )
    layers = jnp.where(valid, layers, jnp.zeros_like(layers))
    own_coef, halo_coef = coefficients(stiffness, layers)
    scale = free / (mass * HALF)

    before = None
    filtered = None
    for k in range(4):
        lower = lax.ppermute(current[1], SLAB, up)
        upper = lax.ppermute(current[0], SLAB, down)
        part = own_part(*current, own_coef)
        result = step(k == 0, k == 3, lower, upper, part, halo_coef, scale, current, before)
        before, current = current, result[:2]
        if k == 3:
            filtered = result[2]
    swap = [(0, 1), (1, 0)]
    lower = lax.ppermute(current[1], SLAB, up)
    upper = lax.ppermute(current[0], SLAB, down)
    by_x = lax.ppermute(filtered, "xl", swap)
    by_core = lax.ppermute(filtered, "core", swap)
    part = own_part(*current, own_coef)
    by_both = lax.ppermute(by_x, "core", swap)
    stiffened = forced(lower, upper, part, halo_coef, free)
    flat = (-1, depth)
    fields = [a.reshape(flat) for a in (filtered, by_core, by_x, by_both)]
    grams = gram(stiffened.reshape(flat), mass.reshape(flat), fields, modes)
    for axis in SLAB[::-1]:
        grams = total_over(grams, axis)
    grams = grams / (float(comps) * planes * slabs * rows * depth)
    swapped = lax.axis_index("core") == 1
    grams = jnp.where(swapped, grams[jnp.array([1, 0, 3, 2])], grams)
    swapped = lax.axis_index("xl") == 1
    grams = jnp.where(swapped, grams[jnp.array([2, 3, 0, 1])], grams)
    grams = grams.reshape(4, modes, 2, modes).transpose(2, 1, 0, 3).reshape(2, modes, 4 * modes)
    return filtered.reshape(modes, comps, planes, rows, depth), grams[0], grams[1]


def solution(mesh):
    finer = Mesh(mesh.devices.reshape(2, 8, 4, 2, 2), SLAB + MODE)
    placed = (
        P(MODE, None, SLAB, None, None),
        P(SLAB, None, None),
        P(SLAB, None, None),
        P(SLAB, None, None),
        P(),
    )
    return jax.shard_map(
        body,
        mesh=finer,
        in_specs=placed,
        out_specs=(P(MODE, None, SLAB, None, None), P(MODE, None), P(MODE, None)),
        check_vma=False,
    )
```

time: 1000 us -> 210 us (0.21)
  waiting for transfers between devices: 675 us -> 75.4 us
  matrix products: 118 us -> 0 us
  local copies, waits for them, and re-layouts: 94.8 us -> 8.07 us
  Pallas kernels: 0 us -> 58.4 us
  other arithmetic: 40 us -> 1.02 us
  starting transfers between devices: 44.8 us -> 63.9 us
  between operations: 14.6 us -> 1.02 us
    psum x1 -> x0, waiting for transfers between devices: 603 us -> none  [body(): grams = lax.psum(grams / dof_count, 'slab')]
    dot_general x32 -> x0, matrix products: 118 us -> none  [the longest x30 106 us: element_nodes(): jnp.einsum('rs,sgxyz->rgxyz', stiffness, local, precision=highest)]
    pallas_call x0 -> x12, Pallas kernels: none -> 58.4 us  [the longest x5 27.3 us: own_part(): pl.pallas_call(own_kernel, grid=(GRID,), in_specs=[block((tile, rows, dep...]
    dynamic_slice x60 -> x0, local copies, waits for them, and re-layouts: 26.9 us -> none  [apply_grouped(): nodes = lax.map(apply_block, blocks)]
    ppermute x11 -> x25, waiting for transfers between devices: 54.1 us -> 75.4 us  [the longest x5 23.4 us: body(): lower = lax.ppermute(current[1], SLAB, up)]
    dynamic_update_slice x30 -> x0, local copies, waits for them, and re-layouts: 20.2 us -> none  [apply_grouped(): nodes = lax.map(apply_block, blocks)]
    ppermute x11 -> x25, starting transfers between devices: 44.5 us -> 63.9 us  [the longest x11 31.8 us: total_over(): lax.ppermute(x, axis, [(i, (i + k) % count) for i in range(count)])]
    broadcast_in_dim x30 -> x0, other arithmetic: 18.5 us -> none  [apply_grouped(): nodes = lax.map(apply_block, blocks)]
  transfers between devices with their start and end apart: 13 -> 25, of which waited for: 12 -> 14; matrix products, arithmetic and copies ran while one was open for 4% -> 1% of each run, Pallas kernels for 0% -> 15%
where the time goes in v1:
time: 210 us; the launch traced here: 208 us
  waiting for transfers between devices  75.4 us (36%)
  starting transfers between devices  63.9 us (30%)
  Pallas kernels  58.4 us (28%)
  local copies, waits for them, and re-layouts  8.07 us (4%)
    ppermute x11, starting transfers between devices, total_over(): lax.ppermute(x, axis, [(i, (i + k) % count) for i in range(count)])  31.8 us
    pallas_call x5, Pallas kernels, own_part(): pl.pallas_call(own_kernel, grid=(GRID,), in_specs=[block((tile, rows, dep...  27.3 us
    ppermute x5, starting transfers between devices, body(): upper = lax.ppermute(current[0], SLAB, down)  23.9 us
    ppermute x5, waiting for transfers between devices, body(): lower = lax.ppermute(current[1], SLAB, up)  23.4 us
    ppermute x1, waiting for transfers between devices, body(): by_x = lax.ppermute(filtered, 'xl', swap)  22.5 us
    ppermute x11, waiting for transfers between devices, total_over(): lax.ppermute(x, axis, [(i, (i + k) % count) for i in range(count)])  21.7 us
    pallas_call x4, Pallas kernels, step(): pl.pallas_call(partial(step_kernel, first, last), grid=(GRID,), in_specs=...  18.5 us
    pallas_call x1, Pallas kernels, gram(): pl.pallas_call(gram_kernel, out_shape=spec((4, modes, 2 * modes)), compil...  7.95 us
  transfers between devices with their start and end apart: 25, of which 14 were waited for; matrix products, arithmetic and copies ran while one was open for 1% of the time, Pallas kernels for 15%

profile of v1, /device:TPU:32, one launch (start us, length us, event | category | flops | bytes accessed | tf_op | source)
XLA Modules:
  0.0 207.9 jit_solution(7096305053986500907)
XLA Ops:
  6.7 2.6 %collective-permute-start.1 = (f32[144,8,128]{2,1,0:T(8,128)S(1)}, f32[144,8,128]{2,1,0:T(8,128)S(1)}, u32[]{:S(2)}, u32[]{:S(2)}) collective-permute-start(f32[144,8,128]{2,1,0:T(8,128)S(1)} %bitcast_multiply_fusion.low_ref.refs_5_.refs_7_), channel_id=1, source_target_pairs={{4,0},{8,4},{12,8},{16,12},{20,16},{24,20},{28,24},{32,28},{36,32}... | collective-permute-start | bytes 1769480 | tf_op jit(solution)/shard_map/ppermute | solution.py:325
  10.7 5.5 %shard_map.95.refs_2_ = f32[144,2,8,128]{3,2,1,0:T(8,128)S(1)} custom-call(f32[144,8,128]{2,1,0:T(8,128)S(1)} %bitcast_multiply_fusion.low_ref.refs_5_.refs_7_, f32[144,8,128]{2,1,0:T(8,128)S(1)} %bitcast_multiply_fusion.1.high_ref.refs_6_.refs_8_, f32[324,8,128]{2,1,0:T(8,128)S(1)} %get-tuple-element.14.coef_ref), custom_call_target="tpu_custom_call" | custom-call | flops 31850496 | bytes 3686400 | tf_op jit(solution)/shard_map/pallas_call | solution.py:132
  16.2 5.8 %collective-permute-done.refs_0_ = f32[144,8,128]{2,1,0:T(8,128)S(1)} collective-permute-done((f32[144,8,128]{2,1,0:T(8,128)S(1)}, f32[144,8,128]{2,1,0:T(8,128)S(1)}, u32[]{:S(2)}, u32[]{:S(2)}) %collective-permute-start) | collective-permute-done | bytes 589856 | tf_op jit(solution)/shard_map/ppermute | solution.py:324
  22.0 3.6 %shard_map.96 = (f32[144,8,128]{2,1,0:T(8,128)S(1)}, f32[144,8,128]{2,1,0:T(8,128)S(1)}) custom-call(f32[144,8,128]{2,1,0:T(8,128)S(1)} %collective-permute-done.refs_0_, f32[144,8,128]{2,1,0:T(8,128)S(1)} %collective-permute-done.1.refs_1_, f32[144,2,8,128]{3,2,1,0:T(8,128)S(1)} %shard_map.95.refs_2_, ...), custom_call_target="tpu_custom_call" | custom-call | flops 15925248 | bytes 6561792 | tf_op jit(solution)/shard_map/pallas_call | solution.py:199
  26.2 3.5 %collective-permute-start.4 = (f32[144,8,128]{2,1,0:T(8,128)S(1)}, f32[144,8,128]{2,1,0:T(8,128)S(1)}, u32[]{:S(2)}, u32[]{:S(2)}) collective-permute-start(f32[144,8,128]{2,1,0:T(8,128)S(1)} %get-tuple-element.17.low_ref.refs_5_.refs_7_), channel_id=1, source_target_pairs={{4,0},{8,4},{12,8},{16,12},{20,16},{24,20},{28,24},{32,28},{36,32}... | collective-permute-start | bytes 1769480 | tf_op jit(solution)/shard_map/ppermute | solution.py:325
  29.8 5.5 %shard_map.97.refs_2_ = f32[144,2,8,128]{3,2,1,0:T(8,128)S(1)} custom-call(f32[144,8,128]{2,1,0:T(8,128)S(1)} %get-tuple-element.17.low_ref.refs_5_.refs_7_, f32[144,8,128]{2,1,0:T(8,128)S(1)} %get-tuple-element.16.high_ref.refs_6_.refs_8_, f32[324,8,128]{2,1,0:T(8,128)S(1)} %get-tuple-element.14.coef_ref), custom_call_target="tpu_custom_call" | custom-call | flops 31850496 | bytes 3686400 | tf_op jit(solution)/shard_map/pallas_call | solution.py:132
  36.3 5.4 %collective-permute-done.3.refs_0_ = f32[144,8,128]{2,1,0:T(8,128)S(1)} collective-permute-done((f32[144,8,128]{2,1,0:T(8,128)S(1)}, f32[144,8,128]{2,1,0:T(8,128)S(1)}, u32[]{:S(2)}, u32[]{:S(2)}) %collective-permute-start.3) | collective-permute-done | bytes 589856 | tf_op jit(solution)/shard_map/ppermute | solution.py:324
  41.6 4.7 %shard_map.98 = (f32[144,8,128]{2,1,0:T(8,128)S(1)}, f32[144,8,128]{2,1,0:T(8,128)S(1)}) custom-call(f32[144,8,128]{2,1,0:T(8,128)S(1)} %collective-permute-done.3.refs_0_, f32[144,8,128]{2,1,0:T(8,128)S(1)} %collective-permute-done.4.refs_1_, f32[144,2,8,128]{3,2,1,0:T(8,128)} %copy-done.1, f32[162,8,128]{2,1,0:T(8,128)S(1)} %get-tuple-element.15.refs_3_.coef_ref, ...), custom_call_target="tpu_custom_call" | custom-call | flops 15925248 | bytes 6561792 | tf_op jit(solution)/shard_map/pallas_call | solution.py:199
  47.8 2.7 %collective-permute-start.6 = (f32[144,8,128]{2,1,0:T(8,128)S(1)}, f32[144,8,128]{2,1,0:T(8,128)S(1)}, u32[]{:S(2)}, u32[]{:S(2)}) collective-permute-start(f32[144,8,128]{2,1,0:T(8,128)S(1)} %get-tuple-element.19.low_ref.refs_5_.refs_7_), channel_id=1, source_target_pairs={{4,0},{8,4},{12,8},{16,12},{20,16},{24,20},{28,24},{32,28},{36,32}... | collective-permute-start | bytes 1769480 | tf_op jit(solution)/shard_map/ppermute | solution.py:325
  50.6 5.5 %shard_map.99.refs_2_ = f32[144,2,8,128]{3,2,1,0:T(8,128)S(1)} custom-call(f32[144,8,128]{2,1,0:T(8,128)S(1)} %get-tuple-element.19.low_ref.refs_5_.refs_7_, f32[144,8,128]{2,1,0:T(8,128)S(1)} %get-tuple-element.18.high_ref.refs_6_.refs_8_, f32[324,8,128]{2,1,0:T(8,128)S(1)} %get-tuple-element.14.coef_ref), custom_call_target="tpu_custom_call" | custom-call | flops 31850496 | bytes 3686400 | tf_op jit(solution)/shard_map/pallas_call | solution.py:132
  57.0 4.5 %collective-permute-done.5.refs_0_ = f32[144,8,128]{2,1,0:T(8,128)S(1)} collective-permute-done((f32[144,8,128]{2,1,0:T(8,128)S(1)}, f32[144,8,128]{2,1,0:T(8,128)S(1)}, u32[]{:S(2)}, u32[]{:S(2)}) %collective-permute-start.5) | collective-permute-done | bytes 589856 | tf_op jit(solution)/shard_map/ppermute | solution.py:324
  61.5 4.7 %shard_map.100 = (f32[144,8,128]{2,1,0:T(8,128)S(1)}, f32[144,8,128]{2,1,0:T(8,128)S(1)}) custom-call(f32[144,8,128]{2,1,0:T(8,128)S(1)} %collective-permute-done.5.refs_0_, f32[144,8,128]{2,1,0:T(8,128)S(1)} %collective-permute-done.6.refs_1_, f32[144,2,8,128]{3,2,1,0:T(8,128)} %copy-done.2, f32[162,8,128]{2,1,0:T(8,128)S(1)} %get-tuple-element.15.refs_3_.coef_ref, ...), custom_call_target="tpu_custom_call" | custom-call | flops 15925248 | bytes 6561792 | tf_op jit(solution)/shard_map/pallas_call | solution.py:199
  67.6 2.8 %collective-permute-start.8 = (f32[144,8,128]{2,1,0:T(8,128)S(1)}, f32[144,8,128]{2,1,0:T(8,128)S(1)}, u32[]{:S(2)}, u32[]{:S(2)}) collective-permute-start(f32[144,8,128]{2,1,0:T(8,128)S(1)} %get-tuple-element.21.low_ref.refs_5_), channel_id=1, source_target_pairs={{4,0},{8,4},{12,8},{16,12},{20,16},{24,20},{28,24},{32,28},{36,32}... | collective-permute-start | bytes 1769480 | tf_op jit(solution)/shard_map/ppermute | solution.py:325
  70.4 5.5 %shard_map.101.refs_2_ = f32[144,2,8,128]{3,2,1,0:T(8,128)S(1)} custom-call(f32[144,8,128]{2,1,0:T(8,128)S(1)} %get-tuple-element.21.low_ref.refs_5_, f32[144,8,128]{2,1,0:T(8,128)S(1)} %get-tuple-element.20.high_ref.refs_6_, f32[324,8,128]{2,1,0:T(8,128)S(1)} %get-tuple-element.14.coef_ref), custom_call_target="tpu_custom_call" | custom-call | flops 31850496 | bytes 3686400 | tf_op jit(solution)/shard_map/pallas_call | solution.py:132
  76.9 3.5 %collective-permute-done.7.refs_0_ = f32[144,8,128]{2,1,0:T(8,128)S(1)} collective-permute-done((f32[144,8,128]{2,1,0:T(8,128)S(1)}, f32[144,8,128]{2,1,0:T(8,128)S(1)}, u32[]{:S(2)}, u32[]{:S(2)}) %collective-permute-start.7) | collective-permute-done | bytes 589856 | tf_op jit(solution)/shard_map/ppermute | solution.py:324
  80.4 5.5 %shard_map.102 = (f32[144,8,128]{2,1,0:T(8,128)S(1)}, f32[144,8,128]{2,1,0:T(8,128)S(1)}, f32[144,2,8,128]{3,2,1,0:T(8,128)}) custom-call(f32[144,8,128]{2,1,0:T(8,128)S(1)} %collective-permute-done.7.refs_0_, f32[144,8,128]{2,1,0:T(8,128)S(1)} %collective-permute-done.8.refs_1_, f32[144,2,8,128]{3,2,1,0:T(8,128)} %copy-done, ...), custom_call_target="tpu_custom_call" | custom-call | flops 15925248 | bytes 6561792 | tf_op jit(solution)/shard_map/pallas_call | solution.py:199
  87.5 22.5 %collective-permute-done.12 = f32[144,2,8,128]{3,2,1,0:T(8,128)S(1)} collective-permute-done((f32[144,2,8,128]{3,2,1,0:T(8,128)}, f32[144,2,8,128]{3,2,1,0:T(8,128)S(1)}, u32[]{:S(2)}, u32[]{:S(2)}) %collective-permute-start.12) | collective-permute-done | bytes 1179680 | tf_op jit(solution)/shard_map/ppermute | solution.py:334
  110.0 12.1 %collective-permute-start.10 = (f32[144,8,128]{2,1,0:T(8,128)S(1)}, f32[144,8,128]{2,1,0:T(8,128)S(1)}, u32[]{:S(2)}, u32[]{:S(2)}) collective-permute-start(f32[144,8,128]{2,1,0:T(8,128)S(1)} %get-tuple-element.24.low_ref), channel_id=1, source_target_pairs={{4,0},{8,4},{12,8},{16,12},{20,16},{24,20},{28,24},{32,28},{36,32}... | collective-permute-start | bytes 1769480 | tf_op jit(solution)/shard_map/ppermute | solution.py:333
  122.1 5.5 %shard_map.103.part_ref = f32[144,2,8,128]{3,2,1,0:T(8,128)S(1)} custom-call(f32[144,8,128]{2,1,0:T(8,128)S(1)} %get-tuple-element.24.low_ref, f32[144,8,128]{2,1,0:T(8,128)S(1)} %get-tuple-element.23.high_ref, f32[324,8,128]{2,1,0:T(8,128)S(1)} %get-tuple-element.14.coef_ref), custom_call_target="tpu_custom_call" | custom-call | flops 31850496 | bytes 3686400 | tf_op jit(solution)/shard_map/pallas_call | solution.py:132
  127.6 7.8 %collective-permute-done.10.upper_ref = f32[144,8,128]{2,1,0:T(8,128)S(1)} collective-permute-done((f32[144,8,128]{2,1,0:T(8,128)S(1)}, f32[144,8,128]{2,1,0:T(8,128)S(1)}, u32[]{:S(2)}, u32[]{:S(2)}) %collective-permute-start.10) | collective-permute-done | bytes 589856 | tf_op jit(solution)/shard_map/ppermute | solution.py:333
  135.3 4.3 %collective-permute-done.9.lower_ref = f32[144,8,128]{2,1,0:T(8,128)S(1)} collective-permute-done((f32[144,8,128]{2,1,0:T(8,128)S(1)}, f32[144,8,128]{2,1,0:T(8,128)S(1)}, u32[]{:S(2)}, u32[]{:S(2)}) %collective-permute-start.9) | collective-permute-done | bytes 589856 | tf_op jit(solution)/shard_map/ppermute | solution.py:332
  139.7 3.5 %shard_map.104 = f32[144,2,8,128]{3,2,1,0:T(8,128)S(1)} custom-call(f32[144,8,128]{2,1,0:T(8,128)S(1)} %collective-permute-done.9.lower_ref, f32[144,8,128]{2,1,0:T(8,128)S(1)} %collective-permute-done.10.upper_ref, f32[144,2,8,128]{3,2,1,0:T(8,128)S(1)} %shard_map.103.part_ref, f32[162,8,128]{2,1,0:T(8,128)S(1)} %get-tuple-element.15.refs_3_.coef_ref, ...), custom_call_target="tpu_custom_call" | custom-call | flops 15925248 | bytes 4202496 | tf_op jit(solution)/shard_map/pallas_call | solution.py:229
  143.2 7.9 %shard_map.105 = f32[4,48,96]{2,1,0:T(8,128)S(1)} custom-call(f32[2304,128]{1,0:T(8,128)S(1)} %bitcast.16, f32[16,128]{1,0:T(8,128)S(1)} %bitcast.22, f32[2304,128]{1,0:T(8,128)S(1)} %bitcast.18, f32[2304,128]{1,0:T(8,128)S(1)} %bitcast.20, f32[2304,128]{1,0:T(8,128)S(1)} %bitcast.19, f32[2304,128]{1,0:T(8,128)S(1)} %bitcast.21), custom_call_target="tpu_custom_call" | custom-call | tf_op jit(solution)/shard_map/pallas_call | solution.py:276
  151.3 3.1 %collective-permute-start.16 = (f32[4,48,96]{2,1,0:T(8,128)S(1)}, f32[4,48,96]{2,1,0:T(8,128)S(1)}, u32[]{:S(2)}, u32[]{:S(2)}) collective-permute-start(f32[4,48,96]{2,1,0:T(8,128)S(1)} %shard_map.105), channel_id=1, source_target_pairs={{0,12},{4,0},{8,4},{12,8},{1,13},{5,1},{9,5},{13,9},{2,14},{6,2},{... | collective-permute-start | bytes 221192 | tf_op jit(solution)/shard_map/ppermute | solution.py:286
  154.5 4.2 %collective-permute-done.14 = f32[4,48,96]{2,1,0:T(8,128)S(1)} collective-permute-done((f32[4,48,96]{2,1,0:T(8,128)S(1)}, f32[4,48,96]{2,1,0:T(8,128)S(1)}, u32[]{:S(2)}, u32[]{:S(2)}) %collective-permute-start.14) | collective-permute-done | bytes 73760 | tf_op jit(solution)/shard_map/ppermute | solution.py:286
  159.4 5.1 %collective-permute-start.18 = (f32[4,48,96]{2,1,0:T(8,128)S(1)}, f32[4,48,96]{2,1,0:T(8,128)S(1)}, u32[]{:S(2)}, u32[]{:S(2)}) collective-permute-start(f32[4,48,96]{2,1,0:T(8,128)S(1)} %add_add_fusion.1), channel_id=1, source_target_pairs={{0,32},{16,48},{32,64},{48,80},{64,96},{80,112},{96,0},{112,16},{1... | collective-permute-start | bytes 221192 | tf_op jit(solution)/shard_map/ppermute | solution.py:286
  164.5 10.4 %collective-permute-start.19 = (f32[4,48,96]{2,1,0:T(8,128)S(1)}, f32[4,48,96]{2,1,0:T(8,128)S(1)}, u32[]{:S(2)}, u32[]{:S(2)}) collective-permute-start(f32[4,48,96]{2,1,0:T(8,128)S(1)} %add_add_fusion.1), channel_id=1, source_target_pairs={{0,48},{16,64},{32,80},{48,96},{64,112},{80,0},{96,16},{112,32},{1... | collective-permute-start | bytes 221192 | tf_op jit(solution)/shard_map/ppermute | solution.py:286
  174.9 7.3 %collective-permute-start.20 = (f32[4,48,96]{2,1,0:T(8,128)S(1)}, f32[4,48,96]{2,1,0:T(8,128)S(1)}, u32[]{:S(2)}, u32[]{:S(2)}) collective-permute-start(f32[4,48,96]{2,1,0:T(8,128)S(1)} %add_add_fusion.1), channel_id=1, source_target_pairs={{0,64},{16,80},{32,96},{48,112},{64,0},{80,16},{96,32},{112,48},{1... | collective-permute-start | bytes 221192 | tf_op jit(solution)/shard_map/ppermute | solution.py:286
  182.2 5.0 %collective-permute-start.21 = (f32[4,48,96]{2,1,0:T(8,128)S(1)}, f32[4,48,96]{2,1,0:T(8,128)S(1)}, u32[]{:S(2)}, u32[]{:S(2)}) collective-permute-start(f32[4,48,96]{2,1,0:T(8,128)S(1)} %add_add_fusion.1), channel_id=1, source_target_pairs={{0,80},{16,96},{32,112},{48,0},{64,16},{80,32},{96,48},{112,64},{1... | collective-permute-start | bytes 221192 | tf_op jit(solution)/shard_map/ppermute | solution.py:286
  187.3 5.8 %collective-permute-done.18 = f32[4,48,96]{2,1,0:T(8,128)S(1)} collective-permute-done((f32[4,48,96]{2,1,0:T(8,128)S(1)}, f32[4,48,96]{2,1,0:T(8,128)S(1)}, u32[]{:S(2)}, u32[]{:S(2)}) %collective-permute-start.18) | collective-permute-done | bytes 73760 | tf_op jit(solution)/shard_map/ppermute | solution.py:286
  194.1 2.6 %collective-permute-done.21 = f32[4,48,96]{2,1,0:T(8,128)S(1)} collective-permute-done((f32[4,48,96]{2,1,0:T(8,128)S(1)}, f32[4,48,96]{2,1,0:T(8,128)S(1)}, u32[]{:S(2)}, u32[]{:S(2)}) %collective-permute-start.21) | collective-permute-done | bytes 73760 | tf_op jit(solution)/shard_map/ppermute | solution.py:286
  199.1 5.7 %collective-permute-done.24 = f32[4,48,96]{2,1,0:T(8,128)S(1)} collective-permute-done((f32[4,48,96]{2,1,0:T(8,128)S(1)}, f32[4,48,96]{2,1,0:T(8,128)S(1)}, u32[]{:S(2)}, u32[]{:S(2)}) %collective-permute-start.24) | collective-permute-done | bytes 73760 | tf_op jit(solution)/shard_map/ppermute | solution.py:286
  (76 shorter events, 22.8 us)
Async XLA Ops:
  1.3 8.1 %collective-permute-start.2 = (f32[1,8,128]{2,1,0:T(8,128)S(1)}, f32[1,8,128]{2,1,0:T(8,128)S(1)}, u32[]{:S(2)}, u32[]{:S(2)}) collective-permute-start(f32[1,8,128]{2,1,0:T(8,128)S(1)} %slice.27), channel_id=1, source_target_pairs={{0,4},{4,8},{8,12},{12,16},{16,20},{20,24},{24,28},{28,32},{32,36}... | collective-permute-start | bytes 12296 | tf_op jit(solution)/shard_map/ppermute | solution.py:298
  4.9 4.5 %copy-start.4 = (f32[2,8,128]{2,1,0:T(8,128)S(1)}, f32[2,8,128]{2,1,0:T(8,128)}, u32[]{:S(2)}) copy-start(f32[2,8,128]{2,1,0:T(8,128)} %param.9) | copy-start | bytes 24580
  4.9 4.5 %copy-start.6 = (s32[2,8,128]{2,1,0:T(8,128)S(1)}, s32[2,8,128]{2,1,0:T(8,128)}, u32[]{:S(2)}) copy-start(s32[2,8,128]{2,1,0:T(8,128)} %param.10) | copy-start | bytes 24580
  4.9 4.5 %copy-start.7 = (f32[2,8,128]{2,1,0:T(8,128)S(1)}, f32[2,8,128]{2,1,0:T(8,128)}, u32[]{:S(2)}) copy-start(f32[2,8,128]{2,1,0:T(8,128)} %param.8) | copy-start | bytes 24580
  5.0 4.6 %copy-start.5 = (f32[24,24]{1,0:T(8,128)S(1)}, f32[24,24]{1,0:T(8,128)}, u32[]{:S(2)}) copy-start(f32[24,24]{1,0:T(8,128)} %stiff_ref.1) | copy-start | bytes 6916
  5.0 17.0 %collective-permute-start = (f32[144,8,128]{2,1,0:T(8,128)S(1)}, f32[144,8,128]{2,1,0:T(8,128)S(1)}, u32[]{:S(2)}, u32[]{:S(2)}) collective-permute-start(f32[144,8,128]{2,1,0:T(8,128)S(1)} %bitcast_multiply_fusion.1.high_ref.refs_6_.refs_8_), channel_id=1, source_target_pairs={{0,4},{4,8},{8,12},{12,16},{16,20},{20,24},{24,28},{28,32},{32,36}... | collective-permute-start | bytes 1769480 | tf_op jit(solution)/shard_map/ppermute | solution.py:324
  6.7 15.3 %collective-permute-start.1 = (f32[144,8,128]{2,1,0:T(8,128)S(1)}, f32[144,8,128]{2,1,0:T(8,128)S(1)}, u32[]{:S(2)}, u32[]{:S(2)}) collective-permute-start(f32[144,8,128]{2,1,0:T(8,128)S(1)} %bitcast_multiply_fusion.low_ref.refs_5_.refs_7_), channel_id=1, source_target_pairs={{4,0},{8,4},{12,8},{16,12},{20,16},{24,20},{28,24},{32,28},{36,32}... | collective-permute-start | bytes 1769480 | tf_op jit(solution)/shard_map/ppermute | solution.py:325
  25.6 16.1 %collective-permute-start.3 = (f32[144,8,128]{2,1,0:T(8,128)S(1)}, f32[144,8,128]{2,1,0:T(8,128)S(1)}, u32[]{:S(2)}, u32[]{:S(2)}) collective-permute-start(f32[144,8,128]{2,1,0:T(8,128)S(1)} %get-tuple-element.16.high_ref.refs_6_.refs_8_), channel_id=1, source_target_pairs={{0,4},{4,8},{8,12},{12,16},{16,20},{20,24},{24,28},{28,32},{32,36}... | collective-permute-start | bytes 1769480 | tf_op jit(solution)/shard_map/ppermute | solution.py:324
  26.2 15.4 %collective-permute-start.4 = (f32[144,8,128]{2,1,0:T(8,128)S(1)}, f32[144,8,128]{2,1,0:T(8,128)S(1)}, u32[]{:S(2)}, u32[]{:S(2)}) collective-permute-start(f32[144,8,128]{2,1,0:T(8,128)S(1)} %get-tuple-element.17.low_ref.refs_5_.refs_7_), channel_id=1, source_target_pairs={{4,0},{8,4},{12,8},{16,12},{20,16},{24,20},{28,24},{32,28},{36,32}... | collective-permute-start | bytes 1769480 | tf_op jit(solution)/shard_map/ppermute | solution.py:325
  46.3 15.1 %collective-permute-start.5 = (f32[144,8,128]{2,1,0:T(8,128)S(1)}, f32[144,8,128]{2,1,0:T(8,128)S(1)}, u32[]{:S(2)}, u32[]{:S(2)}) collective-permute-start(f32[144,8,128]{2,1,0:T(8,128)S(1)} %get-tuple-element.18.high_ref.refs_6_.refs_8_), channel_id=1, source_target_pairs={{0,4},{4,8},{8,12},{12,16},{16,20},{20,24},{24,28},{28,32},{32,36}... | collective-permute-start | bytes 1769480 | tf_op jit(solution)/shard_map/ppermute | solution.py:324
  47.8 13.7 %collective-permute-start.6 = (f32[144,8,128]{2,1,0:T(8,128)S(1)}, f32[144,8,128]{2,1,0:T(8,128)S(1)}, u32[]{:S(2)}, u32[]{:S(2)}) collective-permute-start(f32[144,8,128]{2,1,0:T(8,128)S(1)} %get-tuple-element.19.low_ref.refs_5_.refs_7_), channel_id=1, source_target_pairs={{4,0},{8,4},{12,8},{16,12},{20,16},{24,20},{28,24},{32,28},{36,32}... | collective-permute-start | bytes 1769480 | tf_op jit(solution)/shard_map/ppermute | solution.py:325
  66.2 14.2 %collective-permute-start.7 = (f32[144,8,128]{2,1,0:T(8,128)S(1)}, f32[144,8,128]{2,1,0:T(8,128)S(1)}, u32[]{:S(2)}, u32[]{:S(2)}) collective-permute-start(f32[144,8,128]{2,1,0:T(8,128)S(1)} %get-tuple-element.20.high_ref.refs_6_), channel_id=1, source_target_pairs={{0,4},{4,8},{8,12},{12,16},{16,20},{20,24},{24,28},{28,32},{32,36}... | collective-permute-start | bytes 1769480 | tf_op jit(solution)/shard_map/ppermute | solution.py:324
  67.6 12.8 %collective-permute-start.8 = (f32[144,8,128]{2,1,0:T(8,128)S(1)}, f32[144,8,128]{2,1,0:T(8,128)S(1)}, u32[]{:S(2)}, u32[]{:S(2)}) collective-permute-start(f32[144,8,128]{2,1,0:T(8,128)S(1)} %get-tuple-element.21.low_ref.refs_5_), channel_id=1, source_target_pairs={{4,0},{8,4},{12,8},{16,12},{20,16},{24,20},{28,24},{32,28},{36,32}... | collective-permute-start | bytes 1769480 | tf_op jit(solution)/shard_map/ppermute | solution.py:325
  86.0 24.0 %collective-permute-start.12 = (f32[144,2,8,128]{3,2,1,0:T(8,128)}, f32[144,2,8,128]{3,2,1,0:T(8,128)S(1)}, u32[]{:S(2)}, u32[]{:S(2)}) collective-permute-start(f32[144,2,8,128]{3,2,1,0:T(8,128)} %get-tuple-element.22), channel_id=1, source_target_pairs={{0,2},{2,0},{1,3},{3,1},{4,6},{6,4},{5,7},{7,5},{8,10},{10,8},{9,1... | collective-permute-start | bytes 3538952 | tf_op jit(solution)/shard_map/ppermute | solution.py:334
  87.5 55.7 %collective-permute-start.11 = (f32[144,2,8,128]{3,2,1,0:T(8,128)}, f32[144,2,8,128]{3,2,1,0:T(8,128)S(1)}, u32[]{:S(2)}, u32[]{:S(2)}) collective-permute-start(f32[144,2,8,128]{3,2,1,0:T(8,128)} %get-tuple-element.22), channel_id=1, source_target_pairs={{0,1},{1,0},{2,3},{3,2},{4,5},{5,4},{6,7},{7,6},{8,9},{9,8},{10,11... | collective-permute-start | bytes 3538952 | tf_op jit(solution)/shard_map/ppermute | solution.py:335
  110.0 33.2 %collective-permute-start.13 = (f32[144,2,8,128]{3,2,1,0:T(8,128)S(1)}, f32[144,2,8,128]{3,2,1,0:T(8,128)S(1)}, u32[]{:S(2)}, u32[]{:S(2)}) collective-permute-start(f32[144,2,8,128]{3,2,1,0:T(8,128)S(1)} %collective-permute-done.12), channel_id=1, source_target_pairs={{0,1},{1,0},{2,3},{3,2},{4,5},{5,4},{6,7},{7,6},{8,9},{9,8},{10,11... | collective-permute-start | bytes 3538952 | tf_op jit(solution)/shard_map/ppermute | solution.py:337
  110.0 25.4 %collective-permute-start.10 = (f32[144,8,128]{2,1,0:T(8,128)S(1)}, f32[144,8,128]{2,1,0:T(8,128)S(1)}, u32[]{:S(2)}, u32[]{:S(2)}) collective-permute-start(f32[144,8,128]{2,1,0:T(8,128)S(1)} %get-tuple-element.24.low_ref), channel_id=1, source_target_pairs={{4,0},{8,4},{12,8},{16,12},{20,16},{24,20},{28,24},{32,28},{36,32}... | collective-permute-start | bytes 1769480 | tf_op jit(solution)/shard_map/ppermute | solution.py:333
  122.1 17.6 %collective-permute-start.9 = (f32[144,8,128]{2,1,0:T(8,128)S(1)}, f32[144,8,128]{2,1,0:T(8,128)S(1)}, u32[]{:S(2)}, u32[]{:S(2)}) collective-permute-start(f32[144,8,128]{2,1,0:T(8,128)S(1)} %get-tuple-element.23.high_ref), channel_id=1, source_target_pairs={{0,4},{4,8},{8,12},{12,16},{16,20},{20,24},{24,28},{28,32},{32,36}... | collective-permute-start | bytes 1769480 | tf_op jit(solution)/shard_map/ppermute | solution.py:332
  127.6 15.6 %copy-start.3 = (f32[144,2,8,128]{3,2,1,0:T(8,128)S(1)}, f32[144,2,8,128]{3,2,1,0:T(8,128)}, u32[]{:S(2)}) copy-start(f32[144,2,8,128]{3,2,1,0:T(8,128)} %get-tuple-element.22) | copy-start | bytes 3538948
  143.2 49.9 %copy-start.9 = (s32[4]{0:T(128)S(1)}, s32[4]{0:T(128)}, u32[]{:S(2)}) copy-start(s32[4]{0:T(128)} %constant.64) | copy-start | bytes 52
  151.1 47.9 %copy-start.8 = (s32[4]{0:T(128)S(1)}, s32[4]{0:T(128)}, u32[]{:S(2)}) copy-start(s32[4]{0:T(128)} %constant.65) | copy-start | bytes 52
  151.2 7.5 %collective-permute-start.14 = (f32[4,48,96]{2,1,0:T(8,128)S(1)}, f32[4,48,96]{2,1,0:T(8,128)S(1)}, u32[]{:S(2)}, u32[]{:S(2)}) collective-permute-start(f32[4,48,96]{2,1,0:T(8,128)S(1)} %shard_map.105), channel_id=1, source_target_pairs={{0,4},{4,8},{8,12},{12,0},{1,5},{5,9},{9,13},{13,1},{2,6},{6,10},{... | collective-permute-start | bytes 221192 | tf_op jit(solution)/shard_map/ppermute | solution.py:286
  151.2 7.4 %collective-permute-start.15 = (f32[4,48,96]{2,1,0:T(8,128)S(1)}, f32[4,48,96]{2,1,0:T(8,128)S(1)}, u32[]{:S(2)}, u32[]{:S(2)}) collective-permute-start(f32[4,48,96]{2,1,0:T(8,128)S(1)} %shard_map.105), channel_id=1, source_target_pairs={{0,8},{4,12},{8,0},{12,4},{1,9},{5,13},{9,1},{13,5},{2,10},{6,14},... | collective-permute-start | bytes 221192 | tf_op jit(solution)/shard_map/ppermute | solution.py:286
  151.3 7.9 %collective-permute-start.16 = (f32[4,48,96]{2,1,0:T(8,128)S(1)}, f32[4,48,96]{2,1,0:T(8,128)S(1)}, u32[]{:S(2)}, u32[]{:S(2)}) collective-permute-start(f32[4,48,96]{2,1,0:T(8,128)S(1)} %shard_map.105), channel_id=1, source_target_pairs={{0,12},{4,0},{8,4},{12,8},{1,13},{5,1},{9,5},{13,9},{2,14},{6,2},{... | collective-permute-start | bytes 221192 | tf_op jit(solution)/shard_map/ppermute | solution.py:286
  159.3 28.0 %collective-permute-start.17 = (f32[4,48,96]{2,1,0:T(8,128)S(1)}, f32[4,48,96]{2,1,0:T(8,128)S(1)}, u32[]{:S(2)}, u32[]{:S(2)}) collective-permute-start(f32[4,48,96]{2,1,0:T(8,128)S(1)} %add_add_fusion.1), channel_id=1, source_target_pairs={{0,16},{16,32},{32,48},{48,64},{64,80},{80,96},{96,112},{112,0},{1... | collective-permute-start | bytes 221192 | tf_op jit(solution)/shard_map/ppermute | solution.py:286
  159.4 33.6 %collective-permute-start.18 = (f32[4,48,96]{2,1,0:T(8,128)S(1)}, f32[4,48,96]{2,1,0:T(8,128)S(1)}, u32[]{:S(2)}, u32[]{:S(2)}) collective-permute-start(f32[4,48,96]{2,1,0:T(8,128)S(1)} %add_add_fusion.1), channel_id=1, source_target_pairs={{0,32},{16,48},{32,64},{48,80},{64,96},{80,112},{96,0},{112,16},{1... | collective-permute-start | bytes 221192 | tf_op jit(solution)/shard_map/ppermute | solution.py:286
  164.5 29.6 %collective-permute-start.19 = (f32[4,48,96]{2,1,0:T(8,128)S(1)}, f32[4,48,96]{2,1,0:T(8,128)S(1)}, u32[]{:S(2)}, u32[]{:S(2)}) collective-permute-start(f32[4,48,96]{2,1,0:T(8,128)S(1)} %add_add_fusion.1), channel_id=1, source_target_pairs={{0,48},{16,64},{32,80},{48,96},{64,112},{80,0},{96,16},{112,32},{1... | collective-permute-start | bytes 221192 | tf_op jit(solution)/shard_map/ppermute | solution.py:286
  174.9 19.2 %collective-permute-start.20 = (f32[4,48,96]{2,1,0:T(8,128)S(1)}, f32[4,48,96]{2,1,0:T(8,128)S(1)}, u32[]{:S(2)}, u32[]{:S(2)}) collective-permute-start(f32[4,48,96]{2,1,0:T(8,128)S(1)} %add_add_fusion.1), channel_id=1, source_target_pairs={{0,64},{16,80},{32,96},{48,112},{64,0},{80,16},{96,32},{112,48},{1... | collective-permute-start | bytes 221192 | tf_op jit(solution)/shard_map/ppermute | solution.py:286
  182.2 14.5 %collective-permute-start.21 = (f32[4,48,96]{2,1,0:T(8,128)S(1)}, f32[4,48,96]{2,1,0:T(8,128)S(1)}, u32[]{:S(2)}, u32[]{:S(2)}) collective-permute-start(f32[4,48,96]{2,1,0:T(8,128)S(1)} %add_add_fusion.1), channel_id=1, source_target_pairs={{0,80},{16,96},{32,112},{48,0},{64,16},{80,32},{96,48},{112,64},{1... | collective-permute-start | bytes 221192 | tf_op jit(solution)/shard_map/ppermute | solution.py:286
  187.3 9.5 %collective-permute-start.22 = (f32[4,48,96]{2,1,0:T(8,128)S(1)}, f32[4,48,96]{2,1,0:T(8,128)S(1)}, u32[]{:S(2)}, u32[]{:S(2)}) collective-permute-start(f32[4,48,96]{2,1,0:T(8,128)S(1)} %add_add_fusion.1), channel_id=1, source_target_pairs={{0,96},{16,112},{32,0},{48,16},{64,32},{80,48},{96,64},{112,80},{1... | collective-permute-start | bytes 221192 | tf_op jit(solution)/shard_map/ppermute | solution.py:286
  193.0 5.5 %collective-permute-start.23 = (f32[4,48,96]{2,1,0:T(8,128)S(1)}, f32[4,48,96]{2,1,0:T(8,128)S(1)}, u32[]{:S(2)}, u32[]{:S(2)}) collective-permute-start(f32[4,48,96]{2,1,0:T(8,128)S(1)} %add_add_fusion.1), channel_id=1, source_target_pairs={{0,112},{16,0},{32,16},{48,32},{64,48},{80,64},{96,80},{112,96},{1... | collective-permute-start | bytes 221192 | tf_op jit(solution)/shard_map/ppermute | solution.py:286
  198.6 6.2 %collective-permute-start.24 = (f32[4,48,96]{2,1,0:T(8,128)S(1)}, f32[4,48,96]{2,1,0:T(8,128)S(1)}, u32[]{:S(2)}, u32[]{:S(2)}) collective-permute-start(f32[4,48,96]{2,1,0:T(8,128)S(1)} %add_add_fusion), channel_id=1, source_target_pairs={{0,128},{128,0},{1,129},{129,1},{2,130},{130,2},{3,131},{131,3},{4... | collective-permute-start | bytes 221192 | tf_op jit(solution)/shard_map/ppermute | solution.py:286
  (3 other events, 3.1 us)

commit v2 on v1

v2 whole, which is shorter than its diff:
```python
from functools import partial

import jax
import jax.numpy as jnp
from jax import lax
from jax.experimental import pallas as pl
from jax.experimental.pallas import tpu as pltpu
from jax.sharding import Mesh, PartitionSpec as P

CENTER = 110.0
HALF = 90.0
SLAB = ("xh", "z", "y")
MODE = ("xl", "core")
STEPS = (0, 1, -1)
VMEM_LIMIT = 48 * 1024 * 1024


def spec(shape):
    return jax.ShapeDtypeStruct(shape, jnp.float32)


def own_index(dz, q, e, dy, c, p):
    return ((((STEPS.index(dz) * 2 + q) * 3 + e) * 3 + STEPS.index(dy)) * 3 + c) * 2 + p


def halo_index(dz, side, e, dy, c):
    return (((STEPS.index(dz) * 2 + side) * 3 + e) * 3 + STEPS.index(dy)) * 3 + c


def rolled(x, by, axis):
    by = by % x.shape[axis]
    return x if by == 0 else pltpu.roll(x, by, axis)


def coefficient_kernel(stiff_ref, layers_ref, own_ref, halo_ref):
    turned = {}
    for layer in range(3):
        for b in range(2):
            for d in range(2):
                turned[layer, b, d] = rolled(rolled(layers_ref[layer], b, 0), d, 1)
    for p in range(2):
        for q in range(-1, 3):
            dx = q - p
            if abs(dx) > 1:
                continue
            for dy in STEPS:
                for dz in STEPS:
                    corners = [
                        (a, b, d)
                        for a in range(2)
                        for b in range(2)
                        for d in range(2)
                        if 0 <= a + dx <= 1 and 0 <= b + dy <= 1 and 0 <= d + dz <= 1
                    ]
                    for c in range(3):
                        for e in range(3):
                            total = None
                            for a, b, d in corners:
                                row = 3 * (4 * a + 2 * b + d) + c
                                col = 3 * (4 * (a + dx) + 2 * (b + dy) + d + dz) + e
                                term = stiff_ref[row, col] * turned[p - a + 1, b + dy, d]
                                total = term if total is None else total + term
                            if 0 <= q <= 1:
                                own_ref[own_index(dz, q, e, dy, c, p)] = total
                            else:
                                halo_ref[halo_index(dz, 0 if q < 0 else 1, e, dy, c)] = total


def coefficients(stiffness, layers):
    rows, depth = layers.shape[1:]
    return pl.pallas_call(
        coefficient_kernel,
        in_specs=[pl.BlockSpec(memory_space=pltpu.SMEM), pl.BlockSpec(memory_space=pltpu.VMEM)],
        out_specs=[pl.BlockSpec(memory_space=pltpu.VMEM)] * 2,
        out_shape=[spec((324, rows, depth)), spec((162, rows, depth))],
        compiler_params=pltpu.CompilerParams(vmem_limit_bytes=VMEM_LIMIT),
    )(stiffness, layers)


OWN_MODES = 2
HALO_MODES = 4
IN_VMEM = pl.BlockSpec(memory_space=pltpu.VMEM)
ANYWHERE = pl.BlockSpec(memory_space=pl.ANY)


def cost(flops, nbytes):
    return pl.CostEstimate(flops=flops, bytes_accessed=nbytes, transcendentals=0)


def compiled():
    return pltpu.CompilerParams(vmem_limit_bytes=VMEM_LIMIT)


def gathered(acc):
    return acc[0] + rolled(acc[1], -1, 0) + rolled(acc[2], 1, 0)


def added(acc, key, term):
    acc[key] = acc[key] + term if key in acc else term


def own_kernel(shift, count, *refs):
    low_ref, high_ref, coef_ref, scale_ref = refs[:4]
    before, part_ref = refs[4:-1], refs[-1]
    planes = (low_ref, high_ref)

    def some(i, _):
        base = i * (3 * OWN_MODES)
        acc = {}
        for dz in STEPS:
            for q in range(2):
                for e in range(3):
                    fields = [rolled(planes[q][base + 3 * u + e], -dz, 1) for u in range(OWN_MODES)]
                    for s, dy in enumerate(STEPS):
                        for c in range(3):
                            for p in range(2):
                                coef = coef_ref[own_index(dz, q, e, dy, c, p)]
                                for u in range(OWN_MODES):
                                    added(acc, (u, c, p, s), coef * fields[u])
        for u in range(OWN_MODES):
            for c in range(3):
                at = base + 3 * u + c
                for p in range(2):
                    value = scale_ref[p] * gathered([acc[u, c, p, s] for s in range(3)])
                    if shift:
                        value = value - shift * planes[p][at]
                    if before:
                        value = value - before[p][at]
                    part_ref[at, p] = value
        return 0

    lax.fori_loop(0, count // (3 * OWN_MODES), some, 0)


def own_part(shift, current, coef, scale, before):
    count, rows, depth = current[0].shape
    args = (*current, coef, scale, *before)
    return pl.pallas_call(
        partial(own_kernel, shift, count),
        in_specs=[IN_VMEM] * len(args),
        out_specs=IN_VMEM,
        out_shape=spec((count, 2, rows, depth)),
        cost_estimate=cost(2 * 108 * count * rows * depth, 16 << 20),
        compiler_params=compiled(),
    )(*args)


def halo_kernel(count, lower_ref, upper_ref, part_ref, coef_ref, scale_ref, *outs):
    sides = (lower_ref, upper_ref)

    def some(i, _):
        base = i * (3 * HALO_MODES)
        for p in range(2):
            acc = {}
            for dz in STEPS:
                for e in range(3):
                    fields = [rolled(sides[p][base + 3 * u + e], -dz, 1) for u in range(HALO_MODES)]
                    for s, dy in enumerate(STEPS):
                        for c in range(3):
                            coef = coef_ref[halo_index(dz, p, e, dy, c)]
                            for u in range(HALO_MODES):
                                added(acc, (u, c, s), coef * fields[u])
            for u in range(HALO_MODES):
                for c in range(3):
                    at = base + 3 * u + c
                    near = gathered([acc[u, c, s] for s in range(3)])
                    value = part_ref[at, p] + scale_ref[p] * near
                    if len(outs) > 1:
                        outs[p][at] = value
                    if len(outs) != 2:
                        outs[-1][at, p] = value
        return 0

    lax.fori_loop(0, count // (3 * HALO_MODES), some, 0)


def with_halo(lower, upper, part, coef, scale, outs, passed=None):
    count, rows, depth = lower.shape
    plane, both = spec(lower.shape), spec(part.shape)
    shapes = {1: [both], 2: [plane] * 2, 3: [plane, plane, both]}[outs]
    args = [lower, upper, part, coef, scale]
    specs, out_specs = [IN_VMEM] * 5, [IN_VMEM] * outs
    kernel = partial(halo_kernel, count)
    aliases = {}
    if passed is not None:
        args, specs = args + [passed], specs + [ANYWHERE]
        shapes, out_specs = shapes + [spec(passed.shape)], out_specs + [ANYWHERE]
        aliases = {5: outs}

        def kernel(*refs):
            halo_kernel(count, *refs[:5], *refs[6:-1])

    return pl.pallas_call(
        kernel,
        in_specs=specs,
        out_specs=out_specs,
        out_shape=shapes,
        input_output_aliases=aliases,
        cost_estimate=cost(2 * 54 * count * rows * depth, 9 << 20),
        compiler_params=compiled(),
    )(*args)


def split(x):
    top = x.astype(jnp.bfloat16)
    return top, (x - top.astype(jnp.float32)).astype(jnp.bfloat16)


def dot_t(a, b):
    return lax.dot_general(a, b, (((1,), (1,)), ((), ())), preferred_element_type=jnp.float32)


def gram_kernel(factor, place_ref, stiff_ref, mass_ref, *refs):
    fields, out_ref = refs[:4], refs[4]
    left_top, left_rest, top, rest, turned = refs[5:]
    modes = out_ref.shape[0] // 2
    nodes, depth = mass_ref.shape
    comps = stiff_ref.shape[0] // (modes * nodes)

    def some(n, _):
        weight = mass_ref[pl.ds(n, 1), :]
        for c in range(comps):
            row = c * nodes + n
            at = pl.ds(pl.multiple_of(row * depth, depth), depth)
            for r in range(4):
                value = fields[r][pl.ds(row, modes, stride=comps * nodes), :]
                rows = pl.ds(r * modes, modes)
                top[rows, at], rest[rows, at] = split(value)
                if r == 0:
                    rows = pl.ds(modes, modes)
                    left_top[rows, at], left_rest[rows, at] = split(value * weight)
            value = stiff_ref[pl.ds(row, modes, stride=comps * nodes), :]
            rows = pl.ds(0, modes)
            left_top[rows, at], left_rest[rows, at] = split(value)
        return 0

    lax.fori_loop(0, nodes, some, 0)
    total = dot_t(top[...], left_top[...])
    total = total + dot_t(rest[...], left_top[...])
    total = (total + dot_t(top[...], left_rest[...])) * factor
    for r in range(4):
        at = pl.ds(pl.multiple_of(place_ref[r] * modes, modes), modes)
        turned[at, :] = total[r * modes : (r + 1) * modes]
    out_ref[...] = turned[...].T


def gram(factor, place, stiff, mass, fields, modes):
    wide = stiff.size // modes
    return pl.pallas_call(
        partial(gram_kernel, factor),
        in_specs=[pl.BlockSpec(memory_space=pltpu.SMEM)] + [IN_VMEM] * 6,
        out_specs=IN_VMEM,
        out_shape=spec((2 * modes, 4 * modes)),
        scratch_shapes=[
            pltpu.VMEM((2 * modes, wide), jnp.bfloat16),
            pltpu.VMEM((2 * modes, wide), jnp.bfloat16),
            pltpu.VMEM((4 * modes, wide), jnp.bfloat16),
            pltpu.VMEM((4 * modes, wide), jnp.bfloat16),
            pltpu.VMEM((4 * modes, 2 * modes), jnp.float32),
        ],
        compiler_params=compiled(),
    )(place, stiff, mass, *fields)


def total_over(x, axes, groups):
    above, count, below = groups
    parts = []
    for k in range(1, count):
        pairs = [
            ((i * count + j) * below + l, (i * count + (j + k) % count) * below + l)
            for i in range(above)
            for j in range(count)
            for l in range(below)
        ]
        parts.append(lax.ppermute(x, axes, pairs))
    for part in parts:
        x = x + part
    return x


def body(subspace, modulus, mass, support, stiffness):
    modes, comps, planes, rows, depth = subspace.shape
    slabs = lax.axis_size(SLAB)
    up = [(i, (i + 1) % slabs) for i in range(slabs)]
    down = [((i + 1) % slabs, i) for i in range(slabs)]
    lower_layer = lax.ppermute(modulus[planes - 1 :], SLAB, up)
    free = (1 - support).astype(jnp.float32)

    def masked(p):
        return (free[p] * subspace[:, :, p]).reshape(modes * comps, rows, depth)

    current = (masked(0), masked(1))
    layers = jnp.concatenate([lower_layer, modulus], 0)
    plane_index = (
        lax.axis_index(SLAB) * planes - 1 + lax.broadcasted_iota(jnp.int32, layers.shape, 0)
    )
    row_index = lax.broadcasted_iota(jnp.int32, layers.shape, 1)
    depth_index = lax.broadcasted_iota(jnp.int32, layers.shape, 2)
    valid = (
        (plane_index >= 0)
        & (plane_index < planes * slabs - 1)
        & (row_index < rows - 1)
        & (depth_index < depth - 1)
    )
    layers = jnp.where(valid, layers, jnp.zeros_like(layers))
    own_coef, halo_coef = coefficients(stiffness, layers)
    scale = free / (mass * HALF)

    before = ()
    for k in range(4):
        times = 1.0 if k == 0 else 2.0
        lower = lax.ppermute(current[1], SLAB, up)
        upper = lax.ppermute(current[0], SLAB, down)
        part = own_part(times * CENTER / HALF, current, own_coef, times * scale, before)
        result = with_halo(lower, upper, part, halo_coef, times * scale, 3 if k == 3 else 2)
        before, current = current, tuple(result[:2])
    filtered = result[2]
    swap = [(0, 1), (1, 0)]
    lower = lax.ppermute(current[1], SLAB, up)
    upper = lax.ppermute(current[0], SLAB, down)
    by_x = lax.ppermute(filtered, "xl", swap)
    by_core = lax.ppermute(filtered, "core", swap)
    part = own_part(0.0, current, own_coef, free, ())
    stiffened, by_x = with_halo(lower, upper, part, halo_coef, free, 1, by_x)
    by_both = lax.ppermute(by_x, "core", swap)
    flat = (-1, depth)
    fields = [a.reshape(flat) for a in (filtered, by_core, by_x, by_both)]
    me = lax.axis_index(MODE)
    place = jnp.stack([me ^ r for r in range(4)]).astype(jnp.int32)
    factor = 1.0 / (float(comps) * planes * slabs * rows * depth)
    grams = gram(factor, place, stiffened.reshape(flat), mass.reshape(flat), fields, modes)
    for groups in ((16, 4, 1), (4, 4, 4), (2, 2, 16), (1, 2, 32)):
        grams = total_over(grams, SLAB, groups)
    return filtered.reshape(subspace.shape), grams[:modes], grams[modes:]


def solution(mesh):
    finer = Mesh(mesh.devices.reshape(2, 8, 4, 2, 2), SLAB + MODE)
    placed = (
        P(MODE, None, SLAB, None, None),
        P(SLAB, None, None),
        P(SLAB, None, None),
        P(SLAB, None, None),
        P(),
    )
    return jax.shard_map(
        body,
        mesh=finer,
        in_specs=placed,
        out_specs=(P(MODE, None, SLAB, None, None), P(MODE, None), P(MODE, None)),
        check_vma=False,
    )
```

time: 210 us -> 181 us (0.86)
  waiting for transfers between devices: 75.4 us -> 57.3 us
  Pallas kernels: 58.4 us -> 51.8 us
  local copies, waits for them, and re-layouts: 8.07 us -> 5 us
    ppermute x1, waiting for transfers between devices: 22.5 us -> 5.44 us  [body(): by_x = lax.ppermute(filtered, 'xl', swap)]
    ppermute x11 -> x8, starting transfers between devices: 31.8 us -> 40.9 us  [total_over(): parts.append(lax.ppermute(x, axes, pairs))]
    ppermute x5, starting transfers between devices: 23.9 us -> 15.6 us  [body(): upper = lax.ppermute(current[0], SLAB, down)]
    pallas_call x11, Pallas kernels: 57.2 us -> 50.6 us  [the longest x5 29.3 us: own_part(): pl.pallas_call(partial(own_kernel, shift, count), in_specs=[IN_VMEM] * le...]
    ppermute x5, waiting for transfers between devices: 7.78 us -> 2.4 us  [body(): upper = lax.ppermute(current[0], SLAB, down)]
    ppermute x1, waiting for transfers between devices: 0.01 us -> 2.9 us  [body(): by_both = lax.ppermute(by_x, 'core', swap)]
    ppermute x11 -> x8, waiting for transfers between devices: 21.7 us -> 21.1 us  [total_over(): parts.append(lax.ppermute(x, axes, pairs))]
  transfers between devices with their start and end apart: 25 -> 22, of which waited for: 14 -> 15; matrix products, arithmetic and copies ran while one was open for 1% -> 1% of each run, Pallas kernels for 15% -> 18%
where the time goes in v2:
time: 181 us
  starting transfers between devices  64.7 us (36%)
  waiting for transfers between devices  57.3 us (32%)
  Pallas kernels  51.8 us (29%)
  local copies, waits for them, and re-layouts  5 us (3%)
    ppermute x8, starting transfers between devices, total_over(): parts.append(lax.ppermute(x, axes, pairs))  40.9 us
    pallas_call x5, Pallas kernels, own_part(): pl.pallas_call(partial(own_kernel, shift, count), in_specs=[IN_VMEM] * le...  29.3 us
    ppermute x5, waiting for transfers between devices, body(): lower = lax.ppermute(current[1], SLAB, up)  25.5 us
    ppermute x8, waiting for transfers between devices, total_over(): parts.append(lax.ppermute(x, axes, pairs))  21.1 us
    ppermute x5, starting transfers between devices, body(): upper = lax.ppermute(current[0], SLAB, down)  15.6 us
    pallas_call x5, Pallas kernels, with_halo(): pl.pallas_call(kernel, in_specs=specs, out_specs=out_specs, out_shape=sha...  14.7 us
    pallas_call x1, Pallas kernels, gram(): pl.pallas_call(partial(gram_kernel, factor), in_specs=[pl.BlockSpec(memor...  6.63 us
    ppermute x1, waiting for transfers between devices, body(): by_x = lax.ppermute(filtered, 'xl', swap)  5.44 us
  transfers between devices with their start and end apart: 22, of which 15 were waited for; matrix products, arithmetic and copies ran while one was open for 1% of the time, Pallas kernels for 18%

profile of v2, /device:TPU:32, one launch (start us, length us, event | category | flops | bytes accessed | tf_op | source)
XLA Modules:
  0.0 180.8 jit_solution(11946756410811163363)
XLA Ops:
  6.7 2.6 %collective-permute-start.1 = (f32[144,8,128]{2,1,0:T(8,128)S(1)}, f32[144,8,128]{2,1,0:T(8,128)S(1)}, u32[]{:S(2)}, u32[]{:S(2)}) collective-permute-start(f32[144,8,128]{2,1,0:T(8,128)S(1)} %bitcast_multiply_fusion.refs_0_.refs_4_), channel_id=1, source_target_pairs={{4,0},{8,4},{12,8},{16,12},{20,16},{24,20},{28,24},{32,28},{36,32}... | collective-permute-start | bytes 1769480 | tf_op jit(solution)/shard_map/ppermute | solution.py:313
  10.7 5.8 %shard_map.77.part_ref = f32[144,2,8,128]{3,2,1,0:T(8,128)S(1)} custom-call(f32[144,8,128]{2,1,0:T(8,128)S(1)} %bitcast_multiply_fusion.refs_0_.refs_4_, f32[144,8,128]{2,1,0:T(8,128)S(1)} %bitcast_multiply_fusion.1.refs_1_.refs_5_, f32[324,8,128]{2,1,0:T(8,128)S(1)} %get-tuple-element.16.refs_2_, f32[2,8,128]{2,1,0:T(8,128)S(1)} %get-tuple-element.30.refs_3_.scale_ref), custom_call_target="tpu_custom_call" | custom-call | flops 31850496 | bytes 16777216 | tf_op jit(solution)/shard_map/pallas_call | solution.py:138
  16.6 5.4 %collective-permute-done.lower_ref = f32[144,8,128]{2,1,0:T(8,128)S(1)} collective-permute-done((f32[144,8,128]{2,1,0:T(8,128)S(1)}, f32[144,8,128]{2,1,0:T(8,128)S(1)}, u32[]{:S(2)}, u32[]{:S(2)}) %collective-permute-start) | collective-permute-done | bytes 589856 | tf_op jit(solution)/shard_map/ppermute | solution.py:312
  22.0 2.7 %shard_map.78 = (f32[144,8,128]{2,1,0:T(8,128)S(1)}, f32[144,8,128]{2,1,0:T(8,128)S(1)}) custom-call(f32[144,8,128]{2,1,0:T(8,128)S(1)} %collective-permute-done.lower_ref, f32[144,8,128]{2,1,0:T(8,128)S(1)} %collective-permute-done.1.upper_ref, f32[144,2,8,128]{3,2,1,0:T(8,128)S(1)} %shard_map.77.part_ref, ...), custom_call_target="tpu_custom_call" | custom-call | flops 15925248 | bytes 9437184 | tf_op jit(solution)/shard_map/pallas_call | solution.py:193
  25.4 3.5 %collective-permute-start.4 = (f32[144,8,128]{2,1,0:T(8,128)S(1)}, f32[144,8,128]{2,1,0:T(8,128)S(1)}, u32[]{:S(2)}, u32[]{:S(2)}) collective-permute-start(f32[144,8,128]{2,1,0:T(8,128)S(1)} %get-tuple-element.19.refs_0_.refs_4_), channel_id=1, source_target_pairs={{4,0},{8,4},{12,8},{16,12},{20,16},{24,20},{28,24},{32,28},{36,32}... | collective-permute-start | bytes 1769480 | tf_op jit(solution)/shard_map/ppermute | solution.py:313
  29.0 5.9 %shard_map.79.part_ref = f32[144,2,8,128]{3,2,1,0:T(8,128)S(1)} custom-call(f32[144,8,128]{2,1,0:T(8,128)S(1)} %get-tuple-element.19.refs_0_.refs_4_, f32[144,8,128]{2,1,0:T(8,128)S(1)} %get-tuple-element.18.refs_1_.refs_5_, f32[324,8,128]{2,1,0:T(8,128)S(1)} %get-tuple-element.16.refs_2_, f32[2,8,128]{2,1,0:T(8,128)S(1)} %get-tuple-element.29.refs_3_.scale_ref, ...), custom_call_target="tpu_custom_call" | custom-call | flops 31850496 | bytes 16777216 | tf_op jit(solution)/shard_map/pallas_call | solution.py:138
  34.9 5.9 %collective-permute-done.3.lower_ref = f32[144,8,128]{2,1,0:T(8,128)S(1)} collective-permute-done((f32[144,8,128]{2,1,0:T(8,128)S(1)}, f32[144,8,128]{2,1,0:T(8,128)S(1)}, u32[]{:S(2)}, u32[]{:S(2)}) %collective-permute-start.3) | collective-permute-done | bytes 589856 | tf_op jit(solution)/shard_map/ppermute | solution.py:312
  40.8 2.7 %shard_map.80 = (f32[144,8,128]{2,1,0:T(8,128)S(1)}, f32[144,8,128]{2,1,0:T(8,128)S(1)}) custom-call(f32[144,8,128]{2,1,0:T(8,128)S(1)} %collective-permute-done.3.lower_ref, f32[144,8,128]{2,1,0:T(8,128)S(1)} %collective-permute-done.4.upper_ref, f32[144,2,8,128]{3,2,1,0:T(8,128)S(1)} %shard_map.79.part_ref, ...), custom_call_target="tpu_custom_call" | custom-call | flops 15925248 | bytes 9437184 | tf_op jit(solution)/shard_map/pallas_call | solution.py:193
  45.1 2.7 %collective-permute-start.6 = (f32[144,8,128]{2,1,0:T(8,128)S(1)}, f32[144,8,128]{2,1,0:T(8,128)S(1)}, u32[]{:S(2)}, u32[]{:S(2)}) collective-permute-start(f32[144,8,128]{2,1,0:T(8,128)S(1)} %get-tuple-element.21.refs_0_.refs_4_), channel_id=1, source_target_pairs={{4,0},{8,4},{12,8},{16,12},{20,16},{24,20},{28,24},{32,28},{36,32}... | collective-permute-start | bytes 1769480 | tf_op jit(solution)/shard_map/ppermute | solution.py:313
  47.8 5.9 %shard_map.81.part_ref = f32[144,2,8,128]{3,2,1,0:T(8,128)S(1)} custom-call(f32[144,8,128]{2,1,0:T(8,128)S(1)} %get-tuple-element.21.refs_0_.refs_4_, f32[144,8,128]{2,1,0:T(8,128)S(1)} %get-tuple-element.20.refs_1_.refs_5_, f32[324,8,128]{2,1,0:T(8,128)S(1)} %get-tuple-element.16.refs_2_, f32[2,8,128]{2,1,0:T(8,128)S(1)} %get-tuple-element.29.refs_3_.scale_ref, ...), custom_call_target="tpu_custom_call" | custom-call | flops 31850496 | bytes 16777216 | tf_op jit(solution)/shard_map/pallas_call | solution.py:138
  53.7 5.0 %collective-permute-done.5.lower_ref = f32[144,8,128]{2,1,0:T(8,128)S(1)} collective-permute-done((f32[144,8,128]{2,1,0:T(8,128)S(1)}, f32[144,8,128]{2,1,0:T(8,128)S(1)}, u32[]{:S(2)}, u32[]{:S(2)}) %collective-permute-start.5) | collective-permute-done | bytes 589856 | tf_op jit(solution)/shard_map/ppermute | solution.py:312
  58.7 2.7 %shard_map.82 = (f32[144,8,128]{2,1,0:T(8,128)S(1)}, f32[144,8,128]{2,1,0:T(8,128)S(1)}) custom-call(f32[144,8,128]{2,1,0:T(8,128)S(1)} %collective-permute-done.5.lower_ref, f32[144,8,128]{2,1,0:T(8,128)S(1)} %collective-permute-done.6.upper_ref, f32[144,2,8,128]{3,2,1,0:T(8,128)S(1)} %shard_map.81.part_ref, ...), custom_call_target="tpu_custom_call" | custom-call | flops 15925248 | bytes 9437184 | tf_op jit(solution)/shard_map/pallas_call | solution.py:193
  62.9 2.8 %collective-permute-start.8 = (f32[144,8,128]{2,1,0:T(8,128)S(1)}, f32[144,8,128]{2,1,0:T(8,128)S(1)}, u32[]{:S(2)}, u32[]{:S(2)}) collective-permute-start(f32[144,8,128]{2,1,0:T(8,128)S(1)} %get-tuple-element.23.refs_0_), channel_id=1, source_target_pairs={{4,0},{8,4},{12,8},{16,12},{20,16},{24,20},{28,24},{32,28},{36,32}... | collective-permute-start | bytes 1769480 | tf_op jit(solution)/shard_map/ppermute | solution.py:313
  65.7 5.9 %shard_map.83.part_ref = f32[144,2,8,128]{3,2,1,0:T(8,128)S(1)} custom-call(f32[144,8,128]{2,1,0:T(8,128)S(1)} %get-tuple-element.23.refs_0_, f32[144,8,128]{2,1,0:T(8,128)S(1)} %get-tuple-element.22.refs_1_, f32[324,8,128]{2,1,0:T(8,128)S(1)} %get-tuple-element.16.refs_2_, f32[2,8,128]{2,1,0:T(8,128)S(1)} %get-tuple-element.29.refs_3_.scale_ref, ...), custom_call_target="tpu_custom_call" | custom-call | flops 31850496 | bytes 16777216 | tf_op jit(solution)/shard_map/pallas_call | solution.py:138
  71.6 4.1 %collective-permute-done.7.lower_ref = f32[144,8,128]{2,1,0:T(8,128)S(1)} collective-permute-done((f32[144,8,128]{2,1,0:T(8,128)S(1)}, f32[144,8,128]{2,1,0:T(8,128)S(1)}, u32[]{:S(2)}, u32[]{:S(2)}) %collective-permute-start.7) | collective-permute-done | bytes 589856 | tf_op jit(solution)/shard_map/ppermute | solution.py:312
  75.7 3.7 %shard_map.84 = (f32[144,8,128]{2,1,0:T(8,128)S(1)}, f32[144,8,128]{2,1,0:T(8,128)S(1)}, f32[144,2,8,128]{3,2,1,0:T(8,128)}) custom-call(f32[144,8,128]{2,1,0:T(8,128)S(1)} %collective-permute-done.7.lower_ref, f32[144,8,128]{2,1,0:T(8,128)S(1)} %collective-permute-done.8.upper_ref, f32[144,2,8,128]{3,2,1,0:T(8,128)S(1)} %shard_map.83.part_ref, ...), custom_call_target="tpu_custom_call" | custom-call | flops 15925248 | bytes 9437184 | tf_op jit(solution)/shard_map/pallas_call | solution.py:193
  80.9 3.9 %collective-permute-start.10 = (f32[144,8,128]{2,1,0:T(8,128)S(1)}, f32[144,8,128]{2,1,0:T(8,128)S(1)}, u32[]{:S(2)}, u32[]{:S(2)}) collective-permute-start(f32[144,8,128]{2,1,0:T(8,128)S(1)} %get-tuple-element.26.refs_0_), channel_id=1, source_target_pairs={{4,0},{8,4},{12,8},{16,12},{20,16},{24,20},{28,24},{32,28},{36,32}... | collective-permute-start | bytes 1769480 | tf_op jit(solution)/shard_map/ppermute | solution.py:320
  84.8 5.7 %shard_map.85.refs_2_ = f32[144,2,8,128]{3,2,1,0:T(8,128)S(1)} custom-call(f32[144,8,128]{2,1,0:T(8,128)S(1)} %get-tuple-element.26.refs_0_, f32[144,8,128]{2,1,0:T(8,128)S(1)} %get-tuple-element.25.refs_1_, f32[324,8,128]{2,1,0:T(8,128)S(1)} %get-tuple-element.16.refs_2_, f32[2,8,128]{2,1,0:T(8,128)S(1)} %subtract_convert_fusion.refs_3_.refs_4_), custom_call_target="tpu_custom_call" | custom-call | flops 31850496 | bytes 16777216 | tf_op jit(solution)/shard_map/pallas_call | solution.py:138
  90.5 2.4 %collective-permute-done.10.refs_1_ = f32[144,8,128]{2,1,0:T(8,128)S(1)} collective-permute-done((f32[144,8,128]{2,1,0:T(8,128)S(1)}, f32[144,8,128]{2,1,0:T(8,128)S(1)}, u32[]{:S(2)}, u32[]{:S(2)}) %collective-permute-start.10) | collective-permute-done | bytes 589856 | tf_op jit(solution)/shard_map/ppermute | solution.py:320
  92.9 5.1 %collective-permute-done.9.refs_0_ = f32[144,8,128]{2,1,0:T(8,128)S(1)} collective-permute-done((f32[144,8,128]{2,1,0:T(8,128)S(1)}, f32[144,8,128]{2,1,0:T(8,128)S(1)}, u32[]{:S(2)}, u32[]{:S(2)}) %collective-permute-start.9) | collective-permute-done | bytes 589856 | tf_op jit(solution)/shard_map/ppermute | solution.py:319
  98.0 5.4 %collective-permute-done.11.refs_5_ = f32[144,2,8,128]{3,2,1,0:T(8,128)S(1)} collective-permute-done((f32[144,2,8,128]{3,2,1,0:T(8,128)}, f32[144,2,8,128]{3,2,1,0:T(8,128)S(1)}, u32[]{:S(2)}, u32[]{:S(2)}) %collective-permute-start.11) | collective-permute-done | bytes 1179680 | tf_op jit(solution)/shard_map/ppermute | solution.py:321
  103.4 2.7 %shard_map.86 = (f32[144,2,8,128]{3,2,1,0:T(8,128)S(1)}, f32[144,2,8,128]{3,2,1,0:T(8,128)S(1)}) custom-call(f32[144,8,128]{2,1,0:T(8,128)S(1)} %collective-permute-done.9.refs_0_, f32[144,8,128]{2,1,0:T(8,128)S(1)} %collective-permute-done.10.refs_1_, f32[144,2,8,128]{3,2,1,0:T(8,128)S(1)} %shard_map.85.refs_2_, ...), custom_call_target="tpu_custom_call", output_to_operand_aliasing={{1}: (5, {})} | custom-call | flops 15925248 | bytes 9437184 | tf_op jit(solution)/shard_map/pallas_call | solution.py:193
  107.3 2.9 %collective-permute-done.13 = f32[144,2,8,128]{3,2,1,0:T(8,128)} collective-permute-done((f32[144,2,8,128]{3,2,1,0:T(8,128)S(1)}, f32[144,2,8,128]{3,2,1,0:T(8,128)}, u32[]{:S(2)}, u32[]{:S(2)}) %collective-permute-start.13) | collective-permute-done | bytes 1179680 | tf_op jit(solution)/shard_map/ppermute | solution.py:325
  111.5 6.6 %shard_map.87 = f32[96,192]{1,0:T(8,128)S(1)} custom-call(s32[4]{0:T(128)S(1)} %pad_add_fusion.place_ref, f32[2304,128]{1,0:T(8,128)S(1)} %bitcast.23, f32[16,128]{1,0:T(8,128)S(1)} %bitcast.24, f32[2304,128]{1,0:T(8,128)S(1)} %bitcast.21, f32[2304,128]{1,0:T(8,128)S(1)} %bitcast.22, f32[2304,128]{1,0:T(8,128)S(1)} %bitcast.19, f32[2304,128]{1,0:T(8,128)} %bitcast.14.refs_3_), custom_call_target="tpu_custom_call" | custom-call | tf_op jit(solution)/shard_map/pallas_call | solution.py:249
  119.2 4.5 %collective-permute-start.15 = (f32[96,192]{1,0:T(8,128)S(1)}, f32[96,192]{1,0:T(8,128)S(1)}, u32[]{:S(2)}, u32[]{:S(2)}) collective-permute-start(f32[96,192]{1,0:T(8,128)S(1)} %shard_map.87), channel_id=1, source_target_pairs={{0,8},{4,12},{8,0},{12,4},{16,24},{20,28},{24,16},{28,20},{32,40},... | collective-permute-start | bytes 221192 | tf_op jit(solution)/shard_map/ppermute | solution.py:275
  125.3 3.3 %collective-permute-done.15 = f32[96,192]{1,0:T(8,128)S(1)} collective-permute-done((f32[96,192]{1,0:T(8,128)S(1)}, f32[96,192]{1,0:T(8,128)S(1)}, u32[]{:S(2)}, u32[]{:S(2)}) %collective-permute-start.15) | collective-permute-done | bytes 73760 | tf_op jit(solution)/shard_map/ppermute | solution.py:275
  128.6 2.5 %collective-permute-start.17 = (f32[96,192]{1,0:T(8,128)S(1)}, f32[96,192]{1,0:T(8,128)S(1)}, u32[]{:S(2)}, u32[]{:S(2)}) collective-permute-start(f32[96,192]{1,0:T(8,128)S(1)} %add_add_fusion.1), channel_id=1, source_target_pairs={{0,16},{4,20},{8,24},{12,28},{16,32},{20,36},{24,40},{28,44},{32,4... | collective-permute-start | bytes 221192 | tf_op jit(solution)/shard_map/ppermute | solution.py:275
  131.1 23.1 %collective-permute-start.18 = (f32[96,192]{1,0:T(8,128)S(1)}, f32[96,192]{1,0:T(8,128)S(1)}, u32[]{:S(2)}, u32[]{:S(2)}) collective-permute-start(f32[96,192]{1,0:T(8,128)S(1)} %add_add_fusion.1), channel_id=1, source_target_pairs={{0,32},{4,36},{8,40},{12,44},{16,48},{20,52},{24,56},{28,60},{32,0... | collective-permute-start | bytes 221192 | tf_op jit(solution)/shard_map/ppermute | solution.py:275
  155.1 4.2 %collective-permute-done.18 = f32[96,192]{1,0:T(8,128)S(1)} collective-permute-done((f32[96,192]{1,0:T(8,128)S(1)}, f32[96,192]{1,0:T(8,128)S(1)}, u32[]{:S(2)}, u32[]{:S(2)}) %collective-permute-start.18) | collective-permute-done | bytes 73760 | tf_op jit(solution)/shard_map/ppermute | solution.py:275
  161.7 8.4 %collective-permute-start.20 = (f32[96,192]{1,0:T(8,128)S(1)}, f32[96,192]{1,0:T(8,128)S(1)}, u32[]{:S(2)}, u32[]{:S(2)}) collective-permute-start(f32[96,192]{1,0:T(8,128)S(1)} %add_add_fusion), channel_id=1, source_target_pairs={{0,64},{4,68},{8,72},{12,76},{16,80},{20,84},{24,88},{28,92},{32,9... | collective-permute-start | bytes 221192 | tf_op jit(solution)/shard_map/ppermute | solution.py:275
  170.1 3.8 %collective-permute-done.20 = f32[96,192]{1,0:T(8,128)S(1)} collective-permute-done((f32[96,192]{1,0:T(8,128)S(1)}, f32[96,192]{1,0:T(8,128)S(1)}, u32[]{:S(2)}, u32[]{:S(2)}) %collective-permute-start.20) | collective-permute-done | bytes 73760 | tf_op jit(solution)/shard_map/ppermute | solution.py:275
  175.3 4.9 %collective-permute-done.21 = f32[96,192]{1,0:T(8,128)S(1)} collective-permute-done((f32[96,192]{1,0:T(8,128)S(1)}, f32[96,192]{1,0:T(8,128)S(1)}, u32[]{:S(2)}, u32[]{:S(2)}) %collective-permute-start.21) | collective-permute-done | bytes 73760 | tf_op jit(solution)/shard_map/ppermute | solution.py:275
  (55 shorter events, 22.9 us)
Async XLA Ops:
  1.3 8.1 %collective-permute-start.2 = (f32[1,8,128]{2,1,0:T(8,128)S(1)}, f32[1,8,128]{2,1,0:T(8,128)S(1)}, u32[]{:S(2)}, u32[]{:S(2)}) collective-permute-start(f32[1,8,128]{2,1,0:T(8,128)S(1)} %slice.25), channel_id=1, source_target_pairs={{0,4},{4,8},{8,12},{12,16},{16,20},{20,24},{24,28},{28,32},{32,36}... | collective-permute-start | bytes 12296 | tf_op jit(solution)/shard_map/ppermute | solution.py:286
  4.9 4.5 %copy-start.3 = (f32[2,8,128]{2,1,0:T(8,128)S(1)}, f32[2,8,128]{2,1,0:T(8,128)}, u32[]{:S(2)}) copy-start(f32[2,8,128]{2,1,0:T(8,128)} %param.7) | copy-start | bytes 24580
  4.9 4.5 %copy-start.5 = (s32[2,8,128]{2,1,0:T(8,128)S(1)}, s32[2,8,128]{2,1,0:T(8,128)}, u32[]{:S(2)}) copy-start(s32[2,8,128]{2,1,0:T(8,128)} %param.8) | copy-start | bytes 24580
  4.9 4.5 %copy-start.6 = (f32[2,8,128]{2,1,0:T(8,128)S(1)}, f32[2,8,128]{2,1,0:T(8,128)}, u32[]{:S(2)}) copy-start(f32[2,8,128]{2,1,0:T(8,128)} %param.6) | copy-start | bytes 24580
  5.0 4.6 %copy-start.4 = (f32[24,24]{1,0:T(8,128)S(1)}, f32[24,24]{1,0:T(8,128)}, u32[]{:S(2)}) copy-start(f32[24,24]{1,0:T(8,128)} %stiff_ref.1) | copy-start | bytes 6916
  5.0 17.0 %collective-permute-start = (f32[144,8,128]{2,1,0:T(8,128)S(1)}, f32[144,8,128]{2,1,0:T(8,128)S(1)}, u32[]{:S(2)}, u32[]{:S(2)}) collective-permute-start(f32[144,8,128]{2,1,0:T(8,128)S(1)} %bitcast_multiply_fusion.1.refs_1_.refs_5_), channel_id=1, source_target_pairs={{0,4},{4,8},{8,12},{12,16},{16,20},{20,24},{24,28},{28,32},{32,36}... | collective-permute-start | bytes 1769480 | tf_op jit(solution)/shard_map/ppermute | solution.py:312
  6.7 15.3 %collective-permute-start.1 = (f32[144,8,128]{2,1,0:T(8,128)S(1)}, f32[144,8,128]{2,1,0:T(8,128)S(1)}, u32[]{:S(2)}, u32[]{:S(2)}) collective-permute-start(f32[144,8,128]{2,1,0:T(8,128)S(1)} %bitcast_multiply_fusion.refs_0_.refs_4_), channel_id=1, source_target_pairs={{4,0},{8,4},{12,8},{16,12},{20,16},{24,20},{28,24},{32,28},{36,32}... | collective-permute-start | bytes 1769480 | tf_op jit(solution)/shard_map/ppermute | solution.py:313
  24.8 16.1 %collective-permute-start.3 = (f32[144,8,128]{2,1,0:T(8,128)S(1)}, f32[144,8,128]{2,1,0:T(8,128)S(1)}, u32[]{:S(2)}, u32[]{:S(2)}) collective-permute-start(f32[144,8,128]{2,1,0:T(8,128)S(1)} %get-tuple-element.18.refs_1_.refs_5_), channel_id=1, source_target_pairs={{0,4},{4,8},{8,12},{12,16},{16,20},{20,24},{24,28},{28,32},{32,36}... | collective-permute-start | bytes 1769480 | tf_op jit(solution)/shard_map/ppermute | solution.py:312
  25.4 15.4 %collective-permute-start.4 = (f32[144,8,128]{2,1,0:T(8,128)S(1)}, f32[144,8,128]{2,1,0:T(8,128)S(1)}, u32[]{:S(2)}, u32[]{:S(2)}) collective-permute-start(f32[144,8,128]{2,1,0:T(8,128)S(1)} %get-tuple-element.19.refs_0_.refs_4_), channel_id=1, source_target_pairs={{4,0},{8,4},{12,8},{16,12},{20,16},{24,20},{28,24},{32,28},{36,32}... | collective-permute-start | bytes 1769480 | tf_op jit(solution)/shard_map/ppermute | solution.py:313
  43.6 15.1 %collective-permute-start.5 = (f32[144,8,128]{2,1,0:T(8,128)S(1)}, f32[144,8,128]{2,1,0:T(8,128)S(1)}, u32[]{:S(2)}, u32[]{:S(2)}) collective-permute-start(f32[144,8,128]{2,1,0:T(8,128)S(1)} %get-tuple-element.20.refs_1_.refs_5_), channel_id=1, source_target_pairs={{0,4},{4,8},{8,12},{12,16},{16,20},{20,24},{24,28},{28,32},{32,36}... | collective-permute-start | bytes 1769480 | tf_op jit(solution)/shard_map/ppermute | solution.py:312
  45.1 13.7 %collective-permute-start.6 = (f32[144,8,128]{2,1,0:T(8,128)S(1)}, f32[144,8,128]{2,1,0:T(8,128)S(1)}, u32[]{:S(2)}, u32[]{:S(2)}) collective-permute-start(f32[144,8,128]{2,1,0:T(8,128)S(1)} %get-tuple-element.21.refs_0_.refs_4_), channel_id=1, source_target_pairs={{4,0},{8,4},{12,8},{16,12},{20,16},{24,20},{28,24},{32,28},{36,32}... | collective-permute-start | bytes 1769480 | tf_op jit(solution)/shard_map/ppermute | solution.py:313
  61.5 14.2 %collective-permute-start.7 = (f32[144,8,128]{2,1,0:T(8,128)S(1)}, f32[144,8,128]{2,1,0:T(8,128)S(1)}, u32[]{:S(2)}, u32[]{:S(2)}) collective-permute-start(f32[144,8,128]{2,1,0:T(8,128)S(1)} %get-tuple-element.22.refs_1_), channel_id=1, source_target_pairs={{0,4},{4,8},{8,12},{12,16},{16,20},{20,24},{24,28},{28,32},{32,36}... | collective-permute-start | bytes 1769480 | tf_op jit(solution)/shard_map/ppermute | solution.py:312
  62.9 12.8 %collective-permute-start.8 = (f32[144,8,128]{2,1,0:T(8,128)S(1)}, f32[144,8,128]{2,1,0:T(8,128)S(1)}, u32[]{:S(2)}, u32[]{:S(2)}) collective-permute-start(f32[144,8,128]{2,1,0:T(8,128)S(1)} %get-tuple-element.23.refs_0_), channel_id=1, source_target_pairs={{4,0},{8,4},{12,8},{16,12},{20,16},{24,20},{28,24},{32,28},{36,32}... | collective-permute-start | bytes 1769480 | tf_op jit(solution)/shard_map/ppermute | solution.py:313
  79.4 24.0 %collective-permute-start.11 = (f32[144,2,8,128]{3,2,1,0:T(8,128)}, f32[144,2,8,128]{3,2,1,0:T(8,128)S(1)}, u32[]{:S(2)}, u32[]{:S(2)}) collective-permute-start(f32[144,2,8,128]{3,2,1,0:T(8,128)} %get-tuple-element.24), channel_id=1, source_target_pairs={{0,2},{2,0},{1,3},{3,1},{4,6},{6,4},{5,7},{7,5},{8,10},{10,8},{9,1... | collective-permute-start | bytes 3538952 | tf_op jit(solution)/shard_map/ppermute | solution.py:321
  80.9 11.9 %collective-permute-start.10 = (f32[144,8,128]{2,1,0:T(8,128)S(1)}, f32[144,8,128]{2,1,0:T(8,128)S(1)}, u32[]{:S(2)}, u32[]{:S(2)}) collective-permute-start(f32[144,8,128]{2,1,0:T(8,128)S(1)} %get-tuple-element.26.refs_0_), channel_id=1, source_target_pairs={{4,0},{8,4},{12,8},{16,12},{20,16},{24,20},{28,24},{32,28},{36,32}... | collective-permute-start | bytes 1769480 | tf_op jit(solution)/shard_map/ppermute | solution.py:320
  84.8 13.2 %collective-permute-start.9 = (f32[144,8,128]{2,1,0:T(8,128)S(1)}, f32[144,8,128]{2,1,0:T(8,128)S(1)}, u32[]{:S(2)}, u32[]{:S(2)}) collective-permute-start(f32[144,8,128]{2,1,0:T(8,128)S(1)} %get-tuple-element.25.refs_1_), channel_id=1, source_target_pairs={{0,4},{4,8},{8,12},{12,16},{16,20},{20,24},{24,28},{28,32},{32,36}... | collective-permute-start | bytes 1769480 | tf_op jit(solution)/shard_map/ppermute | solution.py:319
  84.8 22.5 %collective-permute-start.12 = (f32[144,2,8,128]{3,2,1,0:T(8,128)}, f32[144,2,8,128]{3,2,1,0:T(8,128)S(1)}, u32[]{:S(2)}, u32[]{:S(2)}) collective-permute-start(f32[144,2,8,128]{3,2,1,0:T(8,128)} %get-tuple-element.24), channel_id=1, source_target_pairs={{0,1},{1,0},{2,3},{3,2},{4,5},{5,4},{6,7},{7,6},{8,9},{9,8},{10,11... | collective-permute-start | bytes 3538952 | tf_op jit(solution)/shard_map/ppermute | solution.py:322
  90.5 19.7 %copy-start = (f32[144,2,8,128]{3,2,1,0:T(8,128)S(1)}, f32[144,2,8,128]{3,2,1,0:T(8,128)}, u32[]{:S(2)}) copy-start(f32[144,2,8,128]{3,2,1,0:T(8,128)} %get-tuple-element.24) | copy-start | bytes 3538948
  106.1 1.1 copy-start.1
  107.2 3.0 %collective-permute-start.13 = (f32[144,2,8,128]{3,2,1,0:T(8,128)S(1)}, f32[144,2,8,128]{3,2,1,0:T(8,128)}, u32[]{:S(2)}, u32[]{:S(2)}) collective-permute-start(f32[144,2,8,128]{3,2,1,0:T(8,128)S(1)} %get-tuple-element.28), channel_id=1, source_target_pairs={{0,1},{1,0},{2,3},{3,2},{4,5},{5,4},{6,7},{7,6},{8,9},{9,8},{10,11... | collective-permute-start | bytes 3538952 | tf_op jit(solution)/shard_map/ppermute | solution.py:325
  110.2 1.3 copy-start.2
  118.1 7.2 %collective-permute-start.14 = (f32[96,192]{1,0:T(8,128)S(1)}, f32[96,192]{1,0:T(8,128)S(1)}, u32[]{:S(2)}, u32[]{:S(2)}) collective-permute-start(f32[96,192]{1,0:T(8,128)S(1)} %shard_map.87), channel_id=1, source_target_pairs={{0,4},{4,8},{8,12},{12,0},{16,20},{20,24},{24,28},{28,16},{32,36},... | collective-permute-start | bytes 221192 | tf_op jit(solution)/shard_map/ppermute | solution.py:275
  119.2 9.4 %collective-permute-start.15 = (f32[96,192]{1,0:T(8,128)S(1)}, f32[96,192]{1,0:T(8,128)S(1)}, u32[]{:S(2)}, u32[]{:S(2)}) collective-permute-start(f32[96,192]{1,0:T(8,128)S(1)} %shard_map.87), channel_id=1, source_target_pairs={{0,8},{4,12},{8,0},{12,4},{16,24},{20,28},{24,16},{28,20},{32,40},... | collective-permute-start | bytes 221192 | tf_op jit(solution)/shard_map/ppermute | solution.py:275
  123.7 4.9 %collective-permute-start.16 = (f32[96,192]{1,0:T(8,128)S(1)}, f32[96,192]{1,0:T(8,128)S(1)}, u32[]{:S(2)}, u32[]{:S(2)}) collective-permute-start(f32[96,192]{1,0:T(8,128)S(1)} %shard_map.87), channel_id=1, source_target_pairs={{0,12},{4,0},{8,4},{12,8},{16,28},{20,16},{24,20},{28,24},{32,44},... | collective-permute-start | bytes 221192 | tf_op jit(solution)/shard_map/ppermute | solution.py:275
  128.6 26.5 %collective-permute-start.17 = (f32[96,192]{1,0:T(8,128)S(1)}, f32[96,192]{1,0:T(8,128)S(1)}, u32[]{:S(2)}, u32[]{:S(2)}) collective-permute-start(f32[96,192]{1,0:T(8,128)S(1)} %add_add_fusion.1), channel_id=1, source_target_pairs={{0,16},{4,20},{8,24},{12,28},{16,32},{20,36},{24,40},{28,44},{32,4... | collective-permute-start | bytes 221192 | tf_op jit(solution)/shard_map/ppermute | solution.py:275
  131.1 28.3 %collective-permute-start.18 = (f32[96,192]{1,0:T(8,128)S(1)}, f32[96,192]{1,0:T(8,128)S(1)}, u32[]{:S(2)}, u32[]{:S(2)}) collective-permute-start(f32[96,192]{1,0:T(8,128)S(1)} %add_add_fusion.1), channel_id=1, source_target_pairs={{0,32},{4,36},{8,40},{12,44},{16,48},{20,52},{24,56},{28,60},{32,0... | collective-permute-start | bytes 221192 | tf_op jit(solution)/shard_map/ppermute | solution.py:275
  154.2 7.5 %collective-permute-start.19 = (f32[96,192]{1,0:T(8,128)S(1)}, f32[96,192]{1,0:T(8,128)S(1)}, u32[]{:S(2)}, u32[]{:S(2)}) collective-permute-start(f32[96,192]{1,0:T(8,128)S(1)} %add_add_fusion.1), channel_id=1, source_target_pairs={{0,48},{4,52},{8,56},{12,60},{16,0},{20,4},{24,8},{28,12},{32,16},... | collective-permute-start | bytes 221192 | tf_op jit(solution)/shard_map/ppermute | solution.py:275
  161.7 12.2 %collective-permute-start.20 = (f32[96,192]{1,0:T(8,128)S(1)}, f32[96,192]{1,0:T(8,128)S(1)}, u32[]{:S(2)}, u32[]{:S(2)}) collective-permute-start(f32[96,192]{1,0:T(8,128)S(1)} %add_add_fusion), channel_id=1, source_target_pairs={{0,64},{4,68},{8,72},{12,76},{16,80},{20,84},{24,88},{28,92},{32,9... | collective-permute-start | bytes 221192 | tf_op jit(solution)/shard_map/ppermute | solution.py:275
  173.9 6.2 %collective-permute-start.21 = (f32[96,192]{1,0:T(8,128)S(1)}, f32[96,192]{1,0:T(8,128)S(1)}, u32[]{:S(2)}, u32[]{:S(2)}) collective-permute-start(f32[96,192]{1,0:T(8,128)S(1)} %add.52), channel_id=1, source_target_pairs={{0,128},{4,132},{8,136},{12,140},{16,144},{20,148},{24,152},{28,15... | collective-permute-start | bytes 221192 | tf_op jit(solution)/shard_map/ppermute | solution.py:275

commit v3 on v2

v3 whole, which is shorter than its diff:
```python
from functools import partial

import jax
import jax.numpy as jnp
from jax import lax
from jax.experimental import pallas as pl
from jax.experimental.pallas import tpu as pltpu
from jax.sharding import Mesh, PartitionSpec as P

CENTER = 110.0
HALF = 90.0
SLAB = ("xh", "z", "y")
MODE = ("xl", "core")
STEPS = (0, 1, -1)
VMEM_LIMIT = 16 * 1024 * 1024


def spec(shape, dtype=jnp.float32):
    return jax.ShapeDtypeStruct(shape, dtype)


def own_index(dz, q, e, dy, c, p):
    return ((((STEPS.index(dz) * 2 + q) * 3 + e) * 3 + STEPS.index(dy)) * 3 + c) * 2 + p


def halo_index(dz, side, e, dy, c):
    return (((STEPS.index(dz) * 2 + side) * 3 + e) * 3 + STEPS.index(dy)) * 3 + c


def rolled(x, by, axis):
    by = by % x.shape[axis]
    return x if by == 0 else pltpu.roll(x, by, axis)


def coefficient_kernel(stiff_ref, layers_ref, own_ref, halo_ref):
    turned = {}
    for layer in range(3):
        for b in range(2):
            for d in range(2):
                turned[layer, b, d] = rolled(rolled(layers_ref[layer], b, 0), d, 1)
    for p in range(2):
        for q in range(-1, 3):
            dx = q - p
            if abs(dx) > 1:
                continue
            for dy in STEPS:
                for dz in STEPS:
                    corners = [
                        (a, b, d)
                        for a in range(2)
                        for b in range(2)
                        for d in range(2)
                        if 0 <= a + dx <= 1 and 0 <= b + dy <= 1 and 0 <= d + dz <= 1
                    ]
                    for c in range(3):
                        for e in range(3):
                            total = None
                            for a, b, d in corners:
                                row = 3 * (4 * a + 2 * b + d) + c
                                col = 3 * (4 * (a + dx) + 2 * (b + dy) + d + dz) + e
                                term = stiff_ref[row, col] * turned[p - a + 1, b + dy, d]
                                total = term if total is None else total + term
                            if 0 <= q <= 1:
                                own_ref[own_index(dz, q, e, dy, c, p)] = total
                            else:
                                halo_ref[halo_index(dz, 0 if q < 0 else 1, e, dy, c)] = total


def coefficients(stiffness, layers):
    rows, depth = layers.shape[1:]
    return pl.pallas_call(
        coefficient_kernel,
        in_specs=[pl.BlockSpec(memory_space=pltpu.SMEM), pl.BlockSpec(memory_space=pltpu.VMEM)],
        out_specs=[pl.BlockSpec(memory_space=pltpu.VMEM)] * 2,
        out_shape=[spec((324, rows, depth)), spec((162, rows, depth))],
        compiler_params=pltpu.CompilerParams(vmem_limit_bytes=VMEM_LIMIT),
    )(stiffness, layers)


OWN_MODES = 2
HALO_MODES = 4
IN_VMEM = pl.BlockSpec(memory_space=pltpu.VMEM)
ANYWHERE = pl.BlockSpec(memory_space=pl.ANY)


def cost(flops, nbytes):
    return pl.CostEstimate(flops=flops, bytes_accessed=nbytes, transcendentals=0)


def compiled():
    return pltpu.CompilerParams(vmem_limit_bytes=VMEM_LIMIT)


def gathered(acc):
    return acc[0] + rolled(acc[1], -1, 0) + rolled(acc[2], 1, 0)


def added(acc, key, term):
    acc[key] = acc[key] + term if key in acc else term


def own_kernel(shift, count, *refs):
    low_ref, high_ref, coef_ref, scale_ref = refs[:4]
    before, parts = refs[4:-2], refs[-2:]
    planes = (low_ref, high_ref)

    def some(i, _):
        base = i * (3 * OWN_MODES)
        acc = {}
        for dz in STEPS:
            for q in range(2):
                for e in range(3):
                    fields = [rolled(planes[q][base + 3 * u + e], -dz, 1) for u in range(OWN_MODES)]
                    for s, dy in enumerate(STEPS):
                        for c in range(3):
                            for p in range(2):
                                coef = coef_ref[own_index(dz, q, e, dy, c, p)]
                                for u in range(OWN_MODES):
                                    added(acc, (u, c, p, s), coef * fields[u])
        for u in range(OWN_MODES):
            for c in range(3):
                at = base + 3 * u + c
                for p in range(2):
                    value = scale_ref[p] * gathered([acc[u, c, p, s] for s in range(3)])
                    if shift:
                        value = value - shift * planes[p][at]
                    if before:
                        value = value - before[p][at]
                    parts[p][at] = value
        return 0

    lax.fori_loop(0, count // (3 * OWN_MODES), some, 0)


def own_part(shift, current, coef, scale, before):
    count, rows, depth = current[0].shape
    args = (*current, coef, scale, *before)
    return pl.pallas_call(
        partial(own_kernel, shift, count),
        in_specs=[IN_VMEM] * len(args),
        out_specs=[IN_VMEM] * 2,
        out_shape=[spec(current[0].shape)] * 2,
        cost_estimate=cost(2 * 108 * count * rows * depth, 16 << 20),
        compiler_params=compiled(),
    )(*args)


def halo_kernel(p, halo_ref, part_ref, coef_ref, scale_ref, out_ref):
    step = 3 * HALO_MODES

    def some(i, _):
        base = i * step
        acc = {}
        for dz in STEPS:
            for e in range(3):
                fields = [rolled(halo_ref[base + 3 * u + e], -dz, 1) for u in range(HALO_MODES)]
                for s, dy in enumerate(STEPS):
                    for c in range(3):
                        coef = coef_ref[halo_index(dz, p, e, dy, c)]
                        for u in range(HALO_MODES):
                            added(acc, (u, c, s), coef * fields[u])
        scale = scale_ref[p]
        for u in range(HALO_MODES):
            for c in range(3):
                at = base + 3 * u + c
                out_ref[at] = part_ref[at] + scale * gathered([acc[u, c, s] for s in range(3)])
        return 0

    lax.fori_loop(0, halo_ref.shape[0] // step, some, 0)


def with_halo(p, halo, part, coef, scale):
    return pl.pallas_call(
        partial(halo_kernel, p),
        in_specs=[IN_VMEM] * 4,
        out_specs=IN_VMEM,
        out_shape=spec(halo.shape),
        cost_estimate=cost(54 * halo.size, 5 << 20),
        compiler_params=compiled(),
    )(halo, part, coef, scale)


def join_kernel(low_ref, high_ref, out_ref):
    def some(i, _):
        out_ref[i, 0] = low_ref[i]
        out_ref[i, 1] = high_ref[i]
        return 0

    lax.fori_loop(0, low_ref.shape[0], some, 0, unroll=8)


def joined(low, high):
    return pl.pallas_call(
        join_kernel,
        in_specs=[IN_VMEM] * 2,
        out_specs=IN_VMEM,
        out_shape=spec((low.shape[0], 2) + low.shape[1:]),
        cost_estimate=cost(1 << 20, 4 << 20),
        compiler_params=compiled(),
    )(low, high)


def split(x):
    top = x.astype(jnp.bfloat16)
    return top, (x - top.astype(jnp.float32)).astype(jnp.bfloat16)


def dot_t(a, b):
    return lax.dot_general(a, b, (((1,), (1,)), ((), ())), preferred_element_type=jnp.float32)


def product(top, rest, left_top, left_rest):
    return dot_t(top, left_top) + dot_t(rest, left_top) + dot_t(top, left_rest)


def each_row(field_ref, modes, do):
    stride, depth = field_ref.shape[0] // modes, field_ref.shape[1]

    def some(row, _):
        do(row, pl.ds(pl.multiple_of(row * depth, depth), depth))
        return 0

    lax.fori_loop(0, stride, some, 0, unroll=4)


def modes_at(ref, row, modes):
    return ref[pl.ds(row, modes, stride=ref.shape[0] // modes), :]


def held(x, *after):
    return pl.pallas_call(
        lambda *refs: None,
        in_specs=[ANYWHERE] * (1 + len(after)),
        out_specs=ANYWHERE,
        out_shape=spec(x.shape),
        input_output_aliases={0: 0},
        cost_estimate=cost(0, 1 << 10),
        compiler_params=compiled(),
    )(x, *after)


def near_kernel(stiff_ref, own_ref, field_ref, mass_ref, left_top, left_rest, out_ref, top, rest):
    modes = top.shape[0] // 2
    first, second = pl.ds(0, modes), pl.ds(modes, modes)

    def do(row, at):
        own = modes_at(own_ref, row, modes)
        weight = mass_ref[pl.ds(lax.rem(row, mass_ref.shape[0]), 1), :]
        left_top[first, at], left_rest[first, at] = split(modes_at(stiff_ref, row, modes))
        left_top[second, at], left_rest[second, at] = split(own * weight)
        top[first, at], rest[first, at] = split(own)
        top[second, at], rest[second, at] = split(modes_at(field_ref, row, modes))

    each_row(own_ref, modes, do)
    out_ref[...] = product(top[...], rest[...], left_top[...], left_rest[...])


def near_gram(stiff, own, by_x, mass, modes):
    wide = own.size // modes
    shape = (2 * modes, wide)
    depth = mass.shape[-1]
    return pl.pallas_call(
        near_kernel,
        in_specs=[IN_VMEM] * 4,
        out_specs=[IN_VMEM] * 3,
        out_shape=[spec(shape, jnp.bfloat16)] * 2 + [spec((2 * modes, 2 * modes))],
        scratch_shapes=[pltpu.VMEM(shape, jnp.bfloat16)] * 2,
        cost_estimate=cost(1 << 20, 8 << 20),
        compiler_params=compiled(),
    )(*(a.reshape(-1, depth) for a in (stiff, own, by_x)), mass)


def far_product(core_ref, both_ref, left_top, left_rest, top, rest):
    modes = top.shape[0] // 2
    first, second = pl.ds(0, modes), pl.ds(modes, modes)

    def do(row, at):
        top[first, at], rest[first, at] = split(modes_at(core_ref, row, modes))
        top[second, at], rest[second, at] = split(modes_at(both_ref, row, modes))

    each_row(core_ref, modes, do)
    return product(top[...], rest[...], left_top[...], left_rest[...])


def far_kernel(core_ref, both_ref, left_top, left_rest, out_ref, top, rest):
    out_ref[...] = far_product(core_ref, both_ref, left_top, left_rest, top, rest)


def last_kernel(factor, core_ref, both_ref, left_top, left_rest, place_ref, *refs):
    nears, fars, out_ref, top, rest, turned = refs[:2], refs[2:-4], *refs[-4:]
    far = far_product(core_ref, both_ref, left_top, left_rest, top, rest)
    modes = top.shape[0] // 2
    far = far + fars[0][...]
    near = nears[0][...] + nears[1][...]
    blocks = (near[:modes], far[:modes], near[modes:], far[modes:])
    for r in range(4):
        at = pl.ds(pl.multiple_of(place_ref[r] * modes, modes), modes)
        turned[at, :] = blocks[r] * factor
    whole = turned[...].T
    out_ref[0 : 2 * modes, :] = whole[:, :128]
    tail = whole[:, 128:]
    out_ref[2 * modes :, :] = jnp.concatenate([tail[:modes], tail[modes:]], 1)


def far_gram(by_core, by_both, left, modes, last=None):
    wide = by_core.size // modes
    shape = (2 * modes, wide)
    depth = by_core.shape[-1]
    args = [a.reshape(-1, depth) for a in (by_core, by_both)] + list(left)
    specs = [IN_VMEM] * 4
    scratch = [pltpu.VMEM(shape, jnp.bfloat16)] * 2
    if last is None:
        kernel, out = far_kernel, (2 * modes, 2 * modes)
    else:
        factor, place, nears, fars = last
        kernel, out = partial(last_kernel, factor), (3 * modes, 128)
        args += [place, *nears, *fars]
        specs += [pl.BlockSpec(memory_space=pltpu.SMEM)] + [IN_VMEM] * 3
        scratch.append(pltpu.VMEM((4 * modes, 2 * modes), jnp.float32))
    return pl.pallas_call(
        kernel,
        in_specs=specs,
        out_specs=IN_VMEM,
        out_shape=spec(out),
        scratch_shapes=scratch,
        cost_estimate=cost(1 << 20, 8 << 20),
        compiler_params=compiled(),
    )(*args)


def total_over(x, axes, groups):
    above, count, below = groups
    parts = []
    for k in range(1, count):
        pairs = [
            ((i * count + j) * below + l, (i * count + (j + k) % count) * below + l)
            for i in range(above)
            for j in range(count)
            for l in range(below)
        ]
        parts.append(lax.ppermute(x, axes, pairs))
    for part in parts:
        x = x + part
    return x


def body(subspace, modulus, mass, support, stiffness):
    modes, comps, planes, rows, depth = subspace.shape
    slabs = lax.axis_size(SLAB)
    four = lax.axis_size(MODE)
    up = [
        (i * four + m, (i + 1) * four + m if i + 1 < slabs else m ^ 2)
        for i in range(slabs)
        for m in range(four)
    ]
    down = [(b, a) for a, b in up]
    everywhere = SLAB + MODE
    lower_layer = lax.ppermute(modulus[planes - 1 :], everywhere, up)
    free = (1 - support).astype(jnp.float32)

    def masked(p):
        return (free[p] * subspace[:, :, p]).reshape(modes * comps, rows, depth)

    current = (masked(0), masked(1))
    layers = jnp.concatenate([lower_layer, modulus], 0)
    plane_index = (
        lax.axis_index(SLAB) * planes - 1 + lax.broadcasted_iota(jnp.int32, layers.shape, 0)
    )
    row_index = lax.broadcasted_iota(jnp.int32, layers.shape, 1)
    depth_index = lax.broadcasted_iota(jnp.int32, layers.shape, 2)
    valid = (
        (plane_index >= 0)
        & (plane_index < planes * slabs - 1)
        & (row_index < rows - 1)
        & (depth_index < depth - 1)
    )
    layers = jnp.where(valid, layers, jnp.zeros_like(layers))
    own_coef, halo_coef = coefficients(stiffness, layers)
    scale = free / (mass * HALF)

    before = ()
    lower = lax.ppermute(current[1], everywhere, up)
    upper = lax.ppermute(current[0], everywhere, down)
    for k in range(4):
        times = 1.0 if k == 0 else 2.0
        part = own_part(times * CENTER / HALF, current, own_coef, times * scale, before)
        high = with_halo(1, upper, part[1], halo_coef, times * scale)
        below = lax.ppermute(high, everywhere, up)
        low = with_halo(0, lower, part[0], halo_coef, times * scale)
        upper = lax.ppermute(low, everywhere, down)
        lower = below
        before, current = current, (low, high)
    swap = [(0, 1), (1, 0)]
    by_x = [None, None]
    for p in (1, 0):
        by_x[p] = lax.ppermute(current[p], "xl", swap)
    filtered = joined(*current)
    part = own_part(0.0, current, own_coef, free, ())
    stiffened = [with_halo(p, h, part[p], halo_coef, free) for p, h in ((0, lower), (1, upper))]
    me = lax.axis_index(MODE)
    place = jnp.stack([me ^ r for r in range(4)]).astype(jnp.int32)
    factor = 1.0 / (float(comps) * planes * slabs * rows * depth)
    nears, fars = [], []
    after = (*stiffened, filtered)
    for p in (1, 0):
        by_x[p] = held(by_x[p], *after)
        by_core = lax.ppermute(current[p], "core", swap)
        by_both = lax.ppermute(by_x[p], "core", swap)
        *left, near = near_gram(stiffened[p], current[p], by_x[p], mass[p], modes)
        nears.append(near)
        after = (near,)
        last = (factor, place, nears, fars) if p == 0 else None
        fars.append(far_gram(by_core, by_both, left, modes, last))
    grams = fars[-1]
    for groups in ((16, 4, 1), (4, 4, 4), (2, 2, 16), (1, 2, 32)):
        grams = total_over(grams, SLAB, groups)
    tail = grams[2 * modes :]
    wide = 4 * modes - depth
    stiffness_gram = jnp.concatenate([grams[:modes], tail[:, :wide]], 1)
    mass_gram = jnp.concatenate([grams[modes : 2 * modes], tail[:, wide:]], 1)
    return filtered.reshape(subspace.shape), stiffness_gram, mass_gram


def solution(mesh):
    finer = Mesh(mesh.devices.reshape(2, 8, 4, 2, 2), SLAB + MODE)
    placed = (
        P(MODE, None, SLAB, None, None),
        P(SLAB, None, None),
        P(SLAB, None, None),
        P(SLAB, None, None),
        P(),
    )
    return jax.shard_map(
        body,
        mesh=finer,
        in_specs=placed,
        out_specs=(P(MODE, None, SLAB, None, None), P(MODE, None), P(MODE, None)),
        check_vma=False,
    )
```

time: 181 us -> 162 us (0.90)
  starting transfers between devices: 64.7 us -> 42.5 us
  Pallas kernels: 51.8 us -> 55.4 us
    ppermute x8, starting transfers between devices: 40.9 us -> 25.4 us  [total_over(): parts.append(lax.ppermute(x, axes, pairs))]
    ppermute x14 -> x17, starting transfers between devices: 23.9 us -> 17 us  [the longest x4 6.02 us: body(): upper = lax.ppermute(low, everywhere, down)]
    pallas_call x6 -> x17, Pallas kernels: 21.3 us -> 25.9 us  [the longest x10 17 us: with_halo(): pl.pallas_call(partial(halo_kernel, p), in_specs=[IN_VMEM] * 4, out_specs...]
    ppermute x14 -> x17, waiting for transfers between devices: 36.2 us -> 32.6 us  [the longest x4 12.1 us: body(): below = lax.ppermute(high, everywhere, up)]
    ppermute x8, waiting for transfers between devices: 21.1 us -> 24.6 us  [total_over(): parts.append(lax.ppermute(x, axes, pairs))]
  transfers between devices with their start and end apart: 22 -> 25, of which waited for: 15 -> 15; matrix products, arithmetic and copies ran while one was open for 1% -> 1% of each run, Pallas kernels for 18% -> 33%
where the time goes in v3:
time: 162 us
  waiting for transfers between devices  57.2 us (35%)
  Pallas kernels  55.4 us (34%)
  starting transfers between devices  42.5 us (26%)
  local copies, waits for them, and re-layouts  4.39 us (3%)
  other arithmetic  1.68 us (1%)
    pallas_call x5, Pallas kernels, own_part(): pl.pallas_call(partial(own_kernel, shift, count), in_specs=[IN_VMEM] * le...  28.3 us
    ppermute x8, starting transfers between devices, total_over(): parts.append(lax.ppermute(x, axes, pairs))  25.4 us
    ppermute x8, waiting for transfers between devices, total_over(): parts.append(lax.ppermute(x, axes, pairs))  24.6 us
    pallas_call x10, Pallas kernels, with_halo(): pl.pallas_call(partial(halo_kernel, p), in_specs=[IN_VMEM] * 4, out_specs...  17 us
    ppermute x4, waiting for transfers between devices, body(): below = lax.ppermute(high, everywhere, up)  12.1 us
    ppermute x2, waiting for transfers between devices, body(): by_x[p] = lax.ppermute(current[p], 'xl', swap)  7.56 us
    ppermute x4, waiting for transfers between devices, body(): upper = lax.ppermute(low, everywhere, down)  7.28 us
    ppermute x4, starting transfers between devices, body(): upper = lax.ppermute(low, everywhere, down)  6.02 us
  transfers between devices with their start and end apart: 25, of which 15 were waited for; matrix products, arithmetic and copies ran while one was open for 1% of the time, Pallas kernels for 33%

profile of v3, /device:TPU:32, one launch (start us, length us, event | category | flops | bytes accessed | tf_op | source)
XLA Modules:
  0.0 162.2 jit_solution(761906289770178097)
XLA Ops:
  6.7 2.6 %collective-permute-start = (f32[144,8,128]{2,1,0:T(8,128)S(1)}, f32[144,8,128]{2,1,0:T(8,128)S(1)}, u32[]{:S(2)}, u32[]{:S(2)}) collective-permute-start(f32[144,8,128]{2,1,0:T(8,128)S(1)} %bitcast_multiply_fusion.1.refs_0_.refs_4_), channel_id=1, source_target_pairs={{4,0},{5,1},{6,2},{7,3},{8,4},{9,5},{10,6},{11,7},{12,8},{13,9},{1... | collective-permute-start | bytes 1769480 | tf_op jit(solution)/shard_map/ppermute | solution.py:383
  10.7 5.6 %shard_map.77 = (f32[144,8,128]{2,1,0:T(8,128)S(1)}, f32[144,8,128]{2,1,0:T(8,128)S(1)}) custom-call(f32[144,8,128]{2,1,0:T(8,128)S(1)} %bitcast_multiply_fusion.1.refs_0_.refs_4_, f32[144,8,128]{2,1,0:T(8,128)S(1)} %bitcast_multiply_fusion.refs_1_.refs_5_, f32[324,8,128]{2,1,0:T(8,128)S(1)} %get-tuple-element.21.refs_2_, ...), custom_call_target="tpu_custom_call" | custom-call | flops 31850496 | bytes 16777216 | tf_op jit(solution)/shard_map/pallas_call | solution.py:138
  16.4 5.6 %collective-permute-done.3.halo_ref = f32[144,8,128]{2,1,0:T(8,128)S(1)} collective-permute-done((f32[144,8,128]{2,1,0:T(8,128)S(1)}, f32[144,8,128]{2,1,0:T(8,128)S(1)}, u32[]{:S(2)}, u32[]{:S(2)}) %collective-permute-start.3) | collective-permute-done | bytes 589856 | tf_op jit(solution)/shard_map/ppermute | solution.py:382
  24.2 1.7 %shard_map.78.refs_1_.refs_5_ = f32[144,8,128]{2,1,0:T(8,128)S(1)} custom-call(f32[144,8,128]{2,1,0:T(8,128)S(1)} %collective-permute-done.halo_ref, f32[144,8,128]{2,1,0:T(8,128)S(1)} %get-tuple-element.22.part_ref, f32[162,8,128]{2,1,0:T(8,128)S(1)} %get-tuple-element.23.coef_ref, f32[2,8,128]{2,1,0:T(8,128)S(1)} %get-tuple-element.40.refs_3_.scale_ref), custom_call_target="tpu_custom_call" | custom-call | flops 7962624 | bytes 5242880 | tf_op jit(solution)/shard_map/pallas_call | solution.py:173
  27.6 5.7 %shard_map.80 = (f32[144,8,128]{2,1,0:T(8,128)S(1)}, f32[144,8,128]{2,1,0:T(8,128)S(1)}) custom-call(f32[144,8,128]{2,1,0:T(8,128)S(1)} %shard_map.79.refs_0_.refs_4_, f32[144,8,128]{2,1,0:T(8,128)S(1)} %shard_map.78.refs_1_.refs_5_, f32[324,8,128]{2,1,0:T(8,128)S(1)} %get-tuple-element.21.refs_2_, f32[2,8,128]{2,1,0:T(8,128)S(1)} %get-tuple-element.39.refs_3_.scale_ref, ...), custom_call_target="tpu_custom_call" | custom-call | flops 31850496 | bytes 16777216 | tf_op jit(solution)/shard_map/pallas_call | solution.py:138
  33.3 4.3 %collective-permute-done.5.halo_ref = f32[144,8,128]{2,1,0:T(8,128)S(1)} collective-permute-done((f32[144,8,128]{2,1,0:T(8,128)S(1)}, f32[144,8,128]{2,1,0:T(8,128)S(1)}, u32[]{:S(2)}, u32[]{:S(2)}) %collective-permute-start.5) | collective-permute-done | bytes 589856 | tf_op jit(solution)/shard_map/ppermute | solution.py:390
  37.7 1.7 %shard_map.82.refs_1_.refs_5_ = f32[144,8,128]{2,1,0:T(8,128)S(1)} custom-call(f32[144,8,128]{2,1,0:T(8,128)S(1)} %collective-permute-done.5.halo_ref, f32[144,8,128]{2,1,0:T(8,128)S(1)} %get-tuple-element.26.part_ref, f32[162,8,128]{2,1,0:T(8,128)S(1)} %get-tuple-element.23.coef_ref, f32[2,8,128]{2,1,0:T(8,128)S(1)} %get-tuple-element.39.refs_3_.scale_ref), custom_call_target="tpu_custom_call" | custom-call | flops 7962624 | bytes 5242880 | tf_op jit(solution)/shard_map/pallas_call | solution.py:173
  39.5 2.3 %collective-permute-done.2.halo_ref = f32[144,8,128]{2,1,0:T(8,128)S(1)} collective-permute-done((f32[144,8,128]{2,1,0:T(8,128)S(1)}, f32[144,8,128]{2,1,0:T(8,128)S(1)}, u32[]{:S(2)}, u32[]{:S(2)}) %collective-permute-start.2) | collective-permute-done | bytes 589856 | tf_op jit(solution)/shard_map/ppermute | solution.py:388
  43.4 1.9 %collective-permute-start.4 = (f32[144,8,128]{2,1,0:T(8,128)S(1)}, f32[144,8,128]{2,1,0:T(8,128)S(1)}, u32[]{:S(2)}, u32[]{:S(2)}) collective-permute-start(f32[144,8,128]{2,1,0:T(8,128)S(1)} %shard_map.81.refs_0_.refs_4_), channel_id=1, source_target_pairs={{4,0},{5,1},{6,2},{7,3},{8,4},{9,5},{10,6},{11,7},{12,8},{13,9},{1... | collective-permute-start | bytes 1769480 | tf_op jit(solution)/shard_map/ppermute | solution.py:390
  45.4 5.7 %shard_map.83 = (f32[144,8,128]{2,1,0:T(8,128)S(1)}, f32[144,8,128]{2,1,0:T(8,128)S(1)}) custom-call(f32[144,8,128]{2,1,0:T(8,128)S(1)} %shard_map.81.refs_0_.refs_4_, f32[144,8,128]{2,1,0:T(8,128)S(1)} %shard_map.82.refs_1_.refs_5_, f32[324,8,128]{2,1,0:T(8,128)S(1)} %get-tuple-element.21.refs_2_, f32[2,8,128]{2,1,0:T(8,128)S(1)} %get-tuple-element.39.refs_3_.scale_ref, ...), custom_call_target="tpu_custom_call" | custom-call | flops 31850496 | bytes 16777216 | tf_op jit(solution)/shard_map/pallas_call | solution.py:138
  51.1 3.4 %collective-permute-done.7.halo_ref = f32[144,8,128]{2,1,0:T(8,128)S(1)} collective-permute-done((f32[144,8,128]{2,1,0:T(8,128)S(1)}, f32[144,8,128]{2,1,0:T(8,128)S(1)}, u32[]{:S(2)}, u32[]{:S(2)}) %collective-permute-start.7) | collective-permute-done | bytes 589856 | tf_op jit(solution)/shard_map/ppermute | solution.py:388
  54.5 1.7 %shard_map.85.refs_0_ = f32[144,8,128]{2,1,0:T(8,128)S(1)} custom-call(f32[144,8,128]{2,1,0:T(8,128)S(1)} %collective-permute-done.7.halo_ref, f32[144,8,128]{2,1,0:T(8,128)S(1)} %get-tuple-element.28.part_ref, f32[162,8,128]{2,1,0:T(8,128)S(1)} %get-tuple-element.23.coef_ref, f32[2,8,128]{2,1,0:T(8,128)S(1)} %get-tuple-element.39.refs_3_.scale_ref), custom_call_target="tpu_custom_call" | custom-call | flops 7962624 | bytes 5242880 | tf_op jit(solution)/shard_map/pallas_call | solution.py:173
  56.2 1.9 %collective-permute-start.8 = (f32[144,8,128]{2,1,0:T(8,128)S(1)}, f32[144,8,128]{2,1,0:T(8,128)S(1)}, u32[]{:S(2)}, u32[]{:S(2)}) collective-permute-start(f32[144,8,128]{2,1,0:T(8,128)S(1)} %shard_map.85.refs_0_), channel_id=1, source_target_pairs={{4,0},{5,1},{6,2},{7,3},{8,4},{9,5},{10,6},{11,7},{12,8},{13,9},{1... | collective-permute-start | bytes 1769480 | tf_op jit(solution)/shard_map/ppermute | solution.py:390
  58.1 1.7 %shard_map.84.refs_1_ = f32[144,8,128]{2,1,0:T(8,128)S(1)} custom-call(f32[144,8,128]{2,1,0:T(8,128)S(1)} %collective-permute-done.4.halo_ref, f32[144,8,128]{2,1,0:T(8,128)S(1)} %get-tuple-element.27.part_ref, f32[162,8,128]{2,1,0:T(8,128)S(1)} %get-tuple-element.23.coef_ref, f32[2,8,128]{2,1,0:T(8,128)S(1)} %get-tuple-element.39.refs_3_.scale_ref), custom_call_target="tpu_custom_call" | custom-call | flops 7962624 | bytes 5242880 | tf_op jit(solution)/shard_map/pallas_call | solution.py:173
  60.1 5.8 %shard_map.86 = (f32[144,8,128]{2,1,0:T(8,128)S(1)}, f32[144,8,128]{2,1,0:T(8,128)S(1)}) custom-call(f32[144,8,128]{2,1,0:T(8,128)S(1)} %shard_map.85.refs_0_, f32[144,8,128]{2,1,0:T(8,128)S(1)} %shard_map.84.refs_1_, f32[324,8,128]{2,1,0:T(8,128)S(1)} %get-tuple-element.21.refs_2_, f32[2,8,128]{2,1,0:T(8,128)S(1)} %get-tuple-element.39.refs_3_.scale_ref, ...), custom_call_target="tpu_custom_call" | custom-call | flops 31850496 | bytes 16777216 | tf_op jit(solution)/shard_map/pallas_call | solution.py:138
  65.9 3.0 %collective-permute-done.8.halo_ref = f32[144,8,128]{2,1,0:T(8,128)S(1)} collective-permute-done((f32[144,8,128]{2,1,0:T(8,128)S(1)}, f32[144,8,128]{2,1,0:T(8,128)S(1)}, u32[]{:S(2)}, u32[]{:S(2)}) %collective-permute-start.8) | collective-permute-done | bytes 589856 | tf_op jit(solution)/shard_map/ppermute | solution.py:390
  68.8 1.7 %shard_map.88.high_ref.refs_1_ = f32[144,8,128]{2,1,0:T(8,128)S(1)} custom-call(f32[144,8,128]{2,1,0:T(8,128)S(1)} %collective-permute-done.8.halo_ref, f32[144,8,128]{2,1,0:T(8,128)S(1)} %get-tuple-element.30.part_ref, f32[162,8,128]{2,1,0:T(8,128)S(1)} %get-tuple-element.23.coef_ref, f32[2,8,128]{2,1,0:T(8,128)S(1)} %get-tuple-element.39.refs_3_.scale_ref), custom_call_target="tpu_custom_call" | custom-call | flops 7962624 | bytes 5242880 | tf_op jit(solution)/shard_map/pallas_call | solution.py:173
  71.0 6.5 %collective-permute-done.6.halo_ref = f32[144,8,128]{2,1,0:T(8,128)S(1)} collective-permute-done((f32[144,8,128]{2,1,0:T(8,128)S(1)}, f32[144,8,128]{2,1,0:T(8,128)S(1)}, u32[]{:S(2)}, u32[]{:S(2)}) %collective-permute-start.6) | collective-permute-done | bytes 589856 | tf_op jit(solution)/shard_map/ppermute | solution.py:388
  80.9 2.0 %collective-permute-start.10 = (f32[144,8,128]{2,1,0:T(8,128)S(1)}, f32[144,8,128]{2,1,0:T(8,128)}, u32[]{:S(2)}, u32[]{:S(2)}) collective-permute-start(f32[144,8,128]{2,1,0:T(8,128)S(1)} %shard_map.87.low_ref.refs_0_), channel_id=1, source_target_pairs={{0,2},{2,0},{1,3},{3,1},{4,6},{6,4},{5,7},{7,5},{8,10},{10,8},{9,1... | collective-permute-start | bytes 1769480 | tf_op jit(solution)/shard_map/ppermute | solution.py:396
  84.0 5.4 %shard_map.90 = (f32[144,8,128]{2,1,0:T(8,128)S(1)}, f32[144,8,128]{2,1,0:T(8,128)S(1)}) custom-call(f32[144,8,128]{2,1,0:T(8,128)S(1)} %shard_map.87.low_ref.refs_0_, f32[144,8,128]{2,1,0:T(8,128)S(1)} %shard_map.88.high_ref.refs_1_, f32[324,8,128]{2,1,0:T(8,128)S(1)} %get-tuple-element.21.refs_2_, f32[2,8,128]{2,1,0:T(8,128)S(1)} %subtract_convert_fusion.refs_3_.scale_ref), custom_call_target="tpu_custom_call" | custom-call | flops 31850496 | bytes 16777216 | tf_op jit(solution)/shard_map/pallas_call | solution.py:138
  91.8 1.7 %shard_map.91.refs_2_ = f32[144,8,128]{2,1,0:T(8,128)S(1)} custom-call(f32[144,8,128]{2,1,0:T(8,128)S(1)} %collective-permute-done.11.halo_ref, f32[144,8,128]{2,1,0:T(8,128)S(1)} %get-tuple-element.31.part_ref, f32[162,8,128]{2,1,0:T(8,128)S(1)} %get-tuple-element.23.coef_ref, f32[2,8,128]{2,1,0:T(8,128)S(1)} %subtract_convert_fusion.refs_3_.scale_ref), custom_call_target="tpu_custom_call" | custom-call | flops 7962624 | bytes 5242880 | tf_op jit(solution)/shard_map/pallas_call | solution.py:173
  93.5 3.6 %collective-permute-done.12.refs_0_ = f32[144,8,128]{2,1,0:T(8,128)S(1)} collective-permute-done((f32[144,8,128]{2,1,0:T(8,128)S(1)}, f32[144,8,128]{2,1,0:T(8,128)S(1)}, u32[]{:S(2)}, u32[]{:S(2)}) %collective-permute-start.12) | collective-permute-done | bytes 589856 | tf_op jit(solution)/shard_map/ppermute | solution.py:396
  100.0 3.9 %collective-permute-done.10.refs_0_ = f32[144,8,128]{2,1,0:T(8,128)} collective-permute-done((f32[144,8,128]{2,1,0:T(8,128)S(1)}, f32[144,8,128]{2,1,0:T(8,128)}, u32[]{:S(2)}, u32[]{:S(2)}) %collective-permute-start.10) | collective-permute-done | bytes 589856 | tf_op jit(solution)/shard_map/ppermute | solution.py:396
  104.6 2.4 %shard_map.96 = (bf16[96,3072]{1,0:T(8,128)(2,1)S(1)}, bf16[96,3072]{1,0:T(8,128)(2,1)S(1)}, f32[96,96]{1,0:T(8,128)S(1)}) custom-call(f32[1152,128]{1,0:T(8,128)S(1)} %bitcast.29, f32[1152,128]{1,0:T(8,128)S(1)} %bitcast.27, f32[1152,128]{1,0:T(8,128)} %bitcast.13.field_ref, f32[8,128]{1,0:T(8,128)S(1)} %get-tuple-element.47.mass_ref), custom_call_target="tpu_custom_call" | custom-call | flops 1048576 | bytes 8388608 | tf_op jit(solution)/shard_map/pallas_call | solution.py:262
  107.1 2.0 %shard_map.97.refs_2_ = f32[96,96]{1,0:T(8,128)S(1)} custom-call(f32[1152,128]{1,0:T(8,128)} %bitcast.19.core_ref, f32[1152,128]{1,0:T(8,128)S(1)} %bitcast.33, bf16[96,3072]{1,0:T(8,128)(2,1)S(1)} %copy-done.2, bf16[96,3072]{1,0:T(8,128)(2,1)S(1)} %copy-done.4), custom_call_target="tpu_custom_call" | custom-call | flops 1048576 | bytes 8388608 | tf_op jit(solution)/shard_map/pallas_call | solution.py:320
  109.1 2.2 %shard_map.98 = f32[144,128]{1,0:T(8,128)S(1)} custom-call(f32[1152,128]{1,0:T(8,128)} %bitcast.5.core_ref, f32[1152,128]{1,0:T(8,128)S(1)} %bitcast.34, bf16[96,3072]{1,0:T(8,128)(2,1)S(1)} %get-tuple-element.34.left_top, bf16[96,3072]{1,0:T(8,128)(2,1)S(1)} %get-tuple-element.35.left_rest, s32[4]{0:T(128)S(1)} %pad_add_fusion.place_ref, ...), custom_call_target="tpu_custom_call" | custom-call | flops 1048576 | bytes 8388608 | tf_op jit(solution)/shard_map/pallas_call | solution.py:320
  113.0 2.6 %collective-permute-start.19 = (f32[144,128]{1,0:T(8,128)S(1)}, f32[144,128]{1,0:T(8,128)S(1)}, u32[]{:S(2)}, u32[]{:S(2)}) collective-permute-start(f32[144,128]{1,0:T(8,128)S(1)} %shard_map.98), channel_id=1, source_target_pairs={{0,12},{4,0},{8,4},{12,8},{16,28},{20,16},{24,20},{28,24},{32,44},... | collective-permute-start | bytes 221192 | tf_op jit(solution)/shard_map/ppermute | solution.py:341
  115.5 3.3 %collective-permute-done.17 = f32[144,128]{1,0:T(8,128)S(1)} collective-permute-done((f32[144,128]{1,0:T(8,128)S(1)}, f32[144,128]{1,0:T(8,128)S(1)}, u32[]{:S(2)}, u32[]{:S(2)}) %collective-permute-start.17) | collective-permute-done | bytes 73760 | tf_op jit(solution)/shard_map/ppermute | solution.py:341
  119.6 20.9 %collective-permute-start.21 = (f32[144,128]{1,0:T(8,128)S(1)}, f32[144,128]{1,0:T(8,128)S(1)}, u32[]{:S(2)}, u32[]{:S(2)}) collective-permute-start(f32[144,128]{1,0:T(8,128)S(1)} %add_add_fusion.1), channel_id=1, source_target_pairs={{0,32},{4,36},{8,40},{12,44},{16,48},{20,52},{24,56},{28,60},{32,0... | collective-permute-start | bytes 221192 | tf_op jit(solution)/shard_map/ppermute | solution.py:341
  141.0 3.7 %collective-permute-done.21 = f32[144,128]{1,0:T(8,128)S(1)} collective-permute-done((f32[144,128]{1,0:T(8,128)S(1)}, f32[144,128]{1,0:T(8,128)S(1)}, u32[]{:S(2)}, u32[]{:S(2)}) %collective-permute-start.21) | collective-permute-done | bytes 73760 | tf_op jit(solution)/shard_map/ppermute | solution.py:341
  146.3 9.2 %collective-permute-done.23 = f32[144,128]{1,0:T(8,128)S(1)} collective-permute-done((f32[144,128]{1,0:T(8,128)S(1)}, f32[144,128]{1,0:T(8,128)S(1)}, u32[]{:S(2)}, u32[]{:S(2)}) %collective-permute-start.23) | collective-permute-done | bytes 73760 | tf_op jit(solution)/shard_map/ppermute | solution.py:341
  155.6 5.8 %collective-permute-done.24 = f32[144,128]{1,0:T(8,128)S(1)} collective-permute-done((f32[144,128]{1,0:T(8,128)S(1)}, f32[144,128]{1,0:T(8,128)S(1)}, u32[]{:S(2)}, u32[]{:S(2)}) %collective-permute-start.24) | collective-permute-done | bytes 73760 | tf_op jit(solution)/shard_map/ppermute | solution.py:341
  (83 shorter events, 29.5 us)
Async XLA Ops:
  1.3 8.1 %collective-permute-start.1 = (f32[1,8,128]{2,1,0:T(8,128)S(1)}, f32[1,8,128]{2,1,0:T(8,128)S(1)}, u32[]{:S(2)}, u32[]{:S(2)}) collective-permute-start(f32[1,8,128]{2,1,0:T(8,128)S(1)} %slice.40), channel_id=1, source_target_pairs={{0,4},{1,5},{2,6},{3,7},{4,8},{5,9},{6,10},{7,11},{8,12},{9,13},{1... | collective-permute-start | bytes 12296 | tf_op jit(solution)/shard_map/ppermute | solution.py:358
  4.9 4.5 %copy-start.8 = (s32[2,8,128]{2,1,0:T(8,128)S(1)}, s32[2,8,128]{2,1,0:T(8,128)}, u32[]{:S(2)}) copy-start(s32[2,8,128]{2,1,0:T(8,128)} %param.8) | copy-start | bytes 24580
  4.9 4.5 %copy-start.9 = (f32[2,8,128]{2,1,0:T(8,128)S(1)}, f32[2,8,128]{2,1,0:T(8,128)}, u32[]{:S(2)}) copy-start(f32[2,8,128]{2,1,0:T(8,128)} %param.7) | copy-start | bytes 24580
  4.9 4.5 %copy-start.10 = (f32[2,8,128]{2,1,0:T(8,128)S(1)}, f32[2,8,128]{2,1,0:T(8,128)}, u32[]{:S(2)}) copy-start(f32[2,8,128]{2,1,0:T(8,128)} %param.6) | copy-start | bytes 24580
  5.0 4.6 %copy-start.7 = (f32[24,24]{1,0:T(8,128)S(1)}, f32[24,24]{1,0:T(8,128)}, u32[]{:S(2)}) copy-start(f32[24,24]{1,0:T(8,128)} %stiff_ref.1) | copy-start | bytes 6916
  5.0 17.0 %collective-permute-start.3 = (f32[144,8,128]{2,1,0:T(8,128)S(1)}, f32[144,8,128]{2,1,0:T(8,128)S(1)}, u32[]{:S(2)}, u32[]{:S(2)}) collective-permute-start(f32[144,8,128]{2,1,0:T(8,128)S(1)} %bitcast_multiply_fusion.refs_1_.refs_5_), channel_id=1, source_target_pairs={{0,4},{1,5},{2,6},{3,7},{4,8},{5,9},{6,10},{7,11},{8,12},{9,13},{1... | collective-permute-start | bytes 1769480 | tf_op jit(solution)/shard_map/ppermute | solution.py:382
  6.7 17.5 %collective-permute-start = (f32[144,8,128]{2,1,0:T(8,128)S(1)}, f32[144,8,128]{2,1,0:T(8,128)S(1)}, u32[]{:S(2)}, u32[]{:S(2)}) collective-permute-start(f32[144,8,128]{2,1,0:T(8,128)S(1)} %bitcast_multiply_fusion.1.refs_0_.refs_4_), channel_id=1, source_target_pairs={{4,0},{5,1},{6,2},{7,3},{8,4},{9,5},{10,6},{11,7},{12,8},{13,9},{1... | collective-permute-start | bytes 1769480 | tf_op jit(solution)/shard_map/ppermute | solution.py:383
  23.7 14.0 %collective-permute-start.5 = (f32[144,8,128]{2,1,0:T(8,128)S(1)}, f32[144,8,128]{2,1,0:T(8,128)S(1)}, u32[]{:S(2)}, u32[]{:S(2)}) collective-permute-start(f32[144,8,128]{2,1,0:T(8,128)S(1)} %shard_map.79.refs_0_.refs_4_), channel_id=1, source_target_pairs={{4,0},{5,1},{6,2},{7,3},{8,4},{9,5},{10,6},{11,7},{12,8},{13,9},{1... | collective-permute-start | bytes 1769480 | tf_op jit(solution)/shard_map/ppermute | solution.py:390
  25.9 15.8 %collective-permute-start.2 = (f32[144,8,128]{2,1,0:T(8,128)S(1)}, f32[144,8,128]{2,1,0:T(8,128)S(1)}, u32[]{:S(2)}, u32[]{:S(2)}) collective-permute-start(f32[144,8,128]{2,1,0:T(8,128)S(1)} %shard_map.78.refs_1_.refs_5_), channel_id=1, source_target_pairs={{0,4},{1,5},{2,6},{3,7},{4,8},{5,9},{6,10},{7,11},{8,12},{9,13},{1... | collective-permute-start | bytes 1769480 | tf_op jit(solution)/shard_map/ppermute | solution.py:388
  39.4 15.1 %collective-permute-start.7 = (f32[144,8,128]{2,1,0:T(8,128)S(1)}, f32[144,8,128]{2,1,0:T(8,128)S(1)}, u32[]{:S(2)}, u32[]{:S(2)}) collective-permute-start(f32[144,8,128]{2,1,0:T(8,128)S(1)} %shard_map.82.refs_1_.refs_5_), channel_id=1, source_target_pairs={{0,4},{1,5},{2,6},{3,7},{4,8},{5,9},{6,10},{7,11},{8,12},{9,13},{1... | collective-permute-start | bytes 1769480 | tf_op jit(solution)/shard_map/ppermute | solution.py:388
  43.4 14.7 %collective-permute-start.4 = (f32[144,8,128]{2,1,0:T(8,128)S(1)}, f32[144,8,128]{2,1,0:T(8,128)S(1)}, u32[]{:S(2)}, u32[]{:S(2)}) collective-permute-start(f32[144,8,128]{2,1,0:T(8,128)S(1)} %shard_map.81.refs_0_.refs_4_), channel_id=1, source_target_pairs={{4,0},{5,1},{6,2},{7,3},{8,4},{9,5},{10,6},{11,7},{12,8},{13,9},{1... | collective-permute-start | bytes 1769480 | tf_op jit(solution)/shard_map/ppermute | solution.py:390
  56.2 12.6 %collective-permute-start.8 = (f32[144,8,128]{2,1,0:T(8,128)S(1)}, f32[144,8,128]{2,1,0:T(8,128)S(1)}, u32[]{:S(2)}, u32[]{:S(2)}) collective-permute-start(f32[144,8,128]{2,1,0:T(8,128)S(1)} %shard_map.85.refs_0_), channel_id=1, source_target_pairs={{4,0},{5,1},{6,2},{7,3},{8,4},{9,5},{10,6},{11,7},{12,8},{13,9},{1... | collective-permute-start | bytes 1769480 | tf_op jit(solution)/shard_map/ppermute | solution.py:390
  59.8 17.7 %collective-permute-start.6 = (f32[144,8,128]{2,1,0:T(8,128)S(1)}, f32[144,8,128]{2,1,0:T(8,128)S(1)}, u32[]{:S(2)}, u32[]{:S(2)}) collective-permute-start(f32[144,8,128]{2,1,0:T(8,128)S(1)} %shard_map.84.refs_1_), channel_id=1, source_target_pairs={{0,4},{1,5},{2,6},{3,7},{4,8},{5,9},{6,10},{7,11},{8,12},{9,13},{1... | collective-permute-start | bytes 1769480 | tf_op jit(solution)/shard_map/ppermute | solution.py:388
  70.5 18.9 %collective-permute-start.13 = (f32[144,8,128]{2,1,0:T(8,128)S(1)}, f32[144,8,128]{2,1,0:T(8,128)S(1)}, u32[]{:S(2)}, u32[]{:S(2)}) collective-permute-start(f32[144,8,128]{2,1,0:T(8,128)S(1)} %shard_map.88.high_ref.refs_1_), channel_id=1, source_target_pairs={{0,4},{1,5},{2,6},{3,7},{4,8},{5,9},{6,10},{7,11},{8,12},{9,13},{1... | collective-permute-start | bytes 1769480 | tf_op jit(solution)/shard_map/ppermute | solution.py:388
  79.2 12.6 %collective-permute-start.11 = (f32[144,8,128]{2,1,0:T(8,128)S(1)}, f32[144,8,128]{2,1,0:T(8,128)S(1)}, u32[]{:S(2)}, u32[]{:S(2)}) collective-permute-start(f32[144,8,128]{2,1,0:T(8,128)S(1)} %shard_map.87.low_ref.refs_0_), channel_id=1, source_target_pairs={{4,0},{5,1},{6,2},{7,3},{8,4},{9,5},{10,6},{11,7},{12,8},{13,9},{1... | collective-permute-start | bytes 1769480 | tf_op jit(solution)/shard_map/ppermute | solution.py:390
  80.9 16.3 %collective-permute-start.12 = (f32[144,8,128]{2,1,0:T(8,128)S(1)}, f32[144,8,128]{2,1,0:T(8,128)S(1)}, u32[]{:S(2)}, u32[]{:S(2)}) collective-permute-start(f32[144,8,128]{2,1,0:T(8,128)S(1)} %shard_map.88.high_ref.refs_1_), channel_id=1, source_target_pairs={{0,2},{2,0},{1,3},{3,1},{4,6},{6,4},{5,7},{7,5},{8,10},{10,8},{9,1... | collective-permute-start | bytes 1769480 | tf_op jit(solution)/shard_map/ppermute | solution.py:396
  80.9 23.1 %collective-permute-start.10 = (f32[144,8,128]{2,1,0:T(8,128)S(1)}, f32[144,8,128]{2,1,0:T(8,128)}, u32[]{:S(2)}, u32[]{:S(2)}) collective-permute-start(f32[144,8,128]{2,1,0:T(8,128)S(1)} %shard_map.87.low_ref.refs_0_), channel_id=1, source_target_pairs={{0,2},{2,0},{1,3},{3,1},{4,6},{6,4},{5,7},{7,5},{8,10},{10,8},{9,1... | collective-permute-start | bytes 1769480 | tf_op jit(solution)/shard_map/ppermute | solution.py:396
  82.9 24.1 %collective-permute-start.15 = (f32[144,8,128]{2,1,0:T(8,128)S(1)}, f32[144,8,128]{2,1,0:T(8,128)}, u32[]{:S(2)}, u32[]{:S(2)}) collective-permute-start(f32[144,8,128]{2,1,0:T(8,128)S(1)} %shard_map.88.high_ref.refs_1_), channel_id=1, source_target_pairs={{0,1},{1,0},{2,3},{3,2},{4,5},{5,4},{6,7},{7,6},{8,9},{9,8},{10,11... | collective-permute-start | bytes 1769480 | tf_op jit(solution)/shard_map/ppermute | solution.py:407
  89.5 19.6 %collective-permute-start.9 = (f32[144,8,128]{2,1,0:T(8,128)S(1)}, f32[144,8,128]{2,1,0:T(8,128)}, u32[]{:S(2)}, u32[]{:S(2)}) collective-permute-start(f32[144,8,128]{2,1,0:T(8,128)S(1)} %shard_map.87.low_ref.refs_0_), channel_id=1, source_target_pairs={{0,1},{1,0},{2,3},{3,2},{4,5},{5,4},{6,7},{7,6},{8,9},{9,8},{10,11... | collective-permute-start | bytes 1769480 | tf_op jit(solution)/shard_map/ppermute | solution.py:407
  91.8 5.3 %copy-start = (f32[144,2,8,128]{3,2,1,0:T(8,128)S(1)}, f32[144,2,8,128]{3,2,1,0:T(8,128)}, u32[]{:S(2)}) copy-start(f32[144,2,8,128]{3,2,1,0:T(8,128)} %shard_map.89.refs_3_) | copy-start | bytes 3538948
  97.1 9.9 %collective-permute-start.16 = (f32[144,8,128]{2,1,0:T(8,128)S(1)}, f32[144,8,128]{2,1,0:T(8,128)S(1)}, u32[]{:S(2)}, u32[]{:S(2)}) collective-permute-start(f32[144,8,128]{2,1,0:T(8,128)S(1)} %shard_map.93), channel_id=1, source_target_pairs={{0,1},{1,0},{2,3},{3,2},{4,5},{5,4},{6,7},{7,6},{8,9},{9,8},{10,11... | collective-permute-start | bytes 1769480 | tf_op jit(solution)/shard_map/ppermute | solution.py:408
  104.5 4.6 %collective-permute-start.14 = (f32[144,8,128]{2,1,0:T(8,128)}, f32[144,8,128]{2,1,0:T(8,128)S(1)}, u32[]{:S(2)}, u32[]{:S(2)}) collective-permute-start(f32[144,8,128]{2,1,0:T(8,128)} %shard_map.95), channel_id=1, source_target_pairs={{0,1},{1,0},{2,3},{3,2},{4,5},{5,4},{6,7},{7,6},{8,9},{9,8},{10,11... | collective-permute-start | bytes 1769480 | tf_op jit(solution)/shard_map/ppermute | solution.py:408
  104.5 2.5 %copy-start.2 = (bf16[96,3072]{1,0:T(8,128)(2,1)S(1)}, bf16[96,3072]{1,0:T(8,128)(2,1)}, u32[]{:S(2)}) copy-start(bf16[96,3072]{1,0:T(8,128)(2,1)} %copy-done.1) | copy-start | bytes 1769476
  104.5 2.5 %copy-start.4 = (bf16[96,3072]{1,0:T(8,128)(2,1)S(1)}, bf16[96,3072]{1,0:T(8,128)(2,1)}, u32[]{:S(2)}) copy-start(bf16[96,3072]{1,0:T(8,128)(2,1)} %copy-done.3) | copy-start | bytes 1769476
  111.3 7.6 %collective-permute-start.17 = (f32[144,128]{1,0:T(8,128)S(1)}, f32[144,128]{1,0:T(8,128)S(1)}, u32[]{:S(2)}, u32[]{:S(2)}) collective-permute-start(f32[144,128]{1,0:T(8,128)S(1)} %shard_map.98), channel_id=1, source_target_pairs={{0,4},{4,8},{8,12},{12,0},{16,20},{20,24},{24,28},{28,16},{32,36},... | collective-permute-start | bytes 221192 | tf_op jit(solution)/shard_map/ppermute | solution.py:341
  112.8 6.1 %collective-permute-start.18 = (f32[144,128]{1,0:T(8,128)S(1)}, f32[144,128]{1,0:T(8,128)S(1)}, u32[]{:S(2)}, u32[]{:S(2)}) collective-permute-start(f32[144,128]{1,0:T(8,128)S(1)} %shard_map.98), channel_id=1, source_target_pairs={{0,8},{4,12},{8,0},{12,4},{16,24},{20,28},{24,16},{28,20},{32,40},... | collective-permute-start | bytes 221192 | tf_op jit(solution)/shard_map/ppermute | solution.py:341
  113.0 6.5 %collective-permute-start.19 = (f32[144,128]{1,0:T(8,128)S(1)}, f32[144,128]{1,0:T(8,128)S(1)}, u32[]{:S(2)}, u32[]{:S(2)}) collective-permute-start(f32[144,128]{1,0:T(8,128)S(1)} %shard_map.98), channel_id=1, source_target_pairs={{0,12},{4,0},{8,4},{12,8},{16,28},{20,16},{24,20},{28,24},{32,44},... | collective-permute-start | bytes 221192 | tf_op jit(solution)/shard_map/ppermute | solution.py:341
  119.5 21.5 %collective-permute-start.20 = (f32[144,128]{1,0:T(8,128)S(1)}, f32[144,128]{1,0:T(8,128)S(1)}, u32[]{:S(2)}, u32[]{:S(2)}) collective-permute-start(f32[144,128]{1,0:T(8,128)S(1)} %add_add_fusion.1), channel_id=1, source_target_pairs={{0,16},{4,20},{8,24},{12,28},{16,32},{20,36},{24,40},{28,44},{32,4... | collective-permute-start | bytes 221192 | tf_op jit(solution)/shard_map/ppermute | solution.py:341
  119.6 25.0 %collective-permute-start.21 = (f32[144,128]{1,0:T(8,128)S(1)}, f32[144,128]{1,0:T(8,128)S(1)}, u32[]{:S(2)}, u32[]{:S(2)}) collective-permute-start(f32[144,128]{1,0:T(8,128)S(1)} %add_add_fusion.1), channel_id=1, source_target_pairs={{0,32},{4,36},{8,40},{12,44},{16,48},{20,52},{24,56},{28,60},{32,0... | collective-permute-start | bytes 221192 | tf_op jit(solution)/shard_map/ppermute | solution.py:341
  140.5 5.7 %collective-permute-start.22 = (f32[144,128]{1,0:T(8,128)S(1)}, f32[144,128]{1,0:T(8,128)S(1)}, u32[]{:S(2)}, u32[]{:S(2)}) collective-permute-start(f32[144,128]{1,0:T(8,128)S(1)} %add_add_fusion.1), channel_id=1, source_target_pairs={{0,48},{4,52},{8,56},{12,60},{16,0},{20,4},{24,8},{28,12},{32,16},... | collective-permute-start | bytes 221192 | tf_op jit(solution)/shard_map/ppermute | solution.py:341
  146.2 9.3 %collective-permute-start.23 = (f32[144,128]{1,0:T(8,128)S(1)}, f32[144,128]{1,0:T(8,128)S(1)}, u32[]{:S(2)}, u32[]{:S(2)}) collective-permute-start(f32[144,128]{1,0:T(8,128)S(1)} %add_add_fusion), channel_id=1, source_target_pairs={{0,64},{4,68},{8,72},{12,76},{16,80},{20,84},{24,88},{28,92},{32,9... | collective-permute-start | bytes 221192 | tf_op jit(solution)/shard_map/ppermute | solution.py:341
  155.5 5.9 %collective-permute-start.24 = (f32[144,128]{1,0:T(8,128)S(1)}, f32[144,128]{1,0:T(8,128)S(1)}, u32[]{:S(2)}, u32[]{:S(2)}) collective-permute-start(f32[144,128]{1,0:T(8,128)S(1)} %add.52), channel_id=1, source_target_pairs={{0,128},{4,132},{8,136},{12,140},{16,144},{20,148},{24,152},{28,15... | collective-permute-start | bytes 221192 | tf_op jit(solution)/shard_map/ppermute | solution.py:341
  (4 other events, 4.3 us)

commit v4 on v3

--- a/solution.py
+++ b/solution.py
@@ -95,6 +95,30 @@
     return acc[0] + rolled(acc[1], -1, 0) + rolled(acc[2], 1, 0)
 
 
+def start_kernel(field_ref, support_ref, modulus_ref, low_ref, high_ref, edge_ref):
+    free = [(1 - support_ref[p]).astype(jnp.float32) for p in range(2)]
+    low_ref[...] = field_ref[:, 0] * free[0]
+    high_ref[...] = field_ref[:, 1] * free[1]
+    edge_ref[0] = modulus_ref[1]
+
+
+def start(field, support, modulus):
+    count, planes, rows, depth = field.shape
+    tile = count // 4
+    plane = pl.BlockSpec((tile, rows, depth), lambda i: (i, 0, 0))
+    edge = pl.BlockSpec((1, rows, depth), lambda i: (0, 0, 0))
+    both = pl.BlockSpec((planes, rows, depth), lambda i: (0, 0, 0))
+    return pl.pallas_call(
+        start_kernel,
+        grid=(4,),
+        in_specs=[pl.BlockSpec((tile, planes, rows, depth), lambda i: (i, 0, 0, 0)), both, both],
+        out_specs=[plane, plane, edge],
+        out_shape=[spec((count, rows, depth))] * 2 + [spec((1, rows, depth))],
+        cost_estimate=cost(2 * field.size, 8 * field.size),
+        compiler_params=compiled(),
+    )(field, support, modulus)
+
+
 def added(acc, key, term):
     acc[key] = acc[key] + term if key in acc else term
 
@@ -239,7 +263,8 @@
     )(x, *after)
 
 
-def near_kernel(stiff_ref, own_ref, field_ref, mass_ref, left_top, left_rest, out_ref, top, rest):
+def near_kernel(stiff_ref, own_ref, field_ref, mass_ref, *refs):
+    left_top, left_rest, out_ref, top, rest = refs[-5:]
     modes = top.shape[0] // 2
     first, second = pl.ds(0, modes), pl.ds(modes, modes)
 
@@ -255,40 +280,43 @@
     out_ref[...] = product(top[...], rest[...], left_top[...], left_rest[...])
 
 
-def near_gram(stiff, own, by_x, mass, modes):
+def near_gram(stiff, own, by_x, mass, modes, after=()):
     wide = own.size // modes
     shape = (2 * modes, wide)
     depth = mass.shape[-1]
     return pl.pallas_call(
         near_kernel,
-        in_specs=[IN_VMEM] * 4,
+        in_specs=[IN_VMEM] * 4 + [ANYWHERE] * len(after),
         out_specs=[IN_VMEM] * 3,
         out_shape=[spec(shape, jnp.bfloat16)] * 2 + [spec((2 * modes, 2 * modes))],
         scratch_shapes=[pltpu.VMEM(shape, jnp.bfloat16)] * 2,
         cost_estimate=cost(1 << 20, 8 << 20),
         compiler_params=compiled(),
-    )(*(a.reshape(-1, depth) for a in (stiff, own, by_x)), mass)
-
-
-def far_product(core_ref, both_ref, left_top, left_rest, top, rest):
+    )(*(a.reshape(-1, depth) for a in (stiff, own, by_x)), mass, *after)
+
+
+def far_product(p, core_ref, both_ref, left_top, left_rest, top, rest):
     modes = top.shape[0] // 2
     first, second = pl.ds(0, modes), pl.ds(modes, modes)
+    rows = top.shape[1] // (3 * both_ref.shape[1])
 
     def do(row, at):
-        top[first, at], rest[first, at] = split(modes_at(core_ref, row, modes))
+        comp, inner = lax.div(row, rows), lax.rem(row, rows)
+        core_row = (2 * comp + p) * rows + inner
+        top[first, at], rest[first, at] = split(modes_at(core_ref, core_row, modes))
         top[second, at], rest[second, at] = split(modes_at(both_ref, row, modes))
 
-    each_row(core_ref, modes, do)
+    each_row(both_ref, modes, do)
     return product(top[...], rest[...], left_top[...], left_rest[...])
 
 
-def far_kernel(core_ref, both_ref, left_top, left_rest, out_ref, top, rest):
-    out_ref[...] = far_product(core_ref, both_ref, left_top, left_rest, top, rest)
-
-
-def last_kernel(factor, core_ref, both_ref, left_top, left_rest, place_ref, *refs):
+def far_kernel(p, core_ref, both_ref, left_top, left_rest, out_ref, top, rest):
+    out_ref[...] = far_product(p, core_ref, both_ref, left_top, left_rest, top, rest)
+
+
+def last_kernel(factor, p, core_ref, both_ref, left_top, left_rest, place_ref, *refs):
     nears, fars, out_ref, top, rest, turned = refs[:2], refs[2:-4], *refs[-4:]
-    far = far_product(core_ref, both_ref, left_top, left_rest, top, rest)
+    far = far_product(p, core_ref, both_ref, left_top, left_rest, top, rest)
     modes = top.shape[0] // 2
     far = far + fars[0][...]
     near = nears[0][...] + nears[1][...]
@@ -302,18 +330,18 @@
     out_ref[2 * modes :, :] = jnp.concatenate([tail[:modes], tail[modes:]], 1)
 
 
-def far_gram(by_core, by_both, left, modes, last=None):
-    wide = by_core.size // modes
+def far_gram(p, by_core, by_both, left, modes, last=None):
+    wide = by_both.size // modes
     shape = (2 * modes, wide)
     depth = by_core.shape[-1]
     args = [a.reshape(-1, depth) for a in (by_core, by_both)] + list(left)
     specs = [IN_VMEM] * 4
     scratch = [pltpu.VMEM(shape, jnp.bfloat16)] * 2
     if last is None:
-        kernel, out = far_kernel, (2 * modes, 2 * modes)
+        kernel, out = partial(far_kernel, p), (2 * modes, 2 * modes)
     else:
         factor, place, nears, fars = last
-        kernel, out = partial(last_kernel, factor), (3 * modes, 128)
+        kernel, out = partial(last_kernel, factor, p), (3 * modes, 128)
         args += [place, *nears, *fars]
         specs += [pl.BlockSpec(memory_space=pltpu.SMEM)] + [IN_VMEM] * 3
         scratch.append(pltpu.VMEM((4 * modes, 2 * modes), jnp.float32))
@@ -355,13 +383,11 @@
     ]
     down = [(b, a) for a, b in up]
     everywhere = SLAB + MODE
-    lower_layer = lax.ppermute(modulus[planes - 1 :], everywhere, up)
+    *current, edge = start(
+        subspace.reshape(modes * comps, planes, rows, depth), support, modulus
+    )
+    lower_layer = lax.ppermute(edge, everywhere, up)
     free = (1 - support).astype(jnp.float32)
-
-    def masked(p):
-        return (free[p] * subspace[:, :, p]).reshape(modes * comps, rows, depth)
-
-    current = (masked(0), masked(1))
     layers = jnp.concatenate([lower_layer, modulus], 0)
     plane_index = (
         lax.axis_index(SLAB) * planes - 1 + lax.broadcasted_iota(jnp.int32, layers.shape, 0)
@@ -400,19 +426,21 @@
     me = lax.axis_index(MODE)
     place = jnp.stack([me ^ r for r in range(4)]).astype(jnp.int32)
     factor = 1.0 / (float(comps) * planes * slabs * rows * depth)
+    by_core = lax.ppermute(filtered, "core", swap)
     nears, fars = [], []
     after = (*stiffened, filtered)
     for p in (1, 0):
         by_x[p] = held(by_x[p], *after)
-        by_core = lax.ppermute(current[p], "core", swap)
         by_both = lax.ppermute(by_x[p], "core", swap)
-        *left, near = near_gram(stiffened[p], current[p], by_x[p], mass[p], modes)
+        *left, near = near_gram(
+            stiffened[p], current[p], by_x[p], mass[p], modes, by_x[:1] if p else ()
+        )
         nears.append(near)
-        after = (near,)
         last = (factor, place, nears, fars) if p == 0 else None
-        fars.append(far_gram(by_core, by_both, left, modes, last))
+        fars.append(far_gram(p, by_core, by_both, left, modes, last))
+        after = (near, fars[0])
     grams = fars[-1]
-    for groups in ((16, 4, 1), (4, 4, 4), (2, 2, 16), (1, 2, 32)):
+    for groups in ((16, 4, 1), (8, 2, 4), (2, 4, 8), (1, 2, 32)):
         grams = total_over(grams, SLAB, groups)
     tail = grams[2 * modes :]
     wide = 4 * modes - depth

time: 162 us -> 159 us (0.981)
  waiting for transfers between devices: 57.2 us -> 54.5 us
    ppermute x8, waiting for transfers between devices: 24.6 us -> 18.8 us  [total_over(): parts.append(lax.ppermute(x, axes, pairs))]
    ppermute x2, waiting for transfers between devices: 7.56 us -> 10.6 us  [body(): by_x[p] = lax.ppermute(current[p], 'xl', swap)]
    slice x2 -> x0, local copies, waits for them, and re-layouts: 2.01 us -> none  [the longest x1 1.32 us: masked(): return (free[p] * subspace[:, :, p]).reshape(modes * comps, rows, depth)]
    unnamed x22 -> x28, local copies, waits for them, and re-layouts: 2.29 us -> 3.29 us
    pallas_call x2 -> x3, Pallas kernels: 3.6 us -> 2.65 us  [the longest x2 2.5 us: near_gram(): pl.pallas_call(near_kernel, in_specs=[IN_VMEM] * 4 + [ANYWHERE] * len(aft...]
  transfers between devices with their start and end apart: 25 -> 24, of which waited for: 15 -> 16; matrix products, arithmetic and copies ran while one was open for 1% -> 0% of each run, Pallas kernels for 33% -> 32%
where the time goes in v4:
time: 159 us; the launch traced here: 158 us
  waiting for transfers between devices  54.5 us (34%)
  Pallas kernels  54.4 us (34%)
  starting transfers between devices  43.7 us (27%)
  local copies, waits for them, and re-layouts  3.37 us (2%)
    pallas_call x5, Pallas kernels, own_part(): pl.pallas_call(partial(own_kernel, shift, count), in_specs=[IN_VMEM] * le...  29.3 us
    ppermute x8, starting transfers between devices, total_over(): parts.append(lax.ppermute(x, axes, pairs))  26.8 us
    ppermute x8, waiting for transfers between devices, total_over(): parts.append(lax.ppermute(x, axes, pairs))  18.8 us
    pallas_call x10, Pallas kernels, with_halo(): pl.pallas_call(partial(halo_kernel, p), in_specs=[IN_VMEM] * 4, out_specs...  17 us
    ppermute x4, waiting for transfers between devices, body(): below = lax.ppermute(high, everywhere, up)  12.1 us
    ppermute x2, waiting for transfers between devices, body(): by_x[p] = lax.ppermute(current[p], 'xl', swap)  10.6 us
    ppermute x4, starting transfers between devices, body(): upper = lax.ppermute(low, everywhere, down)  6.77 us
    ppermute x4, waiting for transfers between devices, body(): upper = lax.ppermute(low, everywhere, down)  6.76 us
  transfers between devices with their start and end apart: 24, of which 16 were waited for; matrix products, arithmetic and copies ran while one was open for 0% of the time, Pallas kernels for 32%

profile of v4, /device:TPU:32, one launch (start us, length us, event | category | flops | bytes accessed | tf_op | source)
XLA Modules:
  0.0 157.8 jit_solution(14690799079488403301)
XLA Ops:
  6.7 2.6 %collective-permute-start = (f32[144,8,128]{2,1,0:T(8,128)S(1)}, f32[144,8,128]{2,1,0:T(8,128)S(1)}, u32[]{:S(2)}, u32[]{:S(2)}) collective-permute-start(f32[144,8,128]{2,1,0:T(8,128)S(1)} %get-tuple-element.24.refs_0_.refs_4_), channel_id=1, source_target_pairs={{4,0},{5,1},{6,2},{7,3},{8,4},{9,5},{10,6},{11,7},{12,8},{13,9},{1... | collective-permute-start | bytes 1769480 | tf_op jit(solution)/shard_map/ppermute | solution.py:409
  10.6 5.9 %shard_map.78 = (f32[144,8,128]{2,1,0:T(8,128)S(1)}, f32[144,8,128]{2,1,0:T(8,128)S(1)}) custom-call(f32[144,8,128]{2,1,0:T(8,128)S(1)} %get-tuple-element.24.refs_0_.refs_4_, f32[144,8,128]{2,1,0:T(8,128)S(1)} %get-tuple-element.25.refs_1_.refs_5_, f32[324,8,128]{2,1,0:T(8,128)S(1)} %get-tuple-element.27.refs_2_, ...), custom_call_target="tpu_custom_call" | custom-call | flops 31850496 | bytes 16777216 | tf_op jit(solution)/shard_map/pallas_call | solution.py:162
  16.5 5.5 %collective-permute-done.3.halo_ref = f32[144,8,128]{2,1,0:T(8,128)S(1)} collective-permute-done((f32[144,8,128]{2,1,0:T(8,128)S(1)}, f32[144,8,128]{2,1,0:T(8,128)S(1)}, u32[]{:S(2)}, u32[]{:S(2)}) %collective-permute-start.3) | collective-permute-done | bytes 589856 | tf_op jit(solution)/shard_map/ppermute | solution.py:408
  27.6 5.9 %shard_map.81 = (f32[144,8,128]{2,1,0:T(8,128)S(1)}, f32[144,8,128]{2,1,0:T(8,128)S(1)}) custom-call(f32[144,8,128]{2,1,0:T(8,128)S(1)} %shard_map.80.refs_0_.refs_4_, f32[144,8,128]{2,1,0:T(8,128)S(1)} %shard_map.79.refs_1_.refs_5_, f32[324,8,128]{2,1,0:T(8,128)S(1)} %get-tuple-element.27.refs_2_, f32[2,8,128]{2,1,0:T(8,128)S(1)} %get-tuple-element.45.refs_3_.scale_ref, ...), custom_call_target="tpu_custom_call" | custom-call | flops 31850496 | bytes 16777216 | tf_op jit(solution)/shard_map/pallas_call | solution.py:162
  33.6 4.1 %collective-permute-done.5.halo_ref = f32[144,8,128]{2,1,0:T(8,128)S(1)} collective-permute-done((f32[144,8,128]{2,1,0:T(8,128)S(1)}, f32[144,8,128]{2,1,0:T(8,128)S(1)}, u32[]{:S(2)}, u32[]{:S(2)}) %collective-permute-start.5) | collective-permute-done | bytes 589856 | tf_op jit(solution)/shard_map/ppermute | solution.py:416
  37.7 1.7 %shard_map.83.refs_1_.refs_5_ = f32[144,8,128]{2,1,0:T(8,128)S(1)} custom-call(f32[144,8,128]{2,1,0:T(8,128)S(1)} %collective-permute-done.5.halo_ref, f32[144,8,128]{2,1,0:T(8,128)S(1)} %get-tuple-element.32.part_ref, f32[162,8,128]{2,1,0:T(8,128)S(1)} %get-tuple-element.29.coef_ref, f32[2,8,128]{2,1,0:T(8,128)S(1)} %get-tuple-element.45.refs_3_.scale_ref), custom_call_target="tpu_custom_call" | custom-call | flops 7962624 | bytes 5242880 | tf_op jit(solution)/shard_map/pallas_call | solution.py:197
  39.5 2.3 %collective-permute-done.2.halo_ref = f32[144,8,128]{2,1,0:T(8,128)S(1)} collective-permute-done((f32[144,8,128]{2,1,0:T(8,128)S(1)}, f32[144,8,128]{2,1,0:T(8,128)S(1)}, u32[]{:S(2)}, u32[]{:S(2)}) %collective-permute-start.2) | collective-permute-done | bytes 589856 | tf_op jit(solution)/shard_map/ppermute | solution.py:414
  43.5 1.9 %collective-permute-start.4 = (f32[144,8,128]{2,1,0:T(8,128)S(1)}, f32[144,8,128]{2,1,0:T(8,128)S(1)}, u32[]{:S(2)}, u32[]{:S(2)}) collective-permute-start(f32[144,8,128]{2,1,0:T(8,128)S(1)} %shard_map.82.refs_0_.refs_4_), channel_id=1, source_target_pairs={{4,0},{5,1},{6,2},{7,3},{8,4},{9,5},{10,6},{11,7},{12,8},{13,9},{1... | collective-permute-start | bytes 1769480 | tf_op jit(solution)/shard_map/ppermute | solution.py:416
  45.4 5.9 %shard_map.84 = (f32[144,8,128]{2,1,0:T(8,128)S(1)}, f32[144,8,128]{2,1,0:T(8,128)S(1)}) custom-call(f32[144,8,128]{2,1,0:T(8,128)S(1)} %shard_map.82.refs_0_.refs_4_, f32[144,8,128]{2,1,0:T(8,128)S(1)} %shard_map.83.refs_1_.refs_5_, f32[324,8,128]{2,1,0:T(8,128)S(1)} %get-tuple-element.27.refs_2_, f32[2,8,128]{2,1,0:T(8,128)S(1)} %get-tuple-element.45.refs_3_.scale_ref, ...), custom_call_target="tpu_custom_call" | custom-call | flops 31850496 | bytes 16777216 | tf_op jit(solution)/shard_map/pallas_call | solution.py:162
  51.3 3.2 %collective-permute-done.7.halo_ref = f32[144,8,128]{2,1,0:T(8,128)S(1)} collective-permute-done((f32[144,8,128]{2,1,0:T(8,128)S(1)}, f32[144,8,128]{2,1,0:T(8,128)S(1)}, u32[]{:S(2)}, u32[]{:S(2)}) %collective-permute-start.7) | collective-permute-done | bytes 589856 | tf_op jit(solution)/shard_map/ppermute | solution.py:414
  56.2 2.2 %collective-permute-start.8 = (f32[144,8,128]{2,1,0:T(8,128)S(1)}, f32[144,8,128]{2,1,0:T(8,128)S(1)}, u32[]{:S(2)}, u32[]{:S(2)}) collective-permute-start(f32[144,8,128]{2,1,0:T(8,128)S(1)} %shard_map.86.refs_0_), channel_id=1, source_target_pairs={{4,0},{5,1},{6,2},{7,3},{8,4},{9,5},{10,6},{11,7},{12,8},{13,9},{1... | collective-permute-start | bytes 1769480 | tf_op jit(solution)/shard_map/ppermute | solution.py:416
  58.5 1.7 %shard_map.85.refs_1_ = f32[144,8,128]{2,1,0:T(8,128)S(1)} custom-call(f32[144,8,128]{2,1,0:T(8,128)S(1)} %collective-permute-done.4.halo_ref, f32[144,8,128]{2,1,0:T(8,128)S(1)} %get-tuple-element.33.part_ref, f32[162,8,128]{2,1,0:T(8,128)S(1)} %get-tuple-element.29.coef_ref, f32[2,8,128]{2,1,0:T(8,128)S(1)} %get-tuple-element.45.refs_3_.scale_ref), custom_call_target="tpu_custom_call" | custom-call | flops 7962624 | bytes 5242880 | tf_op jit(solution)/shard_map/pallas_call | solution.py:197
  60.3 5.9 %shard_map.87 = (f32[144,8,128]{2,1,0:T(8,128)S(1)}, f32[144,8,128]{2,1,0:T(8,128)S(1)}) custom-call(f32[144,8,128]{2,1,0:T(8,128)S(1)} %shard_map.86.refs_0_, f32[144,8,128]{2,1,0:T(8,128)S(1)} %shard_map.85.refs_1_, f32[324,8,128]{2,1,0:T(8,128)S(1)} %get-tuple-element.27.refs_2_, f32[2,8,128]{2,1,0:T(8,128)S(1)} %get-tuple-element.45.refs_3_.scale_ref, ...), custom_call_target="tpu_custom_call" | custom-call | flops 31850496 | bytes 16777216 | tf_op jit(solution)/shard_map/pallas_call | solution.py:162
  66.2 2.6 %collective-permute-done.8.halo_ref = f32[144,8,128]{2,1,0:T(8,128)S(1)} collective-permute-done((f32[144,8,128]{2,1,0:T(8,128)S(1)}, f32[144,8,128]{2,1,0:T(8,128)S(1)}, u32[]{:S(2)}, u32[]{:S(2)}) %collective-permute-start.8) | collective-permute-done | bytes 589856 | tf_op jit(solution)/shard_map/ppermute | solution.py:416
  68.8 1.7 %shard_map.89.high_ref.refs_1_ = f32[144,8,128]{2,1,0:T(8,128)S(1)} custom-call(f32[144,8,128]{2,1,0:T(8,128)S(1)} %collective-permute-done.8.halo_ref, f32[144,8,128]{2,1,0:T(8,128)S(1)} %get-tuple-element.36.part_ref, f32[162,8,128]{2,1,0:T(8,128)S(1)} %get-tuple-element.29.coef_ref, f32[2,8,128]{2,1,0:T(8,128)S(1)} %get-tuple-element.45.refs_3_.scale_ref), custom_call_target="tpu_custom_call" | custom-call | flops 7962624 | bytes 5242880 | tf_op jit(solution)/shard_map/pallas_call | solution.py:197
  71.1 6.7 %collective-permute-done.6.halo_ref = f32[144,8,128]{2,1,0:T(8,128)S(1)} collective-permute-done((f32[144,8,128]{2,1,0:T(8,128)S(1)}, f32[144,8,128]{2,1,0:T(8,128)S(1)}, u32[]{:S(2)}, u32[]{:S(2)}) %collective-permute-start.6) | collective-permute-done | bytes 589856 | tf_op jit(solution)/shard_map/ppermute | solution.py:414
  79.4 2.1 %collective-permute-start.11 = (f32[144,8,128]{2,1,0:T(8,128)S(1)}, f32[144,8,128]{2,1,0:T(8,128)S(1)}, u32[]{:S(2)}, u32[]{:S(2)}) collective-permute-start(f32[144,8,128]{2,1,0:T(8,128)S(1)} %shard_map.88.low_ref.refs_0_), channel_id=1, source_target_pairs={{4,0},{5,1},{6,2},{7,3},{8,4},{9,5},{10,6},{11,7},{12,8},{13,9},{1... | collective-permute-start | bytes 1769480 | tf_op jit(solution)/shard_map/ppermute | solution.py:416
  82.6 2.0 %collective-permute-start.10 = (f32[144,8,128]{2,1,0:T(8,128)S(1)}, f32[144,8,128]{2,1,0:T(8,128)S(1)}, u32[]{:S(2)}, u32[]{:S(2)}) collective-permute-start(f32[144,8,128]{2,1,0:T(8,128)S(1)} %shard_map.88.low_ref.refs_0_), channel_id=1, source_target_pairs={{0,2},{2,0},{1,3},{3,1},{4,6},{6,4},{5,7},{7,5},{8,10},{10,8},{9,1... | collective-permute-start | bytes 1769480 | tf_op jit(solution)/shard_map/ppermute | solution.py:422
  84.7 5.7 %shard_map.91 = (f32[144,8,128]{2,1,0:T(8,128)S(1)}, f32[144,8,128]{2,1,0:T(8,128)S(1)}) custom-call(f32[144,8,128]{2,1,0:T(8,128)S(1)} %shard_map.88.low_ref.refs_0_, f32[144,8,128]{2,1,0:T(8,128)S(1)} %shard_map.89.high_ref.refs_1_, f32[324,8,128]{2,1,0:T(8,128)S(1)} %get-tuple-element.27.refs_2_, f32[2,8,128]{2,1,0:T(8,128)S(1)} %subtract_convert_fusion.refs_3_.scale_ref), custom_call_target="tpu_custom_call" | custom-call | flops 31850496 | bytes 16777216 | tf_op jit(solution)/shard_map/pallas_call | solution.py:162
  90.4 1.7 %shard_map.93.refs_1_ = f32[144,8,128]{2,1,0:T(8,128)S(1)} custom-call(f32[144,8,128]{2,1,0:T(8,128)S(1)} %collective-permute-done.13.halo_ref, f32[144,8,128]{2,1,0:T(8,128)S(1)} %get-tuple-element.38.part_ref, f32[162,8,128]{2,1,0:T(8,128)S(1)} %get-tuple-element.29.coef_ref, f32[2,8,128]{2,1,0:T(8,128)S(1)} %subtract_convert_fusion.refs_3_.scale_ref), custom_call_target="tpu_custom_call" | custom-call | flops 7962624 | bytes 5242880 | tf_op jit(solution)/shard_map/pallas_call | solution.py:197
  92.1 1.7 %shard_map.92.refs_2_ = f32[144,8,128]{2,1,0:T(8,128)S(1)} custom-call(f32[144,8,128]{2,1,0:T(8,128)S(1)} %collective-permute-done.11.halo_ref, f32[144,8,128]{2,1,0:T(8,128)S(1)} %get-tuple-element.37.part_ref, f32[162,8,128]{2,1,0:T(8,128)S(1)} %get-tuple-element.29.coef_ref, f32[2,8,128]{2,1,0:T(8,128)S(1)} %subtract_convert_fusion.refs_3_.scale_ref), custom_call_target="tpu_custom_call" | custom-call | flops 7962624 | bytes 5242880 | tf_op jit(solution)/shard_map/pallas_call | solution.py:197
  93.8 3.7 %collective-permute-done.12.refs_0_ = f32[144,8,128]{2,1,0:T(8,128)S(1)} collective-permute-done((f32[144,8,128]{2,1,0:T(8,128)S(1)}, f32[144,8,128]{2,1,0:T(8,128)S(1)}, u32[]{:S(2)}, u32[]{:S(2)}) %collective-permute-start.12) | collective-permute-done | bytes 589856 | tf_op jit(solution)/shard_map/ppermute | solution.py:422
  97.5 6.9 %collective-permute-done.10.refs_0_ = f32[144,8,128]{2,1,0:T(8,128)S(1)} collective-permute-done((f32[144,8,128]{2,1,0:T(8,128)S(1)}, f32[144,8,128]{2,1,0:T(8,128)S(1)}, u32[]{:S(2)}, u32[]{:S(2)}) %collective-permute-start.10) | collective-permute-done | bytes 589856 | tf_op jit(solution)/shard_map/ppermute | solution.py:422
  109.5 1.9 %shard_map.99 = f32[144,128]{1,0:T(8,128)S(1)} custom-call(f32[2304,128]{1,0:T(8,128)S(1)} %bitcast.26, f32[1152,128]{1,0:T(8,128)S(1)} %bitcast.29, bf16[96,3072]{1,0:T(8,128)(2,1)S(1)} %get-tuple-element.42.left_top, bf16[96,3072]{1,0:T(8,128)(2,1)S(1)} %get-tuple-element.43.left_rest, s32[4]{0:T(128)S(1)} %pad_add_fusion.place_ref, ...), custom_call_target="tpu_custom_call" | custom-call | flops 1048576 | bytes 8388608 | tf_op jit(solution)/shard_map/pallas_call | solution.py:348
  112.5 2.7 %collective-permute-start.18 = (f32[144,128]{1,0:T(8,128)S(1)}, f32[144,128]{1,0:T(8,128)S(1)}, u32[]{:S(2)}, u32[]{:S(2)}) collective-permute-start(f32[144,128]{1,0:T(8,128)S(1)} %shard_map.99), channel_id=1, source_target_pairs={{0,12},{4,0},{8,4},{12,8},{16,28},{20,16},{24,20},{28,24},{32,44},... | collective-permute-start | bytes 221192 | tf_op jit(solution)/shard_map/ppermute | solution.py:369
  115.1 3.4 %collective-permute-done.16 = f32[144,128]{1,0:T(8,128)S(1)} collective-permute-done((f32[144,128]{1,0:T(8,128)S(1)}, f32[144,128]{1,0:T(8,128)S(1)}, u32[]{:S(2)}, u32[]{:S(2)}) %collective-permute-start.16) | collective-permute-done | bytes 73760 | tf_op jit(solution)/shard_map/ppermute | solution.py:369
  119.1 18.7 %collective-permute-start.19 = (f32[144,128]{1,0:T(8,128)S(1)}, f32[144,128]{1,0:T(8,128)S(1)}, u32[]{:S(2)}, u32[]{:S(2)}) collective-permute-start(f32[144,128]{1,0:T(8,128)S(1)} %add_add_fusion.1), channel_id=1, source_target_pairs={{0,16},{4,20},{8,24},{12,28},{16,0},{20,4},{24,8},{28,12},{32,48},... | collective-permute-start | bytes 221192 | tf_op jit(solution)/shard_map/ppermute | solution.py:369
  137.8 2.4 %collective-permute-done.19 = f32[144,128]{1,0:T(8,128)S(1)} collective-permute-done((f32[144,128]{1,0:T(8,128)S(1)}, f32[144,128]{1,0:T(8,128)S(1)}, u32[]{:S(2)}, u32[]{:S(2)}) %collective-permute-start.19) | collective-permute-done | bytes 73760 | tf_op jit(solution)/shard_map/ppermute | solution.py:369
  140.4 4.0 %collective-permute-start.22 = (f32[144,128]{1,0:T(8,128)S(1)}, f32[144,128]{1,0:T(8,128)S(1)}, u32[]{:S(2)}, u32[]{:S(2)}) collective-permute-start(f32[144,128]{1,0:T(8,128)S(1)} %add.49), channel_id=1, source_target_pairs={{0,96},{4,100},{8,104},{12,108},{16,112},{20,116},{24,120},{28,124... | collective-permute-start | bytes 221192 | tf_op jit(solution)/shard_map/ppermute | solution.py:369
  144.4 3.1 %collective-permute-done.20 = f32[144,128]{1,0:T(8,128)S(1)} collective-permute-done((f32[144,128]{1,0:T(8,128)S(1)}, f32[144,128]{1,0:T(8,128)S(1)}, u32[]{:S(2)}, u32[]{:S(2)}) %collective-permute-start.20) | collective-permute-done | bytes 73760 | tf_op jit(solution)/shard_map/ppermute | solution.py:369
  147.5 3.3 %collective-permute-done.21 = f32[144,128]{1,0:T(8,128)S(1)} collective-permute-done((f32[144,128]{1,0:T(8,128)S(1)}, f32[144,128]{1,0:T(8,128)S(1)}, u32[]{:S(2)}, u32[]{:S(2)}) %collective-permute-start.21) | collective-permute-done | bytes 73760 | tf_op jit(solution)/shard_map/ppermute | solution.py:369
  151.2 5.8 %collective-permute-done.23 = f32[144,128]{1,0:T(8,128)S(1)} collective-permute-done((f32[144,128]{1,0:T(8,128)S(1)}, f32[144,128]{1,0:T(8,128)S(1)}, u32[]{:S(2)}, u32[]{:S(2)}) %collective-permute-start.23) | collective-permute-done | bytes 73760 | tf_op jit(solution)/shard_map/ppermute | solution.py:369
  (83 shorter events, 28.0 us)
Async XLA Ops:
  3.3 6.0 %copy-start.9 = (s32[2,8,128]{2,1,0:T(8,128)S(1)}, s32[2,8,128]{2,1,0:T(8,128)}, u32[]{:S(2)}) copy-start(s32[2,8,128]{2,1,0:T(8,128)} %support_ref.1) | copy-start | bytes 24580
  3.3 6.0 %copy-start.13 = (f32[2,8,128]{2,1,0:T(8,128)S(1)}, f32[2,8,128]{2,1,0:T(8,128)}, u32[]{:S(2)}) copy-start(f32[2,8,128]{2,1,0:T(8,128)} %param.7) | copy-start | bytes 24580
  3.3 6.0 %copy-start.11 = (f32[2,8,128]{2,1,0:T(8,128)S(1)}, f32[2,8,128]{2,1,0:T(8,128)}, u32[]{:S(2)}) copy-start(f32[2,8,128]{2,1,0:T(8,128)} %modulus_ref.1) | copy-start | bytes 24580
  3.3 6.1 %copy-start.12 = (f32[24,24]{1,0:T(8,128)S(1)}, f32[24,24]{1,0:T(8,128)}, u32[]{:S(2)}) copy-start(f32[24,24]{1,0:T(8,128)} %stiff_ref.1) | copy-start | bytes 6916
  3.5 5.9 %collective-permute-start.1 = (f32[1,8,128]{2,1,0:T(8,128)S(1)}, f32[1,8,128]{2,1,0:T(8,128)S(1)}, u32[]{:S(2)}, u32[]{:S(2)}) collective-permute-start(f32[1,8,128]{2,1,0:T(8,128)S(1)} %get-tuple-element.26), channel_id=1, source_target_pairs={{0,4},{1,5},{2,6},{3,7},{4,8},{5,9},{6,10},{7,11},{8,12},{9,13},{1... | collective-permute-start | bytes 12296 | tf_op jit(solution)/shard_map/ppermute | solution.py:389
  5.1 16.9 %collective-permute-start.3 = (f32[144,8,128]{2,1,0:T(8,128)S(1)}, f32[144,8,128]{2,1,0:T(8,128)S(1)}, u32[]{:S(2)}, u32[]{:S(2)}) collective-permute-start(f32[144,8,128]{2,1,0:T(8,128)S(1)} %get-tuple-element.25.refs_1_.refs_5_), channel_id=1, source_target_pairs={{0,4},{1,5},{2,6},{3,7},{4,8},{5,9},{6,10},{7,11},{8,12},{9,13},{1... | collective-permute-start | bytes 1769480 | tf_op jit(solution)/shard_map/ppermute | solution.py:408
  6.7 17.6 %collective-permute-start = (f32[144,8,128]{2,1,0:T(8,128)S(1)}, f32[144,8,128]{2,1,0:T(8,128)S(1)}, u32[]{:S(2)}, u32[]{:S(2)}) collective-permute-start(f32[144,8,128]{2,1,0:T(8,128)S(1)} %get-tuple-element.24.refs_0_.refs_4_), channel_id=1, source_target_pairs={{4,0},{5,1},{6,2},{7,3},{8,4},{9,5},{10,6},{11,7},{12,8},{13,9},{1... | collective-permute-start | bytes 1769480 | tf_op jit(solution)/shard_map/ppermute | solution.py:409
  23.7 14.0 %collective-permute-start.5 = (f32[144,8,128]{2,1,0:T(8,128)S(1)}, f32[144,8,128]{2,1,0:T(8,128)S(1)}, u32[]{:S(2)}, u32[]{:S(2)}) collective-permute-start(f32[144,8,128]{2,1,0:T(8,128)S(1)} %shard_map.80.refs_0_.refs_4_), channel_id=1, source_target_pairs={{4,0},{5,1},{6,2},{7,3},{8,4},{9,5},{10,6},{11,7},{12,8},{13,9},{1... | collective-permute-start | bytes 1769480 | tf_op jit(solution)/shard_map/ppermute | solution.py:416
  26.0 15.8 %collective-permute-start.2 = (f32[144,8,128]{2,1,0:T(8,128)S(1)}, f32[144,8,128]{2,1,0:T(8,128)S(1)}, u32[]{:S(2)}, u32[]{:S(2)}) collective-permute-start(f32[144,8,128]{2,1,0:T(8,128)S(1)} %shard_map.79.refs_1_.refs_5_), channel_id=1, source_target_pairs={{0,4},{1,5},{2,6},{3,7},{4,8},{5,9},{6,10},{7,11},{8,12},{9,13},{1... | collective-permute-start | bytes 1769480 | tf_op jit(solution)/shard_map/ppermute | solution.py:414
  39.4 15.1 %collective-permute-start.7 = (f32[144,8,128]{2,1,0:T(8,128)S(1)}, f32[144,8,128]{2,1,0:T(8,128)S(1)}, u32[]{:S(2)}, u32[]{:S(2)}) collective-permute-start(f32[144,8,128]{2,1,0:T(8,128)S(1)} %shard_map.83.refs_1_.refs_5_), channel_id=1, source_target_pairs={{0,4},{1,5},{2,6},{3,7},{4,8},{5,9},{6,10},{7,11},{8,12},{9,13},{1... | collective-permute-start | bytes 1769480 | tf_op jit(solution)/shard_map/ppermute | solution.py:414
  43.5 15.0 %collective-permute-start.4 = (f32[144,8,128]{2,1,0:T(8,128)S(1)}, f32[144,8,128]{2,1,0:T(8,128)S(1)}, u32[]{:S(2)}, u32[]{:S(2)}) collective-permute-start(f32[144,8,128]{2,1,0:T(8,128)S(1)} %shard_map.82.refs_0_.refs_4_), channel_id=1, source_target_pairs={{4,0},{5,1},{6,2},{7,3},{8,4},{9,5},{10,6},{11,7},{12,8},{13,9},{1... | collective-permute-start | bytes 1769480 | tf_op jit(solution)/shard_map/ppermute | solution.py:416
  56.2 12.6 %collective-permute-start.8 = (f32[144,8,128]{2,1,0:T(8,128)S(1)}, f32[144,8,128]{2,1,0:T(8,128)S(1)}, u32[]{:S(2)}, u32[]{:S(2)}) collective-permute-start(f32[144,8,128]{2,1,0:T(8,128)S(1)} %shard_map.86.refs_0_), channel_id=1, source_target_pairs={{4,0},{5,1},{6,2},{7,3},{8,4},{9,5},{10,6},{11,7},{12,8},{13,9},{1... | collective-permute-start | bytes 1769480 | tf_op jit(solution)/shard_map/ppermute | solution.py:416
  60.2 17.5 %collective-permute-start.6 = (f32[144,8,128]{2,1,0:T(8,128)S(1)}, f32[144,8,128]{2,1,0:T(8,128)S(1)}, u32[]{:S(2)}, u32[]{:S(2)}) collective-permute-start(f32[144,8,128]{2,1,0:T(8,128)S(1)} %shard_map.85.refs_1_), channel_id=1, source_target_pairs={{0,4},{1,5},{2,6},{3,7},{4,8},{5,9},{6,10},{7,11},{8,12},{9,13},{1... | collective-permute-start | bytes 1769480 | tf_op jit(solution)/shard_map/ppermute | solution.py:414
  70.6 19.8 %collective-permute-start.13 = (f32[144,8,128]{2,1,0:T(8,128)S(1)}, f32[144,8,128]{2,1,0:T(8,128)S(1)}, u32[]{:S(2)}, u32[]{:S(2)}) collective-permute-start(f32[144,8,128]{2,1,0:T(8,128)S(1)} %shard_map.89.high_ref.refs_1_), channel_id=1, source_target_pairs={{0,4},{1,5},{2,6},{3,7},{4,8},{5,9},{6,10},{7,11},{8,12},{9,13},{1... | collective-permute-start | bytes 1769480 | tf_op jit(solution)/shard_map/ppermute | solution.py:414
  79.4 12.6 %collective-permute-start.11 = (f32[144,8,128]{2,1,0:T(8,128)S(1)}, f32[144,8,128]{2,1,0:T(8,128)S(1)}, u32[]{:S(2)}, u32[]{:S(2)}) collective-permute-start(f32[144,8,128]{2,1,0:T(8,128)S(1)} %shard_map.88.low_ref.refs_0_), channel_id=1, source_target_pairs={{4,0},{5,1},{6,2},{7,3},{8,4},{9,5},{10,6},{11,7},{12,8},{13,9},{1... | collective-permute-start | bytes 1769480 | tf_op jit(solution)/shard_map/ppermute | solution.py:416
  81.5 16.0 %collective-permute-start.12 = (f32[144,8,128]{2,1,0:T(8,128)S(1)}, f32[144,8,128]{2,1,0:T(8,128)S(1)}, u32[]{:S(2)}, u32[]{:S(2)}) collective-permute-start(f32[144,8,128]{2,1,0:T(8,128)S(1)} %shard_map.89.high_ref.refs_1_), channel_id=1, source_target_pairs={{0,2},{2,0},{1,3},{3,1},{4,6},{6,4},{5,7},{7,5},{8,10},{10,8},{9,1... | collective-permute-start | bytes 1769480 | tf_op jit(solution)/shard_map/ppermute | solution.py:422
  82.6 23.0 %collective-permute-start.9 = (f32[144,2,8,128]{3,2,1,0:T(8,128)}, f32[144,2,8,128]{3,2,1,0:T(8,128)S(1)}, u32[]{:S(2)}, u32[]{:S(2)}) collective-permute-start(f32[144,2,8,128]{3,2,1,0:T(8,128)} %shard_map.90.refs_3_), channel_id=1, source_target_pairs={{0,1},{1,0},{2,3},{3,2},{4,5},{5,4},{6,7},{7,6},{8,9},{9,8},{10,11... | collective-permute-start | bytes 3538952 | tf_op jit(solution)/shard_map/ppermute | solution.py:429
  82.6 21.7 %collective-permute-start.10 = (f32[144,8,128]{2,1,0:T(8,128)S(1)}, f32[144,8,128]{2,1,0:T(8,128)S(1)}, u32[]{:S(2)}, u32[]{:S(2)}) collective-permute-start(f32[144,8,128]{2,1,0:T(8,128)S(1)} %shard_map.88.low_ref.refs_0_), channel_id=1, source_target_pairs={{0,2},{2,0},{1,3},{3,1},{4,6},{6,4},{5,7},{7,5},{8,10},{10,8},{9,1... | collective-permute-start | bytes 1769480 | tf_op jit(solution)/shard_map/ppermute | solution.py:422
  92.1 5.4 %copy-start = (f32[144,2,8,128]{3,2,1,0:T(8,128)S(1)}, f32[144,2,8,128]{3,2,1,0:T(8,128)}, u32[]{:S(2)}) copy-start(f32[144,2,8,128]{3,2,1,0:T(8,128)} %shard_map.90.refs_3_) | copy-start | bytes 3538948
  97.5 8.1 %collective-permute-start.14 = (f32[144,8,128]{2,1,0:T(8,128)S(1)}, f32[144,8,128]{2,1,0:T(8,128)S(1)}, u32[]{:S(2)}, u32[]{:S(2)}) collective-permute-start(f32[144,8,128]{2,1,0:T(8,128)S(1)} %shard_map.94), channel_id=1, source_target_pairs={{0,1},{1,0},{2,3},{3,2},{4,5},{5,4},{6,7},{7,6},{8,9},{9,8},{10,11... | collective-permute-start | bytes 1769480 | tf_op jit(solution)/shard_map/ppermute | solution.py:434
  107.4 2.0 %copy-start.2 = (f32[144,2,8,128]{3,2,1,0:T(8,128)S(1)}, f32[144,2,8,128]{3,2,1,0:T(8,128)}, u32[]{:S(2)}) copy-start(f32[144,2,8,128]{3,2,1,0:T(8,128)} %copy-done.1) | copy-start | bytes 3538948
  107.4 2.0 %collective-permute-start.15 = (f32[144,8,128]{2,1,0:T(8,128)S(1)}, f32[144,8,128]{2,1,0:T(8,128)S(1)}, u32[]{:S(2)}, u32[]{:S(2)}) collective-permute-start(f32[144,8,128]{2,1,0:T(8,128)S(1)} %shard_map.97), channel_id=1, source_target_pairs={{0,1},{1,0},{2,3},{3,2},{4,5},{5,4},{6,7},{7,6},{8,9},{9,8},{10,11... | collective-permute-start | bytes 1769480 | tf_op jit(solution)/shard_map/ppermute | solution.py:434
  107.4 2.0 %copy-start.5 = (f32[96,96]{1,0:T(8,128)S(1)}, f32[96,96]{1,0:T(8,128)}, u32[]{:S(2)}) copy-start(f32[96,96]{1,0:T(8,128)} %copy-done.4) | copy-start | bytes 110596
  107.5 2.0 %copy-start.7 = (f32[96,96]{1,0:T(8,128)S(1)}, f32[96,96]{1,0:T(8,128)}, u32[]{:S(2)}) copy-start(f32[96,96]{1,0:T(8,128)} %copy-done.6) | copy-start | bytes 110596
  111.3 7.2 %collective-permute-start.16 = (f32[144,128]{1,0:T(8,128)S(1)}, f32[144,128]{1,0:T(8,128)S(1)}, u32[]{:S(2)}, u32[]{:S(2)}) collective-permute-start(f32[144,128]{1,0:T(8,128)S(1)} %shard_map.99), channel_id=1, source_target_pairs={{0,4},{4,8},{8,12},{12,0},{16,20},{20,24},{24,28},{28,16},{32,36},... | collective-permute-start | bytes 221192 | tf_op jit(solution)/shard_map/ppermute | solution.py:369
  112.4 6.2 %collective-permute-start.17 = (f32[144,128]{1,0:T(8,128)S(1)}, f32[144,128]{1,0:T(8,128)S(1)}, u32[]{:S(2)}, u32[]{:S(2)}) collective-permute-start(f32[144,128]{1,0:T(8,128)S(1)} %shard_map.99), channel_id=1, source_target_pairs={{0,8},{4,12},{8,0},{12,4},{16,24},{20,28},{24,16},{28,20},{32,40},... | collective-permute-start | bytes 221192 | tf_op jit(solution)/shard_map/ppermute | solution.py:369
  112.5 6.6 %collective-permute-start.18 = (f32[144,128]{1,0:T(8,128)S(1)}, f32[144,128]{1,0:T(8,128)S(1)}, u32[]{:S(2)}, u32[]{:S(2)}) collective-permute-start(f32[144,128]{1,0:T(8,128)S(1)} %shard_map.99), channel_id=1, source_target_pairs={{0,12},{4,0},{8,4},{12,8},{16,28},{20,16},{24,20},{28,24},{32,44},... | collective-permute-start | bytes 221192 | tf_op jit(solution)/shard_map/ppermute | solution.py:369
  119.1 21.1 %collective-permute-start.19 = (f32[144,128]{1,0:T(8,128)S(1)}, f32[144,128]{1,0:T(8,128)S(1)}, u32[]{:S(2)}, u32[]{:S(2)}) collective-permute-start(f32[144,128]{1,0:T(8,128)S(1)} %add_add_fusion.1), channel_id=1, source_target_pairs={{0,16},{4,20},{8,24},{12,28},{16,0},{20,4},{24,8},{28,12},{32,48},... | collective-permute-start | bytes 221192 | tf_op jit(solution)/shard_map/ppermute | solution.py:369
  140.2 7.3 %collective-permute-start.20 = (f32[144,128]{1,0:T(8,128)S(1)}, f32[144,128]{1,0:T(8,128)S(1)}, u32[]{:S(2)}, u32[]{:S(2)}) collective-permute-start(f32[144,128]{1,0:T(8,128)S(1)} %add.49), channel_id=1, source_target_pairs={{0,32},{4,36},{8,40},{12,44},{16,48},{20,52},{24,56},{28,60},{32,6... | collective-permute-start | bytes 221192 | tf_op jit(solution)/shard_map/ppermute | solution.py:369
  140.3 10.4 %collective-permute-start.21 = (f32[144,128]{1,0:T(8,128)S(1)}, f32[144,128]{1,0:T(8,128)S(1)}, u32[]{:S(2)}, u32[]{:S(2)}) collective-permute-start(f32[144,128]{1,0:T(8,128)S(1)} %add.49), channel_id=1, source_target_pairs={{0,64},{4,68},{8,72},{12,76},{16,80},{20,84},{24,88},{28,92},{32,9... | collective-permute-start | bytes 221192 | tf_op jit(solution)/shard_map/ppermute | solution.py:369
  140.4 10.7 %collective-permute-start.22 = (f32[144,128]{1,0:T(8,128)S(1)}, f32[144,128]{1,0:T(8,128)S(1)}, u32[]{:S(2)}, u32[]{:S(2)}) collective-permute-start(f32[144,128]{1,0:T(8,128)S(1)} %add.49), channel_id=1, source_target_pairs={{0,96},{4,100},{8,104},{12,108},{16,112},{20,116},{24,120},{28,124... | collective-permute-start | bytes 221192 | tf_op jit(solution)/shard_map/ppermute | solution.py:369
  151.1 5.9 %collective-permute-start.23 = (f32[144,128]{1,0:T(8,128)S(1)}, f32[144,128]{1,0:T(8,128)S(1)}, u32[]{:S(2)}, u32[]{:S(2)}) collective-permute-start(f32[144,128]{1,0:T(8,128)S(1)} %add_add_fusion), channel_id=1, source_target_pairs={{0,128},{4,132},{8,136},{12,140},{16,144},{20,148},{24,152},{28,15... | collective-permute-start | bytes 221192 | tf_op jit(solution)/shard_map/ppermute | solution.py:369
  (6 other events, 5.7 us)

commit v5 on v4

--- a/solution.py
+++ b/solution.py
@@ -95,27 +95,43 @@
     return acc[0] + rolled(acc[1], -1, 0) + rolled(acc[2], 1, 0)
 
 
-def start_kernel(field_ref, support_ref, modulus_ref, low_ref, high_ref, edge_ref):
-    free = [(1 - support_ref[p]).astype(jnp.float32) for p in range(2)]
-    low_ref[...] = field_ref[:, 0] * free[0]
-    high_ref[...] = field_ref[:, 1] * free[1]
-    edge_ref[0] = modulus_ref[1]
+def start_kernel(field_ref, support_ref, modulus_ref, low_ref, high_ref, edge_ref, field, support, sems):
+    parts = sems.shape[0] - 2
+    tile = field.shape[0] // parts
+    copies = [
+        pltpu.make_async_copy(support_ref, support, sems.at[parts]),
+        pltpu.make_async_copy(modulus_ref.at[pl.ds(1, 1)], edge_ref, sems.at[parts + 1]),
+    ]
+    for i in range(parts):
+        rows = pl.ds(i * tile, tile)
+        copies.append(pltpu.make_async_copy(field_ref.at[rows], field.at[rows], sems.at[i]))
+    for copy in copies:
+        copy.start()
+    copies[0].wait()
+    free = [(1 - support[p]).astype(jnp.float32) for p in range(2)]
+    for i in range(parts):
+        copies[2 + i].wait()
+        rows = pl.ds(i * tile, tile)
+        low_ref[rows] = field[rows, 0] * free[0]
+        high_ref[rows] = field[rows, 1] * free[1]
+    copies[1].wait()
 
 
 def start(field, support, modulus):
     count, planes, rows, depth = field.shape
-    tile = count // 4
-    plane = pl.BlockSpec((tile, rows, depth), lambda i: (i, 0, 0))
-    edge = pl.BlockSpec((1, rows, depth), lambda i: (0, 0, 0))
-    both = pl.BlockSpec((planes, rows, depth), lambda i: (0, 0, 0))
+    parts = 4
     return pl.pallas_call(
         start_kernel,
-        grid=(4,),
-        in_specs=[pl.BlockSpec((tile, planes, rows, depth), lambda i: (i, 0, 0, 0)), both, both],
-        out_specs=[plane, plane, edge],
+        in_specs=[ANYWHERE] * 3,
+        out_specs=[IN_VMEM] * 3,
         out_shape=[spec((count, rows, depth))] * 2 + [spec((1, rows, depth))],
+        scratch_shapes=[
+            pltpu.VMEM(field.shape, jnp.float32),
+            pltpu.VMEM(support.shape, support.dtype),
+            pltpu.SemaphoreType.DMA((parts + 2,)),
+        ],
         cost_estimate=cost(2 * field.size, 8 * field.size),
-        compiler_params=compiled(),
+        compiler_params=pltpu.CompilerParams(vmem_limit_bytes=60 * 1024 * 1024),
     )(field, support, modulus)
 
 
@@ -438,7 +454,7 @@
         nears.append(near)
         last = (factor, place, nears, fars) if p == 0 else None
         fars.append(far_gram(p, by_core, by_both, left, modes, last))
-        after = (near, fars[0])
+        after = (near,)
     grams = fars[-1]
     for groups in ((16, 4, 1), (8, 2, 4), (2, 4, 8), (1, 2, 32)):
         grams = total_over(grams, SLAB, groups)

time: 159 us -> 162 us (1.019)
  Pallas kernels: 54.4 us -> 58.7 us
  waiting for transfers between devices: 54.5 us -> 52.4 us
    pallas_call x1, Pallas kernels: 0.16 us -> 2.35 us  [start(): pl.pallas_call(start_kernel, in_specs=[ANYWHERE] * 3, out_specs=[IN_VMEM]...]
    pallas_call x2, Pallas kernels: 3.02 us -> 5.19 us  [far_gram(): pl.pallas_call(kernel, in_specs=specs, out_specs=IN_VMEM, out_shape=spec(...]
    ppermute x1, waiting for transfers between devices: 5.51 us -> 3.5 us  [body(): lower = lax.ppermute(current[1], everywhere, up)]
    unnamed x28 -> x26, local copies, waits for them, and re-layouts: 3.29 us -> 3.59 us
  transfers between devices with their start and end apart: 24 -> 24, of which waited for: 16 -> 15; matrix products, arithmetic and copies ran while one was open for 0% -> 0% of each run, Pallas kernels for 32% -> 33%
where the time goes in v5:
time: 162 us; the launch traced here: 160 us
  Pallas kernels  58.7 us (36%)
  waiting for transfers between devices  52.4 us (32%)
  starting transfers between devices  43.4 us (27%)
  local copies, waits for them, and re-layouts  3.68 us (2%)
    pallas_call x5, Pallas kernels, own_part(): pl.pallas_call(partial(own_kernel, shift, count), in_specs=[IN_VMEM] * le...  29.3 us
    ppermute x8, starting transfers between devices, total_over(): parts.append(lax.ppermute(x, axes, pairs))  26.5 us
    ppermute x8, waiting for transfers between devices, total_over(): parts.append(lax.ppermute(x, axes, pairs))  19.3 us
    pallas_call x10, Pallas kernels, with_halo(): pl.pallas_call(partial(halo_kernel, p), in_specs=[IN_VMEM] * 4, out_specs...  17 us
    ppermute x4, waiting for transfers between devices, body(): below = lax.ppermute(high, everywhere, up)  12.1 us
    ppermute x2, waiting for transfers between devices, body(): by_x[p] = lax.ppermute(current[p], 'xl', swap)  10.6 us
    ppermute x4, starting transfers between devices, body(): upper = lax.ppermute(low, everywhere, down)  6.77 us
    ppermute x4, waiting for transfers between devices, body(): upper = lax.ppermute(low, everywhere, down)  6.75 us
  transfers between devices with their start and end apart: 24, of which 15 were waited for; matrix products, arithmetic and copies ran while one was open for 0% of the time, Pallas kernels for 33%

profile of v5, /device:TPU:32, one launch (start us, length us, event | category | flops | bytes accessed | tf_op | source)
XLA Modules:
  0.0 160.0 jit_solution(9345854232890857286)
XLA Ops:
  0.7 2.4 %shard_map.76 = (f32[144,8,128]{2,1,0:T(8,128)}, f32[144,8,128]{2,1,0:T(8,128)}, f32[1,8,128]{2,1,0:T(8,128)}) custom-call(f32[144,2,8,128]{3,2,1,0:T(8,128)} %bitcast.27, s32[2,8,128]{2,1,0:T(8,128)} %support_ref.1, f32[2,8,128]{2,1,0:T(8,128)} %modulus_ref.1), custom_call_target="tpu_custom_call" | custom-call | flops 589824 | bytes 2359296 | tf_op jit(solution)/shard_map/pallas_call | solution.py:123
  6.3 2.6 %collective-permute-start = (f32[144,8,128]{2,1,0:T(8,128)}, f32[144,8,128]{2,1,0:T(8,128)S(1)}, u32[]{:S(2)}, u32[]{:S(2)}) collective-permute-start(f32[144,8,128]{2,1,0:T(8,128)} %get-tuple-element.24.refs_0_.refs_4_), channel_id=1, source_target_pairs={{4,0},{5,1},{6,2},{7,3},{8,4},{9,5},{10,6},{11,7},{12,8},{13,9},{1... | collective-permute-start | bytes 1769480 | tf_op jit(solution)/shard_map/ppermute | solution.py:425
  12.5 5.8 %shard_map.78 = (f32[144,8,128]{2,1,0:T(8,128)S(1)}, f32[144,8,128]{2,1,0:T(8,128)S(1)}) custom-call(f32[144,8,128]{2,1,0:T(8,128)S(1)} %copy-done.1, f32[144,8,128]{2,1,0:T(8,128)S(1)} %copy-done.3, f32[324,8,128]{2,1,0:T(8,128)S(1)} %get-tuple-element.27.refs_2_, f32[2,8,128]{2,1,0:T(8,128)S(1)} %get-tuple-element.46.refs_3_.scale_ref), custom_call_target="tpu_custom_call" | custom-call | flops 31850496 | bytes 16777216 | tf_op jit(solution)/shard_map/pallas_call | solution.py:178
  18.3 3.5 %collective-permute-done.3.halo_ref = f32[144,8,128]{2,1,0:T(8,128)S(1)} collective-permute-done((f32[144,8,128]{2,1,0:T(8,128)}, f32[144,8,128]{2,1,0:T(8,128)S(1)}, u32[]{:S(2)}, u32[]{:S(2)}) %collective-permute-start.3) | collective-permute-done | bytes 589856 | tf_op jit(solution)/shard_map/ppermute | solution.py:424
  27.4 5.9 %shard_map.81 = (f32[144,8,128]{2,1,0:T(8,128)S(1)}, f32[144,8,128]{2,1,0:T(8,128)S(1)}) custom-call(f32[144,8,128]{2,1,0:T(8,128)S(1)} %shard_map.80.refs_0_.refs_4_, f32[144,8,128]{2,1,0:T(8,128)S(1)} %shard_map.79.refs_1_.refs_5_, f32[324,8,128]{2,1,0:T(8,128)S(1)} %get-tuple-element.27.refs_2_, f32[2,8,128]{2,1,0:T(8,128)S(1)} %get-tuple-element.45.refs_3_.scale_ref, ...), custom_call_target="tpu_custom_call" | custom-call | flops 31850496 | bytes 16777216 | tf_op jit(solution)/shard_map/pallas_call | solution.py:178
  33.3 4.1 %collective-permute-done.5.halo_ref = f32[144,8,128]{2,1,0:T(8,128)S(1)} collective-permute-done((f32[144,8,128]{2,1,0:T(8,128)S(1)}, f32[144,8,128]{2,1,0:T(8,128)S(1)}, u32[]{:S(2)}, u32[]{:S(2)}) %collective-permute-start.5) | collective-permute-done | bytes 589856 | tf_op jit(solution)/shard_map/ppermute | solution.py:432
  37.5 1.7 %shard_map.83.refs_1_.refs_5_ = f32[144,8,128]{2,1,0:T(8,128)S(1)} custom-call(f32[144,8,128]{2,1,0:T(8,128)S(1)} %collective-permute-done.5.halo_ref, f32[144,8,128]{2,1,0:T(8,128)S(1)} %get-tuple-element.32.part_ref, f32[162,8,128]{2,1,0:T(8,128)S(1)} %get-tuple-element.29.coef_ref, f32[2,8,128]{2,1,0:T(8,128)S(1)} %get-tuple-element.45.refs_3_.scale_ref), custom_call_target="tpu_custom_call" | custom-call | flops 7962624 | bytes 5242880 | tf_op jit(solution)/shard_map/pallas_call | solution.py:213
  39.3 2.3 %collective-permute-done.2.halo_ref = f32[144,8,128]{2,1,0:T(8,128)S(1)} collective-permute-done((f32[144,8,128]{2,1,0:T(8,128)S(1)}, f32[144,8,128]{2,1,0:T(8,128)S(1)}, u32[]{:S(2)}, u32[]{:S(2)}) %collective-permute-start.2) | collective-permute-done | bytes 589856 | tf_op jit(solution)/shard_map/ppermute | solution.py:430
  43.2 1.9 %collective-permute-start.4 = (f32[144,8,128]{2,1,0:T(8,128)S(1)}, f32[144,8,128]{2,1,0:T(8,128)S(1)}, u32[]{:S(2)}, u32[]{:S(2)}) collective-permute-start(f32[144,8,128]{2,1,0:T(8,128)S(1)} %shard_map.82.refs_0_.refs_4_), channel_id=1, source_target_pairs={{4,0},{5,1},{6,2},{7,3},{8,4},{9,5},{10,6},{11,7},{12,8},{13,9},{1... | collective-permute-start | bytes 1769480 | tf_op jit(solution)/shard_map/ppermute | solution.py:432
  45.2 5.9 %shard_map.84 = (f32[144,8,128]{2,1,0:T(8,128)S(1)}, f32[144,8,128]{2,1,0:T(8,128)S(1)}) custom-call(f32[144,8,128]{2,1,0:T(8,128)S(1)} %shard_map.82.refs_0_.refs_4_, f32[144,8,128]{2,1,0:T(8,128)S(1)} %shard_map.83.refs_1_.refs_5_, f32[324,8,128]{2,1,0:T(8,128)S(1)} %get-tuple-element.27.refs_2_, f32[2,8,128]{2,1,0:T(8,128)S(1)} %get-tuple-element.45.refs_3_.scale_ref, ...), custom_call_target="tpu_custom_call" | custom-call | flops 31850496 | bytes 16777216 | tf_op jit(solution)/shard_map/pallas_call | solution.py:178
  51.1 3.2 %collective-permute-done.7.halo_ref = f32[144,8,128]{2,1,0:T(8,128)S(1)} collective-permute-done((f32[144,8,128]{2,1,0:T(8,128)S(1)}, f32[144,8,128]{2,1,0:T(8,128)S(1)}, u32[]{:S(2)}, u32[]{:S(2)}) %collective-permute-start.7) | collective-permute-done | bytes 589856 | tf_op jit(solution)/shard_map/ppermute | solution.py:430
  56.0 2.2 %collective-permute-start.8 = (f32[144,8,128]{2,1,0:T(8,128)S(1)}, f32[144,8,128]{2,1,0:T(8,128)S(1)}, u32[]{:S(2)}, u32[]{:S(2)}) collective-permute-start(f32[144,8,128]{2,1,0:T(8,128)S(1)} %shard_map.86.refs_0_), channel_id=1, source_target_pairs={{4,0},{5,1},{6,2},{7,3},{8,4},{9,5},{10,6},{11,7},{12,8},{13,9},{1... | collective-permute-start | bytes 1769480 | tf_op jit(solution)/shard_map/ppermute | solution.py:432
  58.2 1.7 %shard_map.85.refs_1_ = f32[144,8,128]{2,1,0:T(8,128)S(1)} custom-call(f32[144,8,128]{2,1,0:T(8,128)S(1)} %collective-permute-done.4.halo_ref, f32[144,8,128]{2,1,0:T(8,128)S(1)} %get-tuple-element.33.part_ref, f32[162,8,128]{2,1,0:T(8,128)S(1)} %get-tuple-element.29.coef_ref, f32[2,8,128]{2,1,0:T(8,128)S(1)} %get-tuple-element.45.refs_3_.scale_ref), custom_call_target="tpu_custom_call" | custom-call | flops 7962624 | bytes 5242880 | tf_op jit(solution)/shard_map/pallas_call | solution.py:213
  60.0 5.9 %shard_map.87 = (f32[144,8,128]{2,1,0:T(8,128)S(1)}, f32[144,8,128]{2,1,0:T(8,128)S(1)}) custom-call(f32[144,8,128]{2,1,0:T(8,128)S(1)} %shard_map.86.refs_0_, f32[144,8,128]{2,1,0:T(8,128)S(1)} %shard_map.85.refs_1_, f32[324,8,128]{2,1,0:T(8,128)S(1)} %get-tuple-element.27.refs_2_, f32[2,8,128]{2,1,0:T(8,128)S(1)} %get-tuple-element.45.refs_3_.scale_ref, ...), custom_call_target="tpu_custom_call" | custom-call | flops 31850496 | bytes 16777216 | tf_op jit(solution)/shard_map/pallas_call | solution.py:178
  66.0 2.6 %collective-permute-done.8.halo_ref = f32[144,8,128]{2,1,0:T(8,128)S(1)} collective-permute-done((f32[144,8,128]{2,1,0:T(8,128)S(1)}, f32[144,8,128]{2,1,0:T(8,128)S(1)}, u32[]{:S(2)}, u32[]{:S(2)}) %collective-permute-start.8) | collective-permute-done | bytes 589856 | tf_op jit(solution)/shard_map/ppermute | solution.py:432
  68.6 1.7 %shard_map.89.high_ref.refs_1_ = f32[144,8,128]{2,1,0:T(8,128)S(1)} custom-call(f32[144,8,128]{2,1,0:T(8,128)S(1)} %collective-permute-done.8.halo_ref, f32[144,8,128]{2,1,0:T(8,128)S(1)} %get-tuple-element.36.part_ref, f32[162,8,128]{2,1,0:T(8,128)S(1)} %get-tuple-element.29.coef_ref, f32[2,8,128]{2,1,0:T(8,128)S(1)} %get-tuple-element.45.refs_3_.scale_ref), custom_call_target="tpu_custom_call" | custom-call | flops 7962624 | bytes 5242880 | tf_op jit(solution)/shard_map/pallas_call | solution.py:213
  70.8 6.7 %collective-permute-done.6.halo_ref = f32[144,8,128]{2,1,0:T(8,128)S(1)} collective-permute-done((f32[144,8,128]{2,1,0:T(8,128)S(1)}, f32[144,8,128]{2,1,0:T(8,128)S(1)}, u32[]{:S(2)}, u32[]{:S(2)}) %collective-permute-start.6) | collective-permute-done | bytes 589856 | tf_op jit(solution)/shard_map/ppermute | solution.py:430
  79.2 2.1 %collective-permute-start.11 = (f32[144,8,128]{2,1,0:T(8,128)S(1)}, f32[144,8,128]{2,1,0:T(8,128)S(1)}, u32[]{:S(2)}, u32[]{:S(2)}) collective-permute-start(f32[144,8,128]{2,1,0:T(8,128)S(1)} %shard_map.88.low_ref.refs_0_), channel_id=1, source_target_pairs={{4,0},{5,1},{6,2},{7,3},{8,4},{9,5},{10,6},{11,7},{12,8},{13,9},{1... | collective-permute-start | bytes 1769480 | tf_op jit(solution)/shard_map/ppermute | solution.py:432
  81.3 2.0 %collective-permute-start.10 = (f32[144,8,128]{2,1,0:T(8,128)S(1)}, f32[144,8,128]{2,1,0:T(8,128)S(1)}, u32[]{:S(2)}, u32[]{:S(2)}) collective-permute-start(f32[144,8,128]{2,1,0:T(8,128)S(1)} %shard_map.88.low_ref.refs_0_), channel_id=1, source_target_pairs={{0,2},{2,0},{1,3},{3,1},{4,6},{6,4},{5,7},{7,5},{8,10},{10,8},{9,1... | collective-permute-start | bytes 1769480 | tf_op jit(solution)/shard_map/ppermute | solution.py:438
  84.4 5.7 %shard_map.91 = (f32[144,8,128]{2,1,0:T(8,128)S(1)}, f32[144,8,128]{2,1,0:T(8,128)S(1)}) custom-call(f32[144,8,128]{2,1,0:T(8,128)S(1)} %shard_map.88.low_ref.refs_0_, f32[144,8,128]{2,1,0:T(8,128)S(1)} %shard_map.89.high_ref.refs_1_, f32[324,8,128]{2,1,0:T(8,128)S(1)} %get-tuple-element.27.refs_2_, f32[2,8,128]{2,1,0:T(8,128)S(1)} %subtract_convert_fusion.refs_3_.scale_ref), custom_call_target="tpu_custom_call" | custom-call | flops 31850496 | bytes 16777216 | tf_op jit(solution)/shard_map/pallas_call | solution.py:178
  90.1 1.7 %shard_map.93.refs_1_ = f32[144,8,128]{2,1,0:T(8,128)S(1)} custom-call(f32[144,8,128]{2,1,0:T(8,128)S(1)} %collective-permute-done.13.halo_ref, f32[144,8,128]{2,1,0:T(8,128)S(1)} %get-tuple-element.38.part_ref, f32[162,8,128]{2,1,0:T(8,128)S(1)} %get-tuple-element.29.coef_ref, f32[2,8,128]{2,1,0:T(8,128)S(1)} %subtract_convert_fusion.refs_3_.scale_ref), custom_call_target="tpu_custom_call" | custom-call | flops 7962624 | bytes 5242880 | tf_op jit(solution)/shard_map/pallas_call | solution.py:213
  93.6 4.0 %collective-permute-done.12.refs_0_ = f32[144,8,128]{2,1,0:T(8,128)S(1)} collective-permute-done((f32[144,8,128]{2,1,0:T(8,128)S(1)}, f32[144,8,128]{2,1,0:T(8,128)S(1)}, u32[]{:S(2)}, u32[]{:S(2)}) %collective-permute-start.12) | collective-permute-done | bytes 589856 | tf_op jit(solution)/shard_map/ppermute | solution.py:438
  97.5 6.6 %collective-permute-done.10.refs_0_ = f32[144,8,128]{2,1,0:T(8,128)S(1)} collective-permute-done((f32[144,8,128]{2,1,0:T(8,128)S(1)}, f32[144,8,128]{2,1,0:T(8,128)S(1)}, u32[]{:S(2)}, u32[]{:S(2)}) %collective-permute-start.10) | collective-permute-done | bytes 589856 | tf_op jit(solution)/shard_map/ppermute | solution.py:438
  108.2 2.4 %shard_map.98.refs_2_ = f32[96,96]{1,0:T(8,128)S(1)} custom-call(f32[2304,128]{1,0:T(8,128)} %bitcast.2.core_ref, f32[1152,128]{1,0:T(8,128)S(1)} %bitcast.26, bf16[96,3072]{1,0:T(8,128)(2,1)S(1)} %get-tuple-element.43.left_top, bf16[96,3072]{1,0:T(8,128)(2,1)S(1)} %copy-done.6), custom_call_target="tpu_custom_call" | custom-call | flops 1048576 | bytes 8388608 | tf_op jit(solution)/shard_map/pallas_call | solution.py:364
  110.7 2.8 %shard_map.99 = f32[144,128]{1,0:T(8,128)S(1)} custom-call(f32[2304,128]{1,0:T(8,128)} %bitcast.2.core_ref, f32[1152,128]{1,0:T(8,128)} %bitcast.7.both_ref, bf16[96,3072]{1,0:T(8,128)(2,1)S(1)} %get-tuple-element.40.left_top, bf16[96,3072]{1,0:T(8,128)(2,1)S(1)} %get-tuple-element.41.left_rest, s32[4]{0:T(128)S(1)} %pad_add_fusion.place_ref, ...), custom_call_target="tpu_custom_call" | custom-call | flops 1048576 | bytes 8388608 | tf_op jit(solution)/shard_map/pallas_call | solution.py:364
  114.6 2.7 %collective-permute-start.18 = (f32[144,128]{1,0:T(8,128)S(1)}, f32[144,128]{1,0:T(8,128)S(1)}, u32[]{:S(2)}, u32[]{:S(2)}) collective-permute-start(f32[144,128]{1,0:T(8,128)S(1)} %shard_map.99), channel_id=1, source_target_pairs={{0,12},{4,0},{8,4},{12,8},{16,28},{20,16},{24,20},{28,24},{32,44},... | collective-permute-start | bytes 221192 | tf_op jit(solution)/shard_map/ppermute | solution.py:385
  117.2 3.8 %collective-permute-done.16 = f32[144,128]{1,0:T(8,128)S(1)} collective-permute-done((f32[144,128]{1,0:T(8,128)S(1)}, f32[144,128]{1,0:T(8,128)S(1)}, u32[]{:S(2)}, u32[]{:S(2)}) %collective-permute-start.16) | collective-permute-done | bytes 73760 | tf_op jit(solution)/shard_map/ppermute | solution.py:385
  121.6 18.4 %collective-permute-start.19 = (f32[144,128]{1,0:T(8,128)S(1)}, f32[144,128]{1,0:T(8,128)S(1)}, u32[]{:S(2)}, u32[]{:S(2)}) collective-permute-start(f32[144,128]{1,0:T(8,128)S(1)} %add_add_fusion.1), channel_id=1, source_target_pairs={{0,16},{4,20},{8,24},{12,28},{16,0},{20,4},{24,8},{28,12},{32,48},... | collective-permute-start | bytes 221192 | tf_op jit(solution)/shard_map/ppermute | solution.py:385
  140.0 2.3 %collective-permute-done.19 = f32[144,128]{1,0:T(8,128)S(1)} collective-permute-done((f32[144,128]{1,0:T(8,128)S(1)}, f32[144,128]{1,0:T(8,128)S(1)}, u32[]{:S(2)}, u32[]{:S(2)}) %collective-permute-start.19) | collective-permute-done | bytes 73760 | tf_op jit(solution)/shard_map/ppermute | solution.py:385
  142.5 4.0 %collective-permute-start.22 = (f32[144,128]{1,0:T(8,128)S(1)}, f32[144,128]{1,0:T(8,128)S(1)}, u32[]{:S(2)}, u32[]{:S(2)}) collective-permute-start(f32[144,128]{1,0:T(8,128)S(1)} %add.49), channel_id=1, source_target_pairs={{0,96},{4,100},{8,104},{12,108},{16,112},{20,116},{24,120},{28,124... | collective-permute-start | bytes 221192 | tf_op jit(solution)/shard_map/ppermute | solution.py:385
  146.5 5.2 %collective-permute-done.20 = f32[144,128]{1,0:T(8,128)S(1)} collective-permute-done((f32[144,128]{1,0:T(8,128)S(1)}, f32[144,128]{1,0:T(8,128)S(1)}, u32[]{:S(2)}, u32[]{:S(2)}) %collective-permute-start.20) | collective-permute-done | bytes 73760 | tf_op jit(solution)/shard_map/ppermute | solution.py:385
  153.4 5.8 %collective-permute-done.23 = f32[144,128]{1,0:T(8,128)S(1)} collective-permute-done((f32[144,128]{1,0:T(8,128)S(1)}, f32[144,128]{1,0:T(8,128)S(1)}, u32[]{:S(2)}, u32[]{:S(2)}) %collective-permute-start.23) | collective-permute-done | bytes 73760 | tf_op jit(solution)/shard_map/ppermute | solution.py:385
  (81 shorter events, 29.4 us)
Async XLA Ops:
  0.6 8.4 %copy-start.11 = (f32[2,8,128]{2,1,0:T(8,128)S(1)}, f32[2,8,128]{2,1,0:T(8,128)}, u32[]{:S(2)}) copy-start(f32[2,8,128]{2,1,0:T(8,128)} %modulus_ref.1) | copy-start | bytes 24580
  0.6 8.2 %copy-start.10 = (s32[2,8,128]{2,1,0:T(8,128)S(1)}, s32[2,8,128]{2,1,0:T(8,128)}, u32[]{:S(2)}) copy-start(s32[2,8,128]{2,1,0:T(8,128)} %support_ref.1) | copy-start | bytes 24580
  0.7 8.2 %copy-start.12 = (f32[2,8,128]{2,1,0:T(8,128)S(1)}, f32[2,8,128]{2,1,0:T(8,128)}, u32[]{:S(2)}) copy-start(f32[2,8,128]{2,1,0:T(8,128)} %param.7) | copy-start | bytes 24580
  0.7 8.5 %copy-start.9 = (f32[24,24]{1,0:T(8,128)S(1)}, f32[24,24]{1,0:T(8,128)}, u32[]{:S(2)}) copy-start(f32[24,24]{1,0:T(8,128)} %stiff_ref.1) | copy-start | bytes 6916
  3.0 6.0 %collective-permute-start.1 = (f32[1,8,128]{2,1,0:T(8,128)}, f32[1,8,128]{2,1,0:T(8,128)S(1)}, u32[]{:S(2)}, u32[]{:S(2)}) collective-permute-start(f32[1,8,128]{2,1,0:T(8,128)} %get-tuple-element.26), channel_id=1, source_target_pairs={{0,4},{1,5},{2,6},{3,7},{4,8},{5,9},{6,10},{7,11},{8,12},{9,13},{1... | collective-permute-start | bytes 12296 | tf_op jit(solution)/shard_map/ppermute | solution.py:405
  4.7 17.1 %collective-permute-start.3 = (f32[144,8,128]{2,1,0:T(8,128)}, f32[144,8,128]{2,1,0:T(8,128)S(1)}, u32[]{:S(2)}, u32[]{:S(2)}) collective-permute-start(f32[144,8,128]{2,1,0:T(8,128)} %get-tuple-element.25.refs_1_.refs_5_), channel_id=1, source_target_pairs={{0,4},{1,5},{2,6},{3,7},{4,8},{5,9},{6,10},{7,11},{8,12},{9,13},{1... | collective-permute-start | bytes 1769480 | tf_op jit(solution)/shard_map/ppermute | solution.py:424
  6.3 17.8 %collective-permute-start = (f32[144,8,128]{2,1,0:T(8,128)}, f32[144,8,128]{2,1,0:T(8,128)S(1)}, u32[]{:S(2)}, u32[]{:S(2)}) collective-permute-start(f32[144,8,128]{2,1,0:T(8,128)} %get-tuple-element.24.refs_0_.refs_4_), channel_id=1, source_target_pairs={{4,0},{5,1},{6,2},{7,3},{8,4},{9,5},{10,6},{11,7},{12,8},{13,9},{1... | collective-permute-start | bytes 1769480 | tf_op jit(solution)/shard_map/ppermute | solution.py:425
  23.5 14.0 %collective-permute-start.5 = (f32[144,8,128]{2,1,0:T(8,128)S(1)}, f32[144,8,128]{2,1,0:T(8,128)S(1)}, u32[]{:S(2)}, u32[]{:S(2)}) collective-permute-start(f32[144,8,128]{2,1,0:T(8,128)S(1)} %shard_map.80.refs_0_.refs_4_), channel_id=1, source_target_pairs={{4,0},{5,1},{6,2},{7,3},{8,4},{9,5},{10,6},{11,7},{12,8},{13,9},{1... | collective-permute-start | bytes 1769480 | tf_op jit(solution)/shard_map/ppermute | solution.py:432
  24.0 3.4 %copy-start.2 = (f32[144,8,128]{2,1,0:T(8,128)S(1)}, f32[144,8,128]{2,1,0:T(8,128)}, u32[]{:S(2)}) copy-start(f32[144,8,128]{2,1,0:T(8,128)} %get-tuple-element.24.refs_0_.refs_4_) | copy-start | bytes 1769476
  24.0 3.4 %copy-start.4 = (f32[144,8,128]{2,1,0:T(8,128)S(1)}, f32[144,8,128]{2,1,0:T(8,128)}, u32[]{:S(2)}) copy-start(f32[144,8,128]{2,1,0:T(8,128)} %get-tuple-element.25.refs_1_.refs_5_) | copy-start | bytes 1769476
  25.7 15.8 %collective-permute-start.2 = (f32[144,8,128]{2,1,0:T(8,128)S(1)}, f32[144,8,128]{2,1,0:T(8,128)S(1)}, u32[]{:S(2)}, u32[]{:S(2)}) collective-permute-start(f32[144,8,128]{2,1,0:T(8,128)S(1)} %shard_map.79.refs_1_.refs_5_), channel_id=1, source_target_pairs={{0,4},{1,5},{2,6},{3,7},{4,8},{5,9},{6,10},{7,11},{8,12},{9,13},{1... | collective-permute-start | bytes 1769480 | tf_op jit(solution)/shard_map/ppermute | solution.py:430
  39.2 15.1 %collective-permute-start.7 = (f32[144,8,128]{2,1,0:T(8,128)S(1)}, f32[144,8,128]{2,1,0:T(8,128)S(1)}, u32[]{:S(2)}, u32[]{:S(2)}) collective-permute-start(f32[144,8,128]{2,1,0:T(8,128)S(1)} %shard_map.83.refs_1_.refs_5_), channel_id=1, source_target_pairs={{0,4},{1,5},{2,6},{3,7},{4,8},{5,9},{6,10},{7,11},{8,12},{9,13},{1... | collective-permute-start | bytes 1769480 | tf_op jit(solution)/shard_map/ppermute | solution.py:430
  43.2 15.0 %collective-permute-start.4 = (f32[144,8,128]{2,1,0:T(8,128)S(1)}, f32[144,8,128]{2,1,0:T(8,128)S(1)}, u32[]{:S(2)}, u32[]{:S(2)}) collective-permute-start(f32[144,8,128]{2,1,0:T(8,128)S(1)} %shard_map.82.refs_0_.refs_4_), channel_id=1, source_target_pairs={{4,0},{5,1},{6,2},{7,3},{8,4},{9,5},{10,6},{11,7},{12,8},{13,9},{1... | collective-permute-start | bytes 1769480 | tf_op jit(solution)/shard_map/ppermute | solution.py:432
  56.0 12.6 %collective-permute-start.8 = (f32[144,8,128]{2,1,0:T(8,128)S(1)}, f32[144,8,128]{2,1,0:T(8,128)S(1)}, u32[]{:S(2)}, u32[]{:S(2)}) collective-permute-start(f32[144,8,128]{2,1,0:T(8,128)S(1)} %shard_map.86.refs_0_), channel_id=1, source_target_pairs={{4,0},{5,1},{6,2},{7,3},{8,4},{9,5},{10,6},{11,7},{12,8},{13,9},{1... | collective-permute-start | bytes 1769480 | tf_op jit(solution)/shard_map/ppermute | solution.py:432
  59.9 17.5 %collective-permute-start.6 = (f32[144,8,128]{2,1,0:T(8,128)S(1)}, f32[144,8,128]{2,1,0:T(8,128)S(1)}, u32[]{:S(2)}, u32[]{:S(2)}) collective-permute-start(f32[144,8,128]{2,1,0:T(8,128)S(1)} %shard_map.85.refs_1_), channel_id=1, source_target_pairs={{0,4},{1,5},{2,6},{3,7},{4,8},{5,9},{6,10},{7,11},{8,12},{9,13},{1... | collective-permute-start | bytes 1769480 | tf_op jit(solution)/shard_map/ppermute | solution.py:430
  70.3 19.8 %collective-permute-start.13 = (f32[144,8,128]{2,1,0:T(8,128)S(1)}, f32[144,8,128]{2,1,0:T(8,128)S(1)}, u32[]{:S(2)}, u32[]{:S(2)}) collective-permute-start(f32[144,8,128]{2,1,0:T(8,128)S(1)} %shard_map.89.high_ref.refs_1_), channel_id=1, source_target_pairs={{0,4},{1,5},{2,6},{3,7},{4,8},{5,9},{6,10},{7,11},{8,12},{9,13},{1... | collective-permute-start | bytes 1769480 | tf_op jit(solution)/shard_map/ppermute | solution.py:430
  79.2 12.7 %collective-permute-start.11 = (f32[144,8,128]{2,1,0:T(8,128)S(1)}, f32[144,8,128]{2,1,0:T(8,128)S(1)}, u32[]{:S(2)}, u32[]{:S(2)}) collective-permute-start(f32[144,8,128]{2,1,0:T(8,128)S(1)} %shard_map.88.low_ref.refs_0_), channel_id=1, source_target_pairs={{4,0},{5,1},{6,2},{7,3},{8,4},{9,5},{10,6},{11,7},{12,8},{13,9},{1... | collective-permute-start | bytes 1769480 | tf_op jit(solution)/shard_map/ppermute | solution.py:432
  81.3 16.3 %collective-permute-start.12 = (f32[144,8,128]{2,1,0:T(8,128)S(1)}, f32[144,8,128]{2,1,0:T(8,128)S(1)}, u32[]{:S(2)}, u32[]{:S(2)}) collective-permute-start(f32[144,8,128]{2,1,0:T(8,128)S(1)} %shard_map.89.high_ref.refs_1_), channel_id=1, source_target_pairs={{0,2},{2,0},{1,3},{3,1},{4,6},{6,4},{5,7},{7,5},{8,10},{10,8},{9,1... | collective-permute-start | bytes 1769480 | tf_op jit(solution)/shard_map/ppermute | solution.py:438
  81.3 22.9 %collective-permute-start.10 = (f32[144,8,128]{2,1,0:T(8,128)S(1)}, f32[144,8,128]{2,1,0:T(8,128)S(1)}, u32[]{:S(2)}, u32[]{:S(2)}) collective-permute-start(f32[144,8,128]{2,1,0:T(8,128)S(1)} %shard_map.88.low_ref.refs_0_), channel_id=1, source_target_pairs={{0,2},{2,0},{1,3},{3,1},{4,6},{6,4},{5,7},{7,5},{8,10},{10,8},{9,1... | collective-permute-start | bytes 1769480 | tf_op jit(solution)/shard_map/ppermute | solution.py:438
  84.4 23.8 %collective-permute-start.9 = (f32[144,2,8,128]{3,2,1,0:T(8,128)}, f32[144,2,8,128]{3,2,1,0:T(8,128)}, u32[]{:S(2)}, u32[]{:S(2)}) collective-permute-start(f32[144,2,8,128]{3,2,1,0:T(8,128)} %shard_map.90.refs_3_), channel_id=1, source_target_pairs={{0,1},{1,0},{2,3},{3,2},{4,5},{5,4},{6,7},{7,6},{8,9},{9,8},{10,11... | collective-permute-start | bytes 3538952 | tf_op jit(solution)/shard_map/ppermute | solution.py:445
  91.8 5.7 %copy-start = (f32[144,2,8,128]{3,2,1,0:T(8,128)S(1)}, f32[144,2,8,128]{3,2,1,0:T(8,128)}, u32[]{:S(2)}) copy-start(f32[144,2,8,128]{3,2,1,0:T(8,128)} %shard_map.90.refs_3_) | copy-start | bytes 3538948
  97.5 10.6 %collective-permute-start.15 = (f32[144,8,128]{2,1,0:T(8,128)S(1)}, f32[144,8,128]{2,1,0:T(8,128)S(1)}, u32[]{:S(2)}, u32[]{:S(2)}) collective-permute-start(f32[144,8,128]{2,1,0:T(8,128)S(1)} %shard_map.94), channel_id=1, source_target_pairs={{0,1},{1,0},{2,3},{3,2},{4,5},{5,4},{6,7},{7,6},{8,9},{9,8},{10,11... | collective-permute-start | bytes 1769480 | tf_op jit(solution)/shard_map/ppermute | solution.py:450
  106.9 3.8 %collective-permute-start.14 = (f32[144,8,128]{2,1,0:T(8,128)S(1)}, f32[144,8,128]{2,1,0:T(8,128)}, u32[]{:S(2)}, u32[]{:S(2)}) collective-permute-start(f32[144,8,128]{2,1,0:T(8,128)S(1)} %shard_map.96), channel_id=1, source_target_pairs={{0,1},{1,0},{2,3},{3,2},{4,5},{5,4},{6,7},{7,6},{8,9},{9,8},{10,11... | collective-permute-start | bytes 1769480 | tf_op jit(solution)/shard_map/ppermute | solution.py:450
  108.2 2.5 %copy-start.8 = (f32[96,96]{1,0:T(8,128)S(1)}, f32[96,96]{1,0:T(8,128)}, u32[]{:S(2)}) copy-start(f32[96,96]{1,0:T(8,128)} %copy-done.7) | copy-start | bytes 110596
  113.4 7.5 %collective-permute-start.16 = (f32[144,128]{1,0:T(8,128)S(1)}, f32[144,128]{1,0:T(8,128)S(1)}, u32[]{:S(2)}, u32[]{:S(2)}) collective-permute-start(f32[144,128]{1,0:T(8,128)S(1)} %shard_map.99), channel_id=1, source_target_pairs={{0,4},{4,8},{8,12},{12,0},{16,20},{20,24},{24,28},{28,16},{32,36},... | collective-permute-start | bytes 221192 | tf_op jit(solution)/shard_map/ppermute | solution.py:385
  114.5 6.5 %collective-permute-start.17 = (f32[144,128]{1,0:T(8,128)S(1)}, f32[144,128]{1,0:T(8,128)S(1)}, u32[]{:S(2)}, u32[]{:S(2)}) collective-permute-start(f32[144,128]{1,0:T(8,128)S(1)} %shard_map.99), channel_id=1, source_target_pairs={{0,8},{4,12},{8,0},{12,4},{16,24},{20,28},{24,16},{28,20},{32,40},... | collective-permute-start | bytes 221192 | tf_op jit(solution)/shard_map/ppermute | solution.py:385
  114.6 7.0 %collective-permute-start.18 = (f32[144,128]{1,0:T(8,128)S(1)}, f32[144,128]{1,0:T(8,128)S(1)}, u32[]{:S(2)}, u32[]{:S(2)}) collective-permute-start(f32[144,128]{1,0:T(8,128)S(1)} %shard_map.99), channel_id=1, source_target_pairs={{0,12},{4,0},{8,4},{12,8},{16,28},{20,16},{24,20},{28,24},{32,44},... | collective-permute-start | bytes 221192 | tf_op jit(solution)/shard_map/ppermute | solution.py:385
  121.6 20.7 %collective-permute-start.19 = (f32[144,128]{1,0:T(8,128)S(1)}, f32[144,128]{1,0:T(8,128)S(1)}, u32[]{:S(2)}, u32[]{:S(2)}) collective-permute-start(f32[144,128]{1,0:T(8,128)S(1)} %add_add_fusion.1), channel_id=1, source_target_pairs={{0,16},{4,20},{8,24},{12,28},{16,0},{20,4},{24,8},{28,12},{32,48},... | collective-permute-start | bytes 221192 | tf_op jit(solution)/shard_map/ppermute | solution.py:385
  142.3 9.4 %collective-permute-start.20 = (f32[144,128]{1,0:T(8,128)S(1)}, f32[144,128]{1,0:T(8,128)S(1)}, u32[]{:S(2)}, u32[]{:S(2)}) collective-permute-start(f32[144,128]{1,0:T(8,128)S(1)} %add.49), channel_id=1, source_target_pairs={{0,32},{4,36},{8,40},{12,44},{16,48},{20,52},{24,56},{28,60},{32,6... | collective-permute-start | bytes 221192 | tf_op jit(solution)/shard_map/ppermute | solution.py:385
  142.4 9.3 %collective-permute-start.21 = (f32[144,128]{1,0:T(8,128)S(1)}, f32[144,128]{1,0:T(8,128)S(1)}, u32[]{:S(2)}, u32[]{:S(2)}) collective-permute-start(f32[144,128]{1,0:T(8,128)S(1)} %add.49), channel_id=1, source_target_pairs={{0,64},{4,68},{8,72},{12,76},{16,80},{20,84},{24,88},{28,92},{32,9... | collective-permute-start | bytes 221192 | tf_op jit(solution)/shard_map/ppermute | solution.py:385
  142.5 10.8 %collective-permute-start.22 = (f32[144,128]{1,0:T(8,128)S(1)}, f32[144,128]{1,0:T(8,128)S(1)}, u32[]{:S(2)}, u32[]{:S(2)}) collective-permute-start(f32[144,128]{1,0:T(8,128)S(1)} %add.49), channel_id=1, source_target_pairs={{0,96},{4,100},{8,104},{12,108},{16,112},{20,116},{24,120},{28,124... | collective-permute-start | bytes 221192 | tf_op jit(solution)/shard_map/ppermute | solution.py:385
  153.3 5.9 %collective-permute-start.23 = (f32[144,128]{1,0:T(8,128)S(1)}, f32[144,128]{1,0:T(8,128)S(1)}, u32[]{:S(2)}, u32[]{:S(2)}) collective-permute-start(f32[144,128]{1,0:T(8,128)S(1)} %add_add_fusion), channel_id=1, source_target_pairs={{0,128},{4,132},{8,136},{12,140},{16,144},{20,148},{24,152},{28,15... | collective-permute-start | bytes 221192 | tf_op jit(solution)/shard_map/ppermute | solution.py:385
  (5 other events, 4.9 us)

commit v6 on v4

--- a/solution.py
+++ b/solution.py
@@ -244,7 +244,7 @@
         do(row, pl.ds(pl.multiple_of(row * depth, depth), depth))
         return 0
 
-    lax.fori_loop(0, stride, some, 0, unroll=4)
+    lax.fori_loop(0, stride, some, 0, unroll=12)
 
 
 def modes_at(ref, row, modes):

time: 159 us -> 159 us (level)
  no operation moved by 1% of the time
where the time goes in v6:
time: 159 us; the launch traced here: 158 us
  Pallas kernels  54.5 us (34%)
  waiting for transfers between devices  54.4 us (34%)
  starting transfers between devices  43.7 us (27%)
  local copies, waits for them, and re-layouts  3.37 us (2%)
    pallas_call x5, Pallas kernels, own_part(): pl.pallas_call(partial(own_kernel, shift, count), in_specs=[IN_VMEM] * le...  29.3 us
    ppermute x8, starting transfers between devices, total_over(): parts.append(lax.ppermute(x, axes, pairs))  26.8 us
    ppermute x8, waiting for transfers between devices, total_over(): parts.append(lax.ppermute(x, axes, pairs))  18.8 us
    pallas_call x10, Pallas kernels, with_halo(): pl.pallas_call(partial(halo_kernel, p), in_specs=[IN_VMEM] * 4, out_specs...  17 us
    ppermute x4, waiting for transfers between devices, body(): below = lax.ppermute(high, everywhere, up)  12.1 us
    ppermute x2, waiting for transfers between devices, body(): by_x[p] = lax.ppermute(current[p], 'xl', swap)  10.6 us
    ppermute x4, starting transfers between devices, body(): upper = lax.ppermute(low, everywhere, down)  6.77 us
    ppermute x4, waiting for transfers between devices, body(): upper = lax.ppermute(low, everywhere, down)  6.76 us
  transfers between devices with their start and end apart: 24, of which 16 were waited for; matrix products, arithmetic and copies ran while one was open for 0% of the time, Pallas kernels for 32%

profile of v6, /device:TPU:32, one launch (start us, length us, event | category | flops | bytes accessed | tf_op | source)
XLA Modules:
  0.0 157.9 jit_solution(3317950865734367161)
XLA Ops:
  6.7 2.6 %collective-permute-start = (f32[144,8,128]{2,1,0:T(8,128)S(1)}, f32[144,8,128]{2,1,0:T(8,128)S(1)}, u32[]{:S(2)}, u32[]{:S(2)}) collective-permute-start(f32[144,8,128]{2,1,0:T(8,128)S(1)} %get-tuple-element.24.refs_0_.refs_4_), channel_id=1, source_target_pairs={{4,0},{5,1},{6,2},{7,3},{8,4},{9,5},{10,6},{11,7},{12,8},{13,9},{1... | collective-permute-start | bytes 1769480 | tf_op jit(solution)/shard_map/ppermute | solution.py:409
  10.6 5.9 %shard_map.78 = (f32[144,8,128]{2,1,0:T(8,128)S(1)}, f32[144,8,128]{2,1,0:T(8,128)S(1)}) custom-call(f32[144,8,128]{2,1,0:T(8,128)S(1)} %get-tuple-element.24.refs_0_.refs_4_, f32[144,8,128]{2,1,0:T(8,128)S(1)} %get-tuple-element.25.refs_1_.refs_5_, f32[324,8,128]{2,1,0:T(8,128)S(1)} %get-tuple-element.27.refs_2_, ...), custom_call_target="tpu_custom_call" | custom-call | flops 31850496 | bytes 16777216 | tf_op jit(solution)/shard_map/pallas_call | solution.py:162
  16.5 5.5 %collective-permute-done.3.halo_ref = f32[144,8,128]{2,1,0:T(8,128)S(1)} collective-permute-done((f32[144,8,128]{2,1,0:T(8,128)S(1)}, f32[144,8,128]{2,1,0:T(8,128)S(1)}, u32[]{:S(2)}, u32[]{:S(2)}) %collective-permute-start.3) | collective-permute-done | bytes 589856 | tf_op jit(solution)/shard_map/ppermute | solution.py:408
  27.6 5.9 %shard_map.81 = (f32[144,8,128]{2,1,0:T(8,128)S(1)}, f32[144,8,128]{2,1,0:T(8,128)S(1)}) custom-call(f32[144,8,128]{2,1,0:T(8,128)S(1)} %shard_map.80.refs_0_.refs_4_, f32[144,8,128]{2,1,0:T(8,128)S(1)} %shard_map.79.refs_1_.refs_5_, f32[324,8,128]{2,1,0:T(8,128)S(1)} %get-tuple-element.27.refs_2_, f32[2,8,128]{2,1,0:T(8,128)S(1)} %get-tuple-element.45.refs_3_.scale_ref, ...), custom_call_target="tpu_custom_call" | custom-call | flops 31850496 | bytes 16777216 | tf_op jit(solution)/shard_map/pallas_call | solution.py:162
  33.6 4.1 %collective-permute-done.5.halo_ref = f32[144,8,128]{2,1,0:T(8,128)S(1)} collective-permute-done((f32[144,8,128]{2,1,0:T(8,128)S(1)}, f32[144,8,128]{2,1,0:T(8,128)S(1)}, u32[]{:S(2)}, u32[]{:S(2)}) %collective-permute-start.5) | collective-permute-done | bytes 589856 | tf_op jit(solution)/shard_map/ppermute | solution.py:416
  37.7 1.7 %shard_map.83.refs_1_.refs_5_ = f32[144,8,128]{2,1,0:T(8,128)S(1)} custom-call(f32[144,8,128]{2,1,0:T(8,128)S(1)} %collective-permute-done.5.halo_ref, f32[144,8,128]{2,1,0:T(8,128)S(1)} %get-tuple-element.32.part_ref, f32[162,8,128]{2,1,0:T(8,128)S(1)} %get-tuple-element.29.coef_ref, f32[2,8,128]{2,1,0:T(8,128)S(1)} %get-tuple-element.45.refs_3_.scale_ref), custom_call_target="tpu_custom_call" | custom-call | flops 7962624 | bytes 5242880 | tf_op jit(solution)/shard_map/pallas_call | solution.py:197
  39.5 2.3 %collective-permute-done.2.halo_ref = f32[144,8,128]{2,1,0:T(8,128)S(1)} collective-permute-done((f32[144,8,128]{2,1,0:T(8,128)S(1)}, f32[144,8,128]{2,1,0:T(8,128)S(1)}, u32[]{:S(2)}, u32[]{:S(2)}) %collective-permute-start.2) | collective-permute-done | bytes 589856 | tf_op jit(solution)/shard_map/ppermute | solution.py:414
  43.5 1.9 %collective-permute-start.4 = (f32[144,8,128]{2,1,0:T(8,128)S(1)}, f32[144,8,128]{2,1,0:T(8,128)S(1)}, u32[]{:S(2)}, u32[]{:S(2)}) collective-permute-start(f32[144,8,128]{2,1,0:T(8,128)S(1)} %shard_map.82.refs_0_.refs_4_), channel_id=1, source_target_pairs={{4,0},{5,1},{6,2},{7,3},{8,4},{9,5},{10,6},{11,7},{12,8},{13,9},{1... | collective-permute-start | bytes 1769480 | tf_op jit(solution)/shard_map/ppermute | solution.py:416
  45.4 5.9 %shard_map.84 = (f32[144,8,128]{2,1,0:T(8,128)S(1)}, f32[144,8,128]{2,1,0:T(8,128)S(1)}) custom-call(f32[144,8,128]{2,1,0:T(8,128)S(1)} %shard_map.82.refs_0_.refs_4_, f32[144,8,128]{2,1,0:T(8,128)S(1)} %shard_map.83.refs_1_.refs_5_, f32[324,8,128]{2,1,0:T(8,128)S(1)} %get-tuple-element.27.refs_2_, f32[2,8,128]{2,1,0:T(8,128)S(1)} %get-tuple-element.45.refs_3_.scale_ref, ...), custom_call_target="tpu_custom_call" | custom-call | flops 31850496 | bytes 16777216 | tf_op jit(solution)/shard_map/pallas_call | solution.py:162
  51.3 3.2 %collective-permute-done.7.halo_ref = f32[144,8,128]{2,1,0:T(8,128)S(1)} collective-permute-done((f32[144,8,128]{2,1,0:T(8,128)S(1)}, f32[144,8,128]{2,1,0:T(8,128)S(1)}, u32[]{:S(2)}, u32[]{:S(2)}) %collective-permute-start.7) | collective-permute-done | bytes 589856 | tf_op jit(solution)/shard_map/ppermute | solution.py:414
  56.2 2.2 %collective-permute-start.8 = (f32[144,8,128]{2,1,0:T(8,128)S(1)}, f32[144,8,128]{2,1,0:T(8,128)S(1)}, u32[]{:S(2)}, u32[]{:S(2)}) collective-permute-start(f32[144,8,128]{2,1,0:T(8,128)S(1)} %shard_map.86.refs_0_), channel_id=1, source_target_pairs={{4,0},{5,1},{6,2},{7,3},{8,4},{9,5},{10,6},{11,7},{12,8},{13,9},{1... | collective-permute-start | bytes 1769480 | tf_op jit(solution)/shard_map/ppermute | solution.py:416
  58.5 1.7 %shard_map.85.refs_1_ = f32[144,8,128]{2,1,0:T(8,128)S(1)} custom-call(f32[144,8,128]{2,1,0:T(8,128)S(1)} %collective-permute-done.4.halo_ref, f32[144,8,128]{2,1,0:T(8,128)S(1)} %get-tuple-element.33.part_ref, f32[162,8,128]{2,1,0:T(8,128)S(1)} %get-tuple-element.29.coef_ref, f32[2,8,128]{2,1,0:T(8,128)S(1)} %get-tuple-element.45.refs_3_.scale_ref), custom_call_target="tpu_custom_call" | custom-call | flops 7962624 | bytes 5242880 | tf_op jit(solution)/shard_map/pallas_call | solution.py:197
  60.3 5.9 %shard_map.87 = (f32[144,8,128]{2,1,0:T(8,128)S(1)}, f32[144,8,128]{2,1,0:T(8,128)S(1)}) custom-call(f32[144,8,128]{2,1,0:T(8,128)S(1)} %shard_map.86.refs_0_, f32[144,8,128]{2,1,0:T(8,128)S(1)} %shard_map.85.refs_1_, f32[324,8,128]{2,1,0:T(8,128)S(1)} %get-tuple-element.27.refs_2_, f32[2,8,128]{2,1,0:T(8,128)S(1)} %get-tuple-element.45.refs_3_.scale_ref, ...), custom_call_target="tpu_custom_call" | custom-call | flops 31850496 | bytes 16777216 | tf_op jit(solution)/shard_map/pallas_call | solution.py:162
  66.2 2.6 %collective-permute-done.8.halo_ref = f32[144,8,128]{2,1,0:T(8,128)S(1)} collective-permute-done((f32[144,8,128]{2,1,0:T(8,128)S(1)}, f32[144,8,128]{2,1,0:T(8,128)S(1)}, u32[]{:S(2)}, u32[]{:S(2)}) %collective-permute-start.8) | collective-permute-done | bytes 589856 | tf_op jit(solution)/shard_map/ppermute | solution.py:416
  68.8 1.7 %shard_map.89.high_ref.refs_1_ = f32[144,8,128]{2,1,0:T(8,128)S(1)} custom-call(f32[144,8,128]{2,1,0:T(8,128)S(1)} %collective-permute-done.8.halo_ref, f32[144,8,128]{2,1,0:T(8,128)S(1)} %get-tuple-element.36.part_ref, f32[162,8,128]{2,1,0:T(8,128)S(1)} %get-tuple-element.29.coef_ref, f32[2,8,128]{2,1,0:T(8,128)S(1)} %get-tuple-element.45.refs_3_.scale_ref), custom_call_target="tpu_custom_call" | custom-call | flops 7962624 | bytes 5242880 | tf_op jit(solution)/shard_map/pallas_call | solution.py:197
  71.1 6.7 %collective-permute-done.6.halo_ref = f32[144,8,128]{2,1,0:T(8,128)S(1)} collective-permute-done((f32[144,8,128]{2,1,0:T(8,128)S(1)}, f32[144,8,128]{2,1,0:T(8,128)S(1)}, u32[]{:S(2)}, u32[]{:S(2)}) %collective-permute-start.6) | collective-permute-done | bytes 589856 | tf_op jit(solution)/shard_map/ppermute | solution.py:414
  79.4 2.1 %collective-permute-start.11 = (f32[144,8,128]{2,1,0:T(8,128)S(1)}, f32[144,8,128]{2,1,0:T(8,128)S(1)}, u32[]{:S(2)}, u32[]{:S(2)}) collective-permute-start(f32[144,8,128]{2,1,0:T(8,128)S(1)} %shard_map.88.low_ref.refs_0_), channel_id=1, source_target_pairs={{4,0},{5,1},{6,2},{7,3},{8,4},{9,5},{10,6},{11,7},{12,8},{13,9},{1... | collective-permute-start | bytes 1769480 | tf_op jit(solution)/shard_map/ppermute | solution.py:416
  82.6 2.0 %collective-permute-start.10 = (f32[144,8,128]{2,1,0:T(8,128)S(1)}, f32[144,8,128]{2,1,0:T(8,128)S(1)}, u32[]{:S(2)}, u32[]{:S(2)}) collective-permute-start(f32[144,8,128]{2,1,0:T(8,128)S(1)} %shard_map.88.low_ref.refs_0_), channel_id=1, source_target_pairs={{0,2},{2,0},{1,3},{3,1},{4,6},{6,4},{5,7},{7,5},{8,10},{10,8},{9,1... | collective-permute-start | bytes 1769480 | tf_op jit(solution)/shard_map/ppermute | solution.py:422
  84.7 5.7 %shard_map.91 = (f32[144,8,128]{2,1,0:T(8,128)S(1)}, f32[144,8,128]{2,1,0:T(8,128)S(1)}) custom-call(f32[144,8,128]{2,1,0:T(8,128)S(1)} %shard_map.88.low_ref.refs_0_, f32[144,8,128]{2,1,0:T(8,128)S(1)} %shard_map.89.high_ref.refs_1_, f32[324,8,128]{2,1,0:T(8,128)S(1)} %get-tuple-element.27.refs_2_, f32[2,8,128]{2,1,0:T(8,128)S(1)} %subtract_convert_fusion.refs_3_.scale_ref), custom_call_target="tpu_custom_call" | custom-call | flops 31850496 | bytes 16777216 | tf_op jit(solution)/shard_map/pallas_call | solution.py:162
  90.4 1.7 %shard_map.93.refs_1_ = f32[144,8,128]{2,1,0:T(8,128)S(1)} custom-call(f32[144,8,128]{2,1,0:T(8,128)S(1)} %collective-permute-done.13.halo_ref, f32[144,8,128]{2,1,0:T(8,128)S(1)} %get-tuple-element.38.part_ref, f32[162,8,128]{2,1,0:T(8,128)S(1)} %get-tuple-element.29.coef_ref, f32[2,8,128]{2,1,0:T(8,128)S(1)} %subtract_convert_fusion.refs_3_.scale_ref), custom_call_target="tpu_custom_call" | custom-call | flops 7962624 | bytes 5242880 | tf_op jit(solution)/shard_map/pallas_call | solution.py:197
  92.1 1.7 %shard_map.92.refs_2_ = f32[144,8,128]{2,1,0:T(8,128)S(1)} custom-call(f32[144,8,128]{2,1,0:T(8,128)S(1)} %collective-permute-done.11.halo_ref, f32[144,8,128]{2,1,0:T(8,128)S(1)} %get-tuple-element.37.part_ref, f32[162,8,128]{2,1,0:T(8,128)S(1)} %get-tuple-element.29.coef_ref, f32[2,8,128]{2,1,0:T(8,128)S(1)} %subtract_convert_fusion.refs_3_.scale_ref), custom_call_target="tpu_custom_call" | custom-call | flops 7962624 | bytes 5242880 | tf_op jit(solution)/shard_map/pallas_call | solution.py:197
  93.8 3.7 %collective-permute-done.12.refs_0_ = f32[144,8,128]{2,1,0:T(8,128)S(1)} collective-permute-done((f32[144,8,128]{2,1,0:T(8,128)S(1)}, f32[144,8,128]{2,1,0:T(8,128)S(1)}, u32[]{:S(2)}, u32[]{:S(2)}) %collective-permute-start.12) | collective-permute-done | bytes 589856 | tf_op jit(solution)/shard_map/ppermute | solution.py:422
  97.5 6.9 %collective-permute-done.10.refs_0_ = f32[144,8,128]{2,1,0:T(8,128)S(1)} collective-permute-done((f32[144,8,128]{2,1,0:T(8,128)S(1)}, f32[144,8,128]{2,1,0:T(8,128)S(1)}, u32[]{:S(2)}, u32[]{:S(2)}) %collective-permute-start.10) | collective-permute-done | bytes 589856 | tf_op jit(solution)/shard_map/ppermute | solution.py:422
  109.5 1.9 %shard_map.99 = f32[144,128]{1,0:T(8,128)S(1)} custom-call(f32[2304,128]{1,0:T(8,128)S(1)} %bitcast.26, f32[1152,128]{1,0:T(8,128)S(1)} %bitcast.29, bf16[96,3072]{1,0:T(8,128)(2,1)S(1)} %get-tuple-element.42.left_top, bf16[96,3072]{1,0:T(8,128)(2,1)S(1)} %get-tuple-element.43.left_rest, s32[4]{0:T(128)S(1)} %pad_add_fusion.place_ref, ...), custom_call_target="tpu_custom_call" | custom-call | flops 1048576 | bytes 8388608 | tf_op jit(solution)/shard_map/pallas_call | solution.py:348
  112.5 2.7 %collective-permute-start.18 = (f32[144,128]{1,0:T(8,128)S(1)}, f32[144,128]{1,0:T(8,128)S(1)}, u32[]{:S(2)}, u32[]{:S(2)}) collective-permute-start(f32[144,128]{1,0:T(8,128)S(1)} %shard_map.99), channel_id=1, source_target_pairs={{0,12},{4,0},{8,4},{12,8},{16,28},{20,16},{24,20},{28,24},{32,44},... | collective-permute-start | bytes 221192 | tf_op jit(solution)/shard_map/ppermute | solution.py:369
  115.2 3.4 %collective-permute-done.16 = f32[144,128]{1,0:T(8,128)S(1)} collective-permute-done((f32[144,128]{1,0:T(8,128)S(1)}, f32[144,128]{1,0:T(8,128)S(1)}, u32[]{:S(2)}, u32[]{:S(2)}) %collective-permute-start.16) | collective-permute-done | bytes 73760 | tf_op jit(solution)/shard_map/ppermute | solution.py:369
  119.2 18.7 %collective-permute-start.19 = (f32[144,128]{1,0:T(8,128)S(1)}, f32[144,128]{1,0:T(8,128)S(1)}, u32[]{:S(2)}, u32[]{:S(2)}) collective-permute-start(f32[144,128]{1,0:T(8,128)S(1)} %add_add_fusion.1), channel_id=1, source_target_pairs={{0,16},{4,20},{8,24},{12,28},{16,0},{20,4},{24,8},{28,12},{32,48},... | collective-permute-start | bytes 221192 | tf_op jit(solution)/shard_map/ppermute | solution.py:369
  137.9 2.4 %collective-permute-done.19 = f32[144,128]{1,0:T(8,128)S(1)} collective-permute-done((f32[144,128]{1,0:T(8,128)S(1)}, f32[144,128]{1,0:T(8,128)S(1)}, u32[]{:S(2)}, u32[]{:S(2)}) %collective-permute-start.19) | collective-permute-done | bytes 73760 | tf_op jit(solution)/shard_map/ppermute | solution.py:369
  140.5 4.0 %collective-permute-start.22 = (f32[144,128]{1,0:T(8,128)S(1)}, f32[144,128]{1,0:T(8,128)S(1)}, u32[]{:S(2)}, u32[]{:S(2)}) collective-permute-start(f32[144,128]{1,0:T(8,128)S(1)} %add.49), channel_id=1, source_target_pairs={{0,96},{4,100},{8,104},{12,108},{16,112},{20,116},{24,120},{28,124... | collective-permute-start | bytes 221192 | tf_op jit(solution)/shard_map/ppermute | solution.py:369
  144.5 3.1 %collective-permute-done.20 = f32[144,128]{1,0:T(8,128)S(1)} collective-permute-done((f32[144,128]{1,0:T(8,128)S(1)}, f32[144,128]{1,0:T(8,128)S(1)}, u32[]{:S(2)}, u32[]{:S(2)}) %collective-permute-start.20) | collective-permute-done | bytes 73760 | tf_op jit(solution)/shard_map/ppermute | solution.py:369
  147.5 3.3 %collective-permute-done.21 = f32[144,128]{1,0:T(8,128)S(1)} collective-permute-done((f32[144,128]{1,0:T(8,128)S(1)}, f32[144,128]{1,0:T(8,128)S(1)}, u32[]{:S(2)}, u32[]{:S(2)}) %collective-permute-start.21) | collective-permute-done | bytes 73760 | tf_op jit(solution)/shard_map/ppermute | solution.py:369
  151.3 5.8 %collective-permute-done.23 = f32[144,128]{1,0:T(8,128)S(1)} collective-permute-done((f32[144,128]{1,0:T(8,128)S(1)}, f32[144,128]{1,0:T(8,128)S(1)}, u32[]{:S(2)}, u32[]{:S(2)}) %collective-permute-start.23) | collective-permute-done | bytes 73760 | tf_op jit(solution)/shard_map/ppermute | solution.py:369
  (83 shorter events, 28.0 us)
Async XLA Ops:
  3.3 6.0 %copy-start.9 = (s32[2,8,128]{2,1,0:T(8,128)S(1)}, s32[2,8,128]{2,1,0:T(8,128)}, u32[]{:S(2)}) copy-start(s32[2,8,128]{2,1,0:T(8,128)} %support_ref.1) | copy-start | bytes 24580
  3.3 6.0 %copy-start.13 = (f32[2,8,128]{2,1,0:T(8,128)S(1)}, f32[2,8,128]{2,1,0:T(8,128)}, u32[]{:S(2)}) copy-start(f32[2,8,128]{2,1,0:T(8,128)} %param.7) | copy-start | bytes 24580
  3.3 6.0 %copy-start.11 = (f32[2,8,128]{2,1,0:T(8,128)S(1)}, f32[2,8,128]{2,1,0:T(8,128)}, u32[]{:S(2)}) copy-start(f32[2,8,128]{2,1,0:T(8,128)} %modulus_ref.1) | copy-start | bytes 24580
  3.3 6.1 %copy-start.12 = (f32[24,24]{1,0:T(8,128)S(1)}, f32[24,24]{1,0:T(8,128)}, u32[]{:S(2)}) copy-start(f32[24,24]{1,0:T(8,128)} %stiff_ref.1) | copy-start | bytes 6916
  3.5 5.9 %collective-permute-start.1 = (f32[1,8,128]{2,1,0:T(8,128)S(1)}, f32[1,8,128]{2,1,0:T(8,128)S(1)}, u32[]{:S(2)}, u32[]{:S(2)}) collective-permute-start(f32[1,8,128]{2,1,0:T(8,128)S(1)} %get-tuple-element.26), channel_id=1, source_target_pairs={{0,4},{1,5},{2,6},{3,7},{4,8},{5,9},{6,10},{7,11},{8,12},{9,13},{1... | collective-permute-start | bytes 12296 | tf_op jit(solution)/shard_map/ppermute | solution.py:389
  5.1 16.9 %collective-permute-start.3 = (f32[144,8,128]{2,1,0:T(8,128)S(1)}, f32[144,8,128]{2,1,0:T(8,128)S(1)}, u32[]{:S(2)}, u32[]{:S(2)}) collective-permute-start(f32[144,8,128]{2,1,0:T(8,128)S(1)} %get-tuple-element.25.refs_1_.refs_5_), channel_id=1, source_target_pairs={{0,4},{1,5},{2,6},{3,7},{4,8},{5,9},{6,10},{7,11},{8,12},{9,13},{1... | collective-permute-start | bytes 1769480 | tf_op jit(solution)/shard_map/ppermute | solution.py:408
  6.7 17.6 %collective-permute-start = (f32[144,8,128]{2,1,0:T(8,128)S(1)}, f32[144,8,128]{2,1,0:T(8,128)S(1)}, u32[]{:S(2)}, u32[]{:S(2)}) collective-permute-start(f32[144,8,128]{2,1,0:T(8,128)S(1)} %get-tuple-element.24.refs_0_.refs_4_), channel_id=1, source_target_pairs={{4,0},{5,1},{6,2},{7,3},{8,4},{9,5},{10,6},{11,7},{12,8},{13,9},{1... | collective-permute-start | bytes 1769480 | tf_op jit(solution)/shard_map/ppermute | solution.py:409
  23.7 14.0 %collective-permute-start.5 = (f32[144,8,128]{2,1,0:T(8,128)S(1)}, f32[144,8,128]{2,1,0:T(8,128)S(1)}, u32[]{:S(2)}, u32[]{:S(2)}) collective-permute-start(f32[144,8,128]{2,1,0:T(8,128)S(1)} %shard_map.80.refs_0_.refs_4_), channel_id=1, source_target_pairs={{4,0},{5,1},{6,2},{7,3},{8,4},{9,5},{10,6},{11,7},{12,8},{13,9},{1... | collective-permute-start | bytes 1769480 | tf_op jit(solution)/shard_map/ppermute | solution.py:416
  26.0 15.8 %collective-permute-start.2 = (f32[144,8,128]{2,1,0:T(8,128)S(1)}, f32[144,8,128]{2,1,0:T(8,128)S(1)}, u32[]{:S(2)}, u32[]{:S(2)}) collective-permute-start(f32[144,8,128]{2,1,0:T(8,128)S(1)} %shard_map.79.refs_1_.refs_5_), channel_id=1, source_target_pairs={{0,4},{1,5},{2,6},{3,7},{4,8},{5,9},{6,10},{7,11},{8,12},{9,13},{1... | collective-permute-start | bytes 1769480 | tf_op jit(solution)/shard_map/ppermute | solution.py:414
  39.4 15.1 %collective-permute-start.7 = (f32[144,8,128]{2,1,0:T(8,128)S(1)}, f32[144,8,128]{2,1,0:T(8,128)S(1)}, u32[]{:S(2)}, u32[]{:S(2)}) collective-permute-start(f32[144,8,128]{2,1,0:T(8,128)S(1)} %shard_map.83.refs_1_.refs_5_), channel_id=1, source_target_pairs={{0,4},{1,5},{2,6},{3,7},{4,8},{5,9},{6,10},{7,11},{8,12},{9,13},{1... | collective-permute-start | bytes 1769480 | tf_op jit(solution)/shard_map/ppermute | solution.py:414
  43.5 15.0 %collective-permute-start.4 = (f32[144,8,128]{2,1,0:T(8,128)S(1)}, f32[144,8,128]{2,1,0:T(8,128)S(1)}, u32[]{:S(2)}, u32[]{:S(2)}) collective-permute-start(f32[144,8,128]{2,1,0:T(8,128)S(1)} %shard_map.82.refs_0_.refs_4_), channel_id=1, source_target_pairs={{4,0},{5,1},{6,2},{7,3},{8,4},{9,5},{10,6},{11,7},{12,8},{13,9},{1... | collective-permute-start | bytes 1769480 | tf_op jit(solution)/shard_map/ppermute | solution.py:416
  56.2 12.6 %collective-permute-start.8 = (f32[144,8,128]{2,1,0:T(8,128)S(1)}, f32[144,8,128]{2,1,0:T(8,128)S(1)}, u32[]{:S(2)}, u32[]{:S(2)}) collective-permute-start(f32[144,8,128]{2,1,0:T(8,128)S(1)} %shard_map.86.refs_0_), channel_id=1, source_target_pairs={{4,0},{5,1},{6,2},{7,3},{8,4},{9,5},{10,6},{11,7},{12,8},{13,9},{1... | collective-permute-start | bytes 1769480 | tf_op jit(solution)/shard_map/ppermute | solution.py:416
  60.2 17.5 %collective-permute-start.6 = (f32[144,8,128]{2,1,0:T(8,128)S(1)}, f32[144,8,128]{2,1,0:T(8,128)S(1)}, u32[]{:S(2)}, u32[]{:S(2)}) collective-permute-start(f32[144,8,128]{2,1,0:T(8,128)S(1)} %shard_map.85.refs_1_), channel_id=1, source_target_pairs={{0,4},{1,5},{2,6},{3,7},{4,8},{5,9},{6,10},{7,11},{8,12},{9,13},{1... | collective-permute-start | bytes 1769480 | tf_op jit(solution)/shard_map/ppermute | solution.py:414
  70.6 19.8 %collective-permute-start.13 = (f32[144,8,128]{2,1,0:T(8,128)S(1)}, f32[144,8,128]{2,1,0:T(8,128)S(1)}, u32[]{:S(2)}, u32[]{:S(2)}) collective-permute-start(f32[144,8,128]{2,1,0:T(8,128)S(1)} %shard_map.89.high_ref.refs_1_), channel_id=1, source_target_pairs={{0,4},{1,5},{2,6},{3,7},{4,8},{5,9},{6,10},{7,11},{8,12},{9,13},{1... | collective-permute-start | bytes 1769480 | tf_op jit(solution)/shard_map/ppermute | solution.py:414
  79.4 12.6 %collective-permute-start.11 = (f32[144,8,128]{2,1,0:T(8,128)S(1)}, f32[144,8,128]{2,1,0:T(8,128)S(1)}, u32[]{:S(2)}, u32[]{:S(2)}) collective-permute-start(f32[144,8,128]{2,1,0:T(8,128)S(1)} %shard_map.88.low_ref.refs_0_), channel_id=1, source_target_pairs={{4,0},{5,1},{6,2},{7,3},{8,4},{9,5},{10,6},{11,7},{12,8},{13,9},{1... | collective-permute-start | bytes 1769480 | tf_op jit(solution)/shard_map/ppermute | solution.py:416
  81.5 16.0 %collective-permute-start.12 = (f32[144,8,128]{2,1,0:T(8,128)S(1)}, f32[144,8,128]{2,1,0:T(8,128)S(1)}, u32[]{:S(2)}, u32[]{:S(2)}) collective-permute-start(f32[144,8,128]{2,1,0:T(8,128)S(1)} %shard_map.89.high_ref.refs_1_), channel_id=1, source_target_pairs={{0,2},{2,0},{1,3},{3,1},{4,6},{6,4},{5,7},{7,5},{8,10},{10,8},{9,1... | collective-permute-start | bytes 1769480 | tf_op jit(solution)/shard_map/ppermute | solution.py:422
  82.6 23.0 %collective-permute-start.9 = (f32[144,2,8,128]{3,2,1,0:T(8,128)}, f32[144,2,8,128]{3,2,1,0:T(8,128)S(1)}, u32[]{:S(2)}, u32[]{:S(2)}) collective-permute-start(f32[144,2,8,128]{3,2,1,0:T(8,128)} %shard_map.90.refs_3_), channel_id=1, source_target_pairs={{0,1},{1,0},{2,3},{3,2},{4,5},{5,4},{6,7},{7,6},{8,9},{9,8},{10,11... | collective-permute-start | bytes 3538952 | tf_op jit(solution)/shard_map/ppermute | solution.py:429
  82.6 21.7 %collective-permute-start.10 = (f32[144,8,128]{2,1,0:T(8,128)S(1)}, f32[144,8,128]{2,1,0:T(8,128)S(1)}, u32[]{:S(2)}, u32[]{:S(2)}) collective-permute-start(f32[144,8,128]{2,1,0:T(8,128)S(1)} %shard_map.88.low_ref.refs_0_), channel_id=1, source_target_pairs={{0,2},{2,0},{1,3},{3,1},{4,6},{6,4},{5,7},{7,5},{8,10},{10,8},{9,1... | collective-permute-start | bytes 1769480 | tf_op jit(solution)/shard_map/ppermute | solution.py:422
  92.1 5.4 %copy-start = (f32[144,2,8,128]{3,2,1,0:T(8,128)S(1)}, f32[144,2,8,128]{3,2,1,0:T(8,128)}, u32[]{:S(2)}) copy-start(f32[144,2,8,128]{3,2,1,0:T(8,128)} %shard_map.90.refs_3_) | copy-start | bytes 3538948
  97.5 8.2 %collective-permute-start.14 = (f32[144,8,128]{2,1,0:T(8,128)S(1)}, f32[144,8,128]{2,1,0:T(8,128)S(1)}, u32[]{:S(2)}, u32[]{:S(2)}) collective-permute-start(f32[144,8,128]{2,1,0:T(8,128)S(1)} %shard_map.94), channel_id=1, source_target_pairs={{0,1},{1,0},{2,3},{3,2},{4,5},{5,4},{6,7},{7,6},{8,9},{9,8},{10,11... | collective-permute-start | bytes 1769480 | tf_op jit(solution)/shard_map/ppermute | solution.py:434
  107.5 2.0 %copy-start.2 = (f32[144,2,8,128]{3,2,1,0:T(8,128)S(1)}, f32[144,2,8,128]{3,2,1,0:T(8,128)}, u32[]{:S(2)}) copy-start(f32[144,2,8,128]{3,2,1,0:T(8,128)} %copy-done.1) | copy-start | bytes 3538948
  107.5 2.0 %collective-permute-start.15 = (f32[144,8,128]{2,1,0:T(8,128)S(1)}, f32[144,8,128]{2,1,0:T(8,128)S(1)}, u32[]{:S(2)}, u32[]{:S(2)}) collective-permute-start(f32[144,8,128]{2,1,0:T(8,128)S(1)} %shard_map.97), channel_id=1, source_target_pairs={{0,1},{1,0},{2,3},{3,2},{4,5},{5,4},{6,7},{7,6},{8,9},{9,8},{10,11... | collective-permute-start | bytes 1769480 | tf_op jit(solution)/shard_map/ppermute | solution.py:434
  107.5 2.0 %copy-start.5 = (f32[96,96]{1,0:T(8,128)S(1)}, f32[96,96]{1,0:T(8,128)}, u32[]{:S(2)}) copy-start(f32[96,96]{1,0:T(8,128)} %copy-done.4) | copy-start | bytes 110596
  107.5 2.0 %copy-start.7 = (f32[96,96]{1,0:T(8,128)S(1)}, f32[96,96]{1,0:T(8,128)}, u32[]{:S(2)}) copy-start(f32[96,96]{1,0:T(8,128)} %copy-done.6) | copy-start | bytes 110596
  111.4 7.2 %collective-permute-start.16 = (f32[144,128]{1,0:T(8,128)S(1)}, f32[144,128]{1,0:T(8,128)S(1)}, u32[]{:S(2)}, u32[]{:S(2)}) collective-permute-start(f32[144,128]{1,0:T(8,128)S(1)} %shard_map.99), channel_id=1, source_target_pairs={{0,4},{4,8},{8,12},{12,0},{16,20},{20,24},{24,28},{28,16},{32,36},... | collective-permute-start | bytes 221192 | tf_op jit(solution)/shard_map/ppermute | solution.py:369
  112.4 6.2 %collective-permute-start.17 = (f32[144,128]{1,0:T(8,128)S(1)}, f32[144,128]{1,0:T(8,128)S(1)}, u32[]{:S(2)}, u32[]{:S(2)}) collective-permute-start(f32[144,128]{1,0:T(8,128)S(1)} %shard_map.99), channel_id=1, source_target_pairs={{0,8},{4,12},{8,0},{12,4},{16,24},{20,28},{24,16},{28,20},{32,40},... | collective-permute-start | bytes 221192 | tf_op jit(solution)/shard_map/ppermute | solution.py:369
  112.5 6.6 %collective-permute-start.18 = (f32[144,128]{1,0:T(8,128)S(1)}, f32[144,128]{1,0:T(8,128)S(1)}, u32[]{:S(2)}, u32[]{:S(2)}) collective-permute-start(f32[144,128]{1,0:T(8,128)S(1)} %shard_map.99), channel_id=1, source_target_pairs={{0,12},{4,0},{8,4},{12,8},{16,28},{20,16},{24,20},{28,24},{32,44},... | collective-permute-start | bytes 221192 | tf_op jit(solution)/shard_map/ppermute | solution.py:369
  119.2 21.1 %collective-permute-start.19 = (f32[144,128]{1,0:T(8,128)S(1)}, f32[144,128]{1,0:T(8,128)S(1)}, u32[]{:S(2)}, u32[]{:S(2)}) collective-permute-start(f32[144,128]{1,0:T(8,128)S(1)} %add_add_fusion.1), channel_id=1, source_target_pairs={{0,16},{4,20},{8,24},{12,28},{16,0},{20,4},{24,8},{28,12},{32,48},... | collective-permute-start | bytes 221192 | tf_op jit(solution)/shard_map/ppermute | solution.py:369
  140.3 7.3 %collective-permute-start.20 = (f32[144,128]{1,0:T(8,128)S(1)}, f32[144,128]{1,0:T(8,128)S(1)}, u32[]{:S(2)}, u32[]{:S(2)}) collective-permute-start(f32[144,128]{1,0:T(8,128)S(1)} %add.49), channel_id=1, source_target_pairs={{0,32},{4,36},{8,40},{12,44},{16,48},{20,52},{24,56},{28,60},{32,6... | collective-permute-start | bytes 221192 | tf_op jit(solution)/shard_map/ppermute | solution.py:369
  140.4 10.4 %collective-permute-start.21 = (f32[144,128]{1,0:T(8,128)S(1)}, f32[144,128]{1,0:T(8,128)S(1)}, u32[]{:S(2)}, u32[]{:S(2)}) collective-permute-start(f32[144,128]{1,0:T(8,128)S(1)} %add.49), channel_id=1, source_target_pairs={{0,64},{4,68},{8,72},{12,76},{16,80},{20,84},{24,88},{28,92},{32,9... | collective-permute-start | bytes 221192 | tf_op jit(solution)/shard_map/ppermute | solution.py:369
  140.5 10.7 %collective-permute-start.22 = (f32[144,128]{1,0:T(8,128)S(1)}, f32[144,128]{1,0:T(8,128)S(1)}, u32[]{:S(2)}, u32[]{:S(2)}) collective-permute-start(f32[144,128]{1,0:T(8,128)S(1)} %add.49), channel_id=1, source_target_pairs={{0,96},{4,100},{8,104},{12,108},{16,112},{20,116},{24,120},{28,124... | collective-permute-start | bytes 221192 | tf_op jit(solution)/shard_map/ppermute | solution.py:369
  151.2 5.9 %collective-permute-start.23 = (f32[144,128]{1,0:T(8,128)S(1)}, f32[144,128]{1,0:T(8,128)S(1)}, u32[]{:S(2)}, u32[]{:S(2)}) collective-permute-start(f32[144,128]{1,0:T(8,128)S(1)} %add_add_fusion), channel_id=1, source_target_pairs={{0,128},{4,132},{8,136},{12,140},{16,144},{20,148},{24,152},{28,15... | collective-permute-start | bytes 221192 | tf_op jit(solution)/shard_map/ppermute | solution.py:369
  (6 other events, 5.7 us)
